TPU v7x, 32 devices: a whole 2x2x4 slice. The times are simulated.
32 devices in a mesh: group: 2 (over x), inst: 4 (over z), tp: 4 (over y, core).
Axes of the slice: x: 2, y: 2, z: 4, core: 2. Of those that a mesh axis runs over, the one named last changes fastest.
Arguments:
- queries: bfloat16 [2048, 2048], P(('group', 'inst'), 'tp'), parts along dimension 0, may hold values from -12 to 12
- new_kv: bfloat16 [4, 2048, 256], P('tp', ('group', 'inst')), parts along dimension 1, may hold values from -12 to 12
- kv_pool: bfloat16 [4, 1024, 128, 256], P('tp', ('group', 'inst')), parts along dimension 1, may hold values from -4 to 4
- out_weight: bfloat16 [2048, 8192], P('tp'), may hold values from -0.5 to 0.5
- lengths: int32 [256], P('group'), parts along dimension 0, may hold values from 1 to 4, as said below
- page_table: int32 [256, 4], P(('group', 'inst')), parts along dimension 0, may hold values from 0 to 127, as said below
- migration: int32 [24, 4], P('group'), parts along dimension 0, may hold values from 0 to 31, as said below
Outputs:
- mixed: bfloat16 [2048, 8192], P(('group', 'inst'), 'tp'), parts along dimension 0
There are 2 independent parts, one for each index of `group`. A program takes and returns all parts, laid end to end along the dimension named above; an argument that names none is the same for every part. Nothing has to cross between parts.
Inputs may be any that keep to these rules, and one draw needn't show every extreme that they name: context lengths in whole pages of 128 tokens; some request has 4 pages in every draw. `page_table`: row g lists the pages of request g in the pool of its home instance g // 32; the entries of one instance's requests are all different. `migration`: each row moves one request; each instance hands exactly 3 of its requests to other instances and takes exactly 3 in, into the slots that its own departing requests leave; at most one request goes from one instance to another.
All inputs are finite; a program needn't handle non-finite values.
Results may differ from a plain program's by a relative error of at most 0.0057.
Values may be sent and summed in bfloat16 or wider, within the bound.
No kernel may reach another device: no remote copies, remote signals or barrier semaphores. Data moves between devices by JAX's collectives and lax.ppermute only.
A program may use at most 128 MiB of HBM per device.

v0:
```python
import functools

import jax
import jax.numpy as jnp
from jax import lax
from jax.experimental import pallas as pl
from jax.experimental.pallas import tpu as pltpu
from jax.sharding import PartitionSpec as P

LOG2E = 1.4426950408889634
MASKED = -1e30
GROUP = 6
NEVER = 2**30

VMEM = pl.BlockSpec(memory_space=pltpu.VMEM)
SMEM = pl.BlockSpec(memory_space=pltpu.SMEM)
ANY = pl.BlockSpec(memory_space=pl.ANY)


def attend_group(queries, tokens, contexts, live_lengths, step_count):
    count = len(queries)
    head_dim = tokens[0].shape[1] // 2
    head_count = queries[0].shape[1] // head_dim
    rows = head_count * step_count
    gain = LOG2E / head_dim**0.5
    stacked = jnp.concatenate(
        [
            query[:, h * head_dim : (h + 1) * head_dim]
            for query in queries
            for h in range(head_count)
        ],
        axis=0,
    ).astype(jnp.bfloat16)
    tokens = jnp.concatenate(tokens, axis=0).astype(jnp.bfloat16)
    score_new = contract_last(stacked, tokens[:, :head_dim])
    row_ids = lax.broadcasted_iota(jnp.int32, score_new.shape, 0)
    column_ids = lax.broadcasted_iota(jnp.int32, score_new.shape, 1)
    allowed = (row_ids // rows == column_ids // step_count) & (
        column_ids % step_count <= row_ids % step_count
    )
    score_new = jnp.where(allowed, score_new, MASKED)
    new_max = jnp.max(score_new, axis=1, keepdims=True)
    maxima, scores = [], []
    for g in range(count):
        keys = jnp.concatenate([page[:, :head_dim] for page in contexts[g]], axis=0)
        score = contract_last(stacked[g * rows : (g + 1) * rows], keys)
        position = lax.broadcasted_iota(jnp.int32, score.shape, 1)
        score = jnp.where(position < live_lengths[g], score, MASKED)
        scores.append(score)
        maxima.append(
            jnp.maximum(
                jnp.max(score, axis=1, keepdims=True), new_max[g * rows : (g + 1) * rows]
            )
        )
    exp_new = jnp.exp2((score_new - jnp.concatenate(maxima, axis=0)) * gain)
    new_total = jnp.sum(exp_new, axis=1, keepdims=True)
    results, inverses = [], []
    for g in range(count):
        exp_ctx = jnp.exp2((scores[g] - maxima[g]) * gain)
        total = jnp.sum(exp_ctx, axis=1, keepdims=True) + new_total[g * rows : (g + 1) * rows]
        inverse = 1.0 / total
        inverses.append(inverse)
        values = jnp.concatenate([page[:, head_dim:] for page in contexts[g]], axis=0)
        results.append(
            jnp.dot(
                (exp_ctx * inverse).astype(jnp.bfloat16),
                values,
                preferred_element_type=jnp.float32,
            )
        )
    weight_new = (exp_new * jnp.concatenate(inverses, axis=0)).astype(jnp.bfloat16)
    result = jnp.concatenate(results, axis=0) + jnp.dot(
        weight_new, tokens[:, head_dim:], preferred_element_type=jnp.float32
    )
    return [
        jnp.concatenate(
            [
                result[g * rows + h * step_count : g * rows + (h + 1) * step_count]
                for h in range(head_count)
            ],
            axis=1,
        )
        for g in range(count)
    ]


def contract_last(a, b):
    return lax.dot_general(a, b, (((1,), (1,)), ((), ())), preferred_element_type=jnp.float32)


def route_of(migration, own_index, peer, arriving):
    ours, theirs, slot_row = (2, 0, 3) if arriving else (0, 2, 1)
    slot = jnp.int32(0)
    for row in range(migration.shape[1]):
        match = (migration[ours, row] == own_index) & (migration[theirs, row] == peer)
        slot = jnp.where(match, migration[slot_row, row], slot)
    return slot


def arrivals_of(migration, inst_count):
    me = lax.axis_index("inst")
    incoming = migration.shape[1] // inst_count
    slots = [jnp.int32(NEVER)] * incoming
    sources = [jnp.int32(0)] * incoming
    for row in range(migration.shape[1]):
        slot = jnp.where(migration[2, row] == me, migration[3, row], NEVER)
        source = migration[0, row]
        for i in range(incoming):
            before = slot < slots[i]
            slots[i], slot = jnp.where(before, slot, slots[i]), jnp.where(before, slots[i], slot)
            sources[i], source = (
                jnp.where(before, source, sources[i]),
                jnp.where(before, sources[i], source),
            )
    return slots, sources


def slot_at(position, arrivals, slot_count):
    kept = slot_count - len(arrivals)
    if position >= kept:
        return jnp.minimum(arrivals[position - kept], slot_count - 1)
    slot = jnp.int32(position)
    for arrival in arrivals:
        slot = slot + (slot >= arrival).astype(jnp.int32)
    return slot


def peer_of(me, k, count):
    return me ^ k if count & (count - 1) == 0 else (count - me + k) % count


def pack_rows(inst_count, migration, queries, new_tokens, packs):
    me = lax.axis_index("inst")
    width = queries.shape[2]
    for k, pack in packs.items():
        slot = route_of(migration, me, peer_of(me, k, inst_count), True)
        pack[:, :width] = queries[slot]
        pack[:, width:] = new_tokens[slot]


def page_copies(pool, buffer, sems, page_table, item, slot):
    page_count = page_table.shape[0]
    for j in range(page_count):
        pltpu.make_async_copy(
            pool.at[page_table[j, slot]], buffer.at[item, j], sems.at[item]
        ).start()


def wait_copies(pool, buffer, sems, item):
    pltpu.make_async_copy(
        pool.at[pl.ds(0, buffer.shape[1])], buffer.at[item], sems.at[item]
    ).wait()


def away_slot(migration, inst_count, k):
    me = lax.axis_index("inst")
    return route_of(migration, me, peer_of(me, k, inst_count), False)


def away_kernel(
    inst_count, rounds, lengths, migration, pages, second, far_weight, *refs
):
    count = len(rounds)
    received, answers, (keep, send) = refs[:count], refs[count : 2 * count], refs[2 * count :]
    _, page_count, page_len, _ = pages.shape
    step_count, width = answers[0].shape
    first = lax.axis_index("inst") * (lengths.shape[0] // inst_count)
    result = attend_group(
        [ref[:, :width].astype(jnp.float32) for ref in received],
        [ref[:, width:].astype(jnp.float32) for ref in received],
        [[pages.at[i, j] for j in range(page_count)] for i in range(count)],
        [lengths[first + away_slot(migration, inst_count, k)] * page_len for k in rounds],
        step_count,
    )
    for answer, rows in zip(answers, result):
        answer[...] = rows.astype(answer.dtype)
    project_far(second, far_weight, keep, send)


def project(rows, weight, first, columns, target, row_offset=0, offset=0):
    tile = min(512, columns)
    rows = rows[...]
    for j in range(0, columns, tile):
        start = pl.multiple_of(first + j, tile)
        target[row_offset : row_offset + rows.shape[0], offset + j : offset + j + tile] = jnp.dot(
            rows, weight[:, pl.ds(start, tile)], preferred_element_type=jnp.float32
        ).astype(target.dtype)


def project_far(attended, far_weight, keep, send):
    core = lax.rem(lax.axis_index("tp"), 2)
    chips = lax.axis_size("tp") // 2
    columns = far_weight.shape[1] // (2 * chips - 2)
    for target, side in ((send, 1 - core), (keep, core)):
        for d in range(chips - 1):
            first = (2 * d + side) * columns
            project(attended, far_weight, first, columns, target, 0, d * columns)


def attend_slots(slots, lengths, queries, new_tokens, pages, wait=lambda i: None):
    page_count, page_len = pages.shape[1:3]
    first = lax.axis_index("inst") * queries.shape[0]
    rows = []
    for base in range(0, len(slots), GROUP):
        items = range(base, min(base + GROUP, len(slots)))
        for i in items:
            wait(i)
        rows += attend_group(
            [queries[slots[i]].astype(jnp.float32) for i in items],
            [new_tokens[slots[i]].astype(jnp.float32) for i in items],
            [[pages.at[i, j] for j in range(page_count)] for i in items],
            [lengths[first + slots[i]] * page_len for i in items],
            queries.shape[1],
        )
    return rows


def store_rows(rows, target, at=0):
    step_count = rows[0].shape[0]
    for pair in range(0, len(rows), 2):
        start = at + pair * step_count
        target[start : start + 2 * step_count, :] = jnp.concatenate(
            rows[pair : pair + 2], axis=0
        ).astype(jnp.bfloat16)


def first_kernel(
    inst_count, rounds, migration, lengths, page_table, queries_in, new_in, pool, weight,
    attended, keep, send, far_weight, queries, new_tokens, second_pages, away_pages, *refs,
):
    packs = dict(zip(rounds, refs))
    buffer, small_sems, first_sems, second_sems, away_sems, weight_sems = refs[len(rounds) :]
    own_tp = lax.axis_index("tp")
    chips = lax.axis_size("tp") // 2
    pair_columns = weight.shape[1] // chips
    slot_count, step_count, _ = queries.shape
    small = [
        pltpu.make_async_copy(queries_in, queries, small_sems.at[0]),
        pltpu.make_async_copy(new_in, new_tokens, small_sems.at[1]),
    ]
    for copy in small:
        copy.start()
    arrivals, _ = arrivals_of(migration, inst_count)
    count = attended.shape[0] // step_count
    total = count + second_pages.shape[0]
    slots = [slot_at(position, arrivals, slot_count) for position in range(total)]
    for i in range(count):
        page_copies(pool, buffer, first_sems, page_table, i, slots[i])

    def weight_copy(d):
        chip = lax.rem(own_tp // 2 + d, chips)
        start = pl.multiple_of(chip * pair_columns, pair_columns)
        return pltpu.make_async_copy(
            weight.at[:, pl.ds(start, pair_columns)],
            far_weight.at[:, pl.ds((d - 1) * pair_columns, pair_columns)],
            weight_sems.at[d - 1],
        )

    for d in range(1, chips):
        weight_copy(d).start()
    for i, slot in enumerate(slots[count:]):
        page_copies(pool, second_pages, second_sems, page_table, i, slot)
    for i, k in enumerate(rounds):
        slot = away_slot(migration, inst_count, k)
        page_copies(pool, away_pages, away_sems, page_table, i, slot)
    for copy in small:
        copy.wait()
    pack_rows(inst_count, migration, queries, new_tokens, packs)
    store_rows(
        attend_slots(
            slots[:count], lengths, queries, new_tokens, buffer,
            lambda i: wait_copies(pool, buffer, first_sems, i),
        ),
        attended,
    )
    for d in range(1, chips):
        weight_copy(d).wait()
    project_far(attended, far_weight, keep, send)
    for i in range(total - count):
        wait_copies(pool, second_pages, second_sems, i)
    for i in range(len(rounds)):
        wait_copies(pool, away_pages, away_sems, i)


def second_kernel(
    inst_count, first, migration, lengths, queries, new_tokens, pages, weight, after,
    attended, extra, near_weight, sems,
):
    slot_count, step_count, _ = queries.shape
    core = lax.rem(lax.axis_index("tp"), 2)
    chip = lax.axis_index("tp") // 2
    columns = near_weight.shape[2]
    copies = []
    for n, side in enumerate((1 - core, core)):
        start = pl.multiple_of((chip * 2 + side) * columns, columns)
        copies.append(
            pltpu.make_async_copy(
                weight.at[:, pl.ds(start, columns)], near_weight.at[n], sems.at[n]
            )
        )
        copies[n].start()
    arrivals, _ = arrivals_of(migration, inst_count)
    slots = [slot_at(first + i, arrivals, slot_count) for i in range(pages.shape[0])]
    rows = attend_slots(slots, lengths, queries, new_tokens, pages)
    count = attended.shape[0] // step_count
    store_rows(rows[:count], attended)
    for i, row in enumerate(rows[count:]):
        extra[i] = row.astype(extra.dtype)
    for copy in copies:
        copy.wait()


def own_kernel(near_weight, first, second, after, keep, *refs):
    sends, rows = refs[:-1], refs[-1]
    rows[: first.shape[0], :] = first[...]
    rows[first.shape[0] :, :] = second[...]
    at = 0
    for send in sends:
        project(rows, near_weight.at[0], at, send.shape[1], send)
        at += send.shape[1]
    project(rows, near_weight.at[1], 0, keep.shape[1], keep)


def last_rows_kernel(
    inst_count, rounds, migration, near_weight, far_weight, extra, after, *refs
):
    answers, (keep, send, rows) = refs[:-3], refs[-3:]
    core = lax.rem(lax.axis_index("tp"), 2)
    chips = lax.axis_size("tp") // 2
    me = lax.axis_index("inst")
    columns = keep.shape[1]
    _, sources = arrivals_of(migration, inst_count)
    last = [extra[i].astype(jnp.float32) for i in range(extra.shape[0])]
    given = [answer[...].astype(jnp.float32) for answer in answers]
    for source in sources:
        row = given[0]
        for k, answer in zip(rounds[1:], given[1:]):
            row = jnp.where(source == peer_of(me, k, inst_count), answer, row)
        last.append(row)
    size = rows.shape[0]
    store_rows(last, rows)
    for n, (target, side) in enumerate(((send, 1 - core), (keep, core))):
        for d in range(chips - 1):
            project(rows, far_weight, (2 * d + side) * columns, columns, target, d * size)
        project(rows, near_weight.at[n], 0, columns, target, (chips - 1) * size)


def sum_kernel(inst_count, chunks, piece_count, migration, keep, *refs):
    mates, parts, (out, staged, sem) = refs[:piece_count], refs[piece_count:-3], refs[-3:]
    slot_count, step_count, _ = out.shape
    pair = 2 * step_count
    width = mates[0].shape[1]
    arrivals, _ = arrivals_of(migration, inst_count)
    share = len(parts) // len(chunks)
    at = 0
    for n, chunk in enumerate(chunks):
        for base in range(0, chunk, pair):
            for m, mate in enumerate(mates):
                columns = slice(m * width, (m + 1) * width)
                total = keep[at : at + pair, columns] + mate[at : at + pair, :].astype(jnp.float32)
                for part in parts[n * share : (n + 1) * share]:
                    total = total + part[base : base + pair, columns].astype(jnp.float32)
                total = total.astype(jnp.bfloat16)
                for half in range(2):
                    staged[at // step_count + half, :, columns] = total[
                        half * step_count : (half + 1) * step_count
                    ]
            at += pair
    scatter_rows(staged, out, arrivals, 0, sem)


def scatter_rows(staged, out, arrivals, first, sem):
    slot_count = out.shape[0]
    for i in range(staged.shape[0]):
        slot = slot_at(first + i, arrivals, slot_count)
        pltpu.make_async_copy(staged.at[i], out.at[slot], sem.at[0]).start()
    pltpu.make_async_copy(staged, out.at[pl.ds(0, staged.shape[0])], sem.at[0]).wait()


def last_kernel(inst_count, first, migration, keep, mate, *refs):
    parts, (out, staged, sem) = refs[:-4], refs[-3:]
    step_count = out.shape[1]
    pair = 2 * step_count
    size = parts[0].shape[0]
    arrivals, _ = arrivals_of(migration, inst_count)
    for at in range(0, size, pair):
        own = keep.shape[0] - size + at
        total = keep[own : own + pair, :] + mate[own : own + pair, :].astype(jnp.float32)
        for part in parts:
            total = total + part[at : at + pair, :].astype(jnp.float32)
        total = total.astype(jnp.bfloat16)
        for half in range(2):
            staged[at // step_count + half] = total[half * step_count : (half + 1) * step_count]
    scatter_rows(staged, out, arrivals, first, sem)


def in_hbm(value):
    return pltpu.with_memory_space_constraint(value, pltpu.HBM)


def in_vmem(value):
    return pltpu.with_memory_space_constraint(value, pltpu.VMEM)


def on_device(queries, new_kv, kv_pool, out_weight, lengths, page_table, migration):
    inst_count = lax.axis_size("inst")
    tp_count = lax.axis_size("tp")
    chips = tp_count // 2
    slot_count, page_count = page_table.shape
    row_count, width = queries.shape
    step_count = row_count // slot_count
    queries = in_hbm(queries.reshape(slot_count, step_count, width))
    new_tokens = in_hbm(new_kv[0].reshape(slot_count, step_count, new_kv.shape[2]))
    pool = in_hbm(kv_pool[0])
    columns = out_weight.shape[1] // tp_count
    incoming = migration.shape[0] // inst_count
    weight = in_hbm(out_weight)
    lengths = in_hbm(lengths)
    page_table = in_hbm(page_table.T)
    migration = in_hbm(migration.T)
    limit = pltpu.CompilerParams(vmem_limit_bytes=32 * 2**20)
    light = pl.CostEstimate(flops=1, bytes_accessed=1, transcendentals=0)
    bf16, f32 = jnp.bfloat16, jnp.float32
    shape = jax.ShapeDtypeStruct
    swap = [(t, t ^ 1) for t in range(tp_count)]
    far = (chips - 1) * columns

    def hold(value, until):
        return pl.pallas_call(
            lambda *refs: None,
            out_shape=pltpu.VMEM(value.shape, value.dtype),
            in_specs=[ANY] * (1 + len(until)),
            out_specs=ANY,
            input_output_aliases={0: 0},
            compiler_params=pltpu.CompilerParams(vmem_limit_bytes=2**20),
            cost_estimate=light,
            name="hold",
        )(in_vmem(value), *until)

    def send_far(summed):
        return [
            lax.ppermute(
                part, "tp", [(t, (t + 2 * d) % tp_count) for t in range(tp_count)]
            )
            for d, part in enumerate(summed, 1)
        ]

    def split_far(summed):
        return [summed[:, d * columns : (d + 1) * columns] for d in range(chips - 1)]

    def chunk_shapes(count):
        rows = count * step_count
        return [pltpu.VMEM((rows, far), f32), pltpu.VMEM((rows, far), bf16)]

    def rows_shape(count):
        return pltpu.VMEM((count * step_count, width), bf16)

    last_count = incoming + incoming % 2
    extra_count = last_count - incoming
    first_count = slot_count // 4 * 2
    second_count = slot_count - first_count - last_count
    last_rows = last_count * step_count

    def page_shape(count):
        return pltpu.VMEM((count, page_count, *pool.shape[1:]), bf16)

    dma = pltpu.SemaphoreType.DMA
    rounds = [
        k
        for k in range(inst_count)
        if any(peer_of(i, k, inst_count) != i for i in range(inst_count))
    ]
    pairs = {k: [(i, peer_of(i, k, inst_count)) for i in range(inst_count)] for k in rounds}
    rest_count = second_count + extra_count
    (
        first, keep, send, far_weight, queries, new_tokens, second_pages, away_pages, *packs
    ) = pl.pallas_call(
        functools.partial(first_kernel, inst_count, rounds),
        out_shape=[
            rows_shape(first_count),
            *chunk_shapes(first_count),
            pltpu.VMEM((width, 2 * far), bf16),
            pltpu.VMEM(queries.shape, bf16),
            pltpu.VMEM(new_tokens.shape, bf16),
            page_shape(rest_count),
            page_shape(len(rounds)),
        ]
        + [shape((step_count, width + new_tokens.shape[2]), bf16)] * len(rounds),
        in_specs=[SMEM, SMEM, SMEM, ANY, ANY, ANY, ANY],
        out_specs=[VMEM] * (8 + len(rounds)),
        scratch_shapes=[
            page_shape(first_count),
            dma((2,)),
            dma((first_count,)),
            dma((rest_count,)),
            dma((len(rounds),)),
            dma((chips - 1,)),
        ],
        compiler_params=limit,
        cost_estimate=light,
        name="attend_first",
    )(migration, lengths, page_table, queries, new_tokens, pool, weight)
    far_weight = in_vmem(far_weight)
    mate = lax.ppermute(send, "tp", swap)
    summed = (keep + mate.astype(f32)).astype(bf16)
    arrived_first = send_far(split_far(summed))
    received = [lax.ppermute(pack, "inst", pairs[k]) for k, pack in zip(rounds, packs)]

    second, extra, near_weight = pl.pallas_call(
        functools.partial(second_kernel, inst_count, first_count),
        out_shape=[
            rows_shape(second_count),
            pltpu.VMEM((extra_count, step_count, width), bf16),
            pltpu.VMEM((2, width, columns), bf16),
        ],
        in_specs=[SMEM, SMEM, VMEM, VMEM, VMEM, ANY, ANY],
        out_specs=[VMEM] * 3,
        scratch_shapes=[dma((2,))],
        compiler_params=limit,
        cost_estimate=light,
        name="attend_second",
    )(
        migration, lengths, in_vmem(queries), in_vmem(new_tokens), in_vmem(second_pages), weight,
        summed,
    )
    second, near_weight = in_vmem(second), in_vmem(near_weight)
    *answers, keep, send = pl.pallas_call(
        functools.partial(away_kernel, inst_count, rounds),
        out_shape=[shape((step_count, width), bf16)] * len(rounds) + chunk_shapes(second_count),
        in_specs=[SMEM, SMEM] + [VMEM] * (3 + len(rounds)),
        out_specs=[VMEM] * (2 + len(rounds)),
        compiler_params=limit,
        cost_estimate=light,
        name="attend_away",
    )(lengths, migration, in_vmem(away_pages), second, far_weight, *received)
    mate = lax.ppermute(send, "tp", swap)
    answers = [lax.ppermute(answer, "inst", pairs[k]) for k, answer in zip(rounds, answers)]
    keep = hold(keep, arrived_first)
    summed = (keep + mate.astype(f32)).astype(bf16)
    arrived_second = send_far(split_far(summed))

    early_rows = (first_count + second_count) * step_count
    pieces = 2
    early_keep, *early_sends = pl.pallas_call(
        own_kernel,
        out_shape=[
            pltpu.VMEM((early_rows, columns), f32),
            *[pltpu.VMEM((early_rows, columns // pieces), bf16)] * pieces,
        ],
        in_specs=[VMEM, VMEM, VMEM, ANY],
        out_specs=[VMEM] * (1 + pieces),
        scratch_shapes=[pltpu.VMEM((early_rows, width), bf16)],
        compiler_params=limit,
        cost_estimate=light,
        name="own_columns",
    )(near_weight, in_vmem(first), second, summed)
    early_mates = [lax.ppermute(early_send, "tp", swap) for early_send in early_sends]

    keep, send = pl.pallas_call(
        functools.partial(last_rows_kernel, inst_count, rounds),
        out_shape=[
            pltpu.VMEM((last_rows * chips, columns), f32),
            pltpu.VMEM((last_rows * chips, columns), bf16),
        ],
        in_specs=[SMEM] + [VMEM] * 3 + [ANY] + [VMEM] * len(rounds),
        out_specs=[VMEM] * 2,
        scratch_shapes=[pltpu.VMEM((last_rows, width), bf16)],
        compiler_params=limit,
        cost_estimate=light,
        name="last_rows",
    )(migration, near_weight, far_weight, in_vmem(extra), early_keep, *answers)
    mate = lax.ppermute(send, "tp", swap)
    keep = hold(keep, arrived_second)
    summed = (keep[:-last_rows] + mate[:-last_rows].astype(f32)).astype(bf16)
    arrived_last = send_far([summed[d * last_rows : (d + 1) * last_rows] for d in range(chips - 1)])

    early = slot_count - last_count
    out_shape = (slot_count, step_count, columns)
    out = pl.pallas_call(
        functools.partial(
            sum_kernel, inst_count, [first_count * step_count, second_count * step_count], pieces
        ),
        out_shape=pltpu.HBM(out_shape, bf16),
        in_specs=[SMEM] + [VMEM] * (1 + pieces + 2 * (chips - 1)),
        out_specs=ANY,
        scratch_shapes=[
            pltpu.VMEM((early, step_count, columns), bf16),
            pltpu.SemaphoreType.DMA((1,)),
        ],
        compiler_params=limit,
        cost_estimate=light,
        name="sum_early",
    )(migration, in_vmem(early_keep), *early_mates, *arrived_first, *arrived_second)
    out = pl.pallas_call(
        functools.partial(last_kernel, inst_count, early),
        out_shape=pltpu.HBM(out_shape, bf16),
        in_specs=[SMEM] + [VMEM] * (chips + 1) + [ANY],
        out_specs=ANY,
        scratch_shapes=[
            pltpu.VMEM((last_count, step_count, columns), bf16),
            pltpu.SemaphoreType.DMA((1,)),
        ],
        input_output_aliases={2 + chips: 0},
        compiler_params=limit,
        cost_estimate=light,
        name="sum_last",
    )(migration, in_vmem(keep), mate, *arrived_last, out)
    return out.reshape(row_count, columns)


def solution(mesh):
    placed = (
        P(("group", "inst"), "tp"),
        P("tp", ("group", "inst"), None),
        P("tp", ("group", "inst"), None, None),
        P("tp", None),
        P("group"),
        P(("group", "inst"), None),
        P("group", None),
    )
    return jax.shard_map(
        on_device, mesh=mesh, in_specs=placed, out_specs=P(("group", "inst"), "tp"), check_vma=False
    )
```

profile of v0, /device:TPU:0, one launch (start us, length us, event | category | flops | bytes accessed | tf_op | source)
XLA Modules:
  0.0 47.6 jit_solution(9984863730552643422)
XLA Ops:
  0.0 7.9 %attend_first.1 = (bf16[128,512]{1,0:T(8,128)(2,1)S(1)}, f32[128,2048]{1,0:T(8,128)S(1)}, bf16[128,2048]{1,0:T(8,128)(2,1)S(1)}, bf16[512,4096]{1,0:T(8,128)(2,1...) custom-call(s32[4,12]{1,0:T(4,128)} %bitcast.9, ...), custom_call_target="tpu_custom_call" | custom-call | flops 1 | bytes 1 | tf_op jit(solution)/shard_map/attend_first/pallas_call | solution.py:477
  7.9 0.5 %collective-permute-start = (bf16[128,2048]{1,0:T(8,128)(2,1)S(1)}, bf16[128,2048]{1,0:T(8,128)(2,1)S(1)}, u32[]{:S(2)}, u32[]{:S(2)}) collective-permute-start(bf16[128,2048]{1,0:T(8,128)(2,1)S(1)} %get-tuple-element.33), channel_id=1, source_target_pairs={{0,1},{1,0},{2,3},{3,2},{4,5},{5,4},{6,7},{7,6},{8,9},{9,8},{10,11... | collective-permute-start | bytes 1572872 | tf_op jit(solution)/shard_map/ppermute | solution.py:504
  8.4 1.5 %collective-permute-done = bf16[128,2048]{1,0:T(8,128)(2,1)S(1)} collective-permute-done((bf16[128,2048]{1,0:T(8,128)(2,1)S(1)}, bf16[128,2048]{1,0:T(8,128)(2,1)S(1)}, u32[]{:S(2)}, u32[]{:S(2)}) %collective-permute-start) | collective-permute-done | bytes 524320 | tf_op jit(solution)/shard_map/ppermute | solution.py:504
  10.0 0.1 add_convert_fusion.after
  10.1 3.0 %collective-permute-start.4 = (bf16[128,2048]{1,0:T(8,128)(2,1)S(1)}, bf16[128,2048]{1,0:T(8,128)(2,1)S(1)}, u32[]{:S(2)}, u32[]{:S(2)}) collective-permute-start(bf16[128,2048]{1,0:T(8,128)(2,1)S(1)} %add_convert_fusion.after), channel_id=1, source_target_pairs={{0,2},{1,3},{2,0},{3,1},{4,6},{5,7},{6,4},{7,5},{8,10},{9,11},{10,... | collective-permute-start | bytes 1572872 | tf_op jit(solution)/shard_map/ppermute | solution.py:442
  13.0 1.6 %collective-permute-start.1 = (bf16[8,768]{1,0:T(8,128)(2,1)S(1)}, bf16[8,768]{1,0:T(8,128)(2,1)S(1)}, u32[]{:S(2)}, u32[]{:S(2)}) collective-permute-start(bf16[8,768]{1,0:T(8,128)(2,1)S(1)} %get-tuple-element.40), channel_id=1, source_target_pairs={{0,4},{4,0},{8,12},{12,8},{1,5},{5,1},{9,13},{13,9},{2,6},{6,2},{1... | collective-permute-start | bytes 36872 | tf_op jit(solution)/shard_map/ppermute | solution.py:507
  14.6 2.6 %collective-permute-start.2 = (bf16[8,768]{1,0:T(8,128)(2,1)S(1)}, bf16[8,768]{1,0:T(8,128)(2,1)S(1)}, u32[]{:S(2)}, u32[]{:S(2)}) collective-permute-start(bf16[8,768]{1,0:T(8,128)(2,1)S(1)} %get-tuple-element.41), channel_id=1, source_target_pairs={{0,8},{4,12},{8,0},{12,4},{1,9},{5,13},{9,1},{13,5},{2,10},{6,14},... | collective-permute-start | bytes 36872 | tf_op jit(solution)/shard_map/ppermute | solution.py:507
  17.2 0.2 collective-permute-start.3
  17.4 4.9 %attend_second.1 = (bf16[96,512]{1,0:T(8,128)(2,1)S(1)}, bf16[1,8,512]{2,1,0:T(8,128)(2,1)S(1)}, bf16[2,512,2048]{2,1,0:T(8,128)(2,1)S(1)}) custom-call(s32[4,12]{1,0:T(4,128)} %bitcast.10, s32[128]{0:T(128)} %lengths.5, bf16[32,8,512]{2,1,0:T(8,128)(2,1)S(1)} %get-tuple-element.29.queries, bf16[32,8,256]{2,1,0:T(8,128)(2,1)S(1)} %get-tuple-element.30.new_tokens, ...), custom_call_target="tpu_custom_call" | custom-call | flops 1 | bytes 1 | tf_op jit(solution)/shard_map/attend_second/pallas_call | solution.py:509
  22.3 0.0 collective-permute-done.1.refs_0_
  22.3 0.0 collective-permute-done.2.refs_1_
  22.3 0.4 collective-permute-done.3.refs_2_
  22.7 2.0 %attend_away.1 = (bf16[8,512]{1,0:T(8,128)(2,1)S(1)}, bf16[8,512]{1,0:T(8,128)(2,1)S(1)}, bf16[8,512]{1,0:T(8,128)(2,1)S(1)}, f32[96,2048]{1,0:T(8,128)S(1)}, bf16[96,2048]{1,0:T(8,128)(2,1)S(1)}) custom-call(s32[128]{0:T(128)} %lengths.5, s32[4,12]{1,0:T(4,128)} %bitcast.11, bf16[3,4,128,256]{3,2,1,0:T(8,128)(2,1)S(1)} %get-tuple-element.39.pages, ...), custom_call_target="tpu_custom_call" | custom-call | flops 1 | bytes 1 | tf_op jit(solution)/shard_map/attend_away/pallas_call | solution.py:527
  24.7 0.1 collective-permute-start.5
  24.8 0.5 %collective-permute-done.4.refs_1_.refs_2_ = bf16[128,2048]{1,0:T(8,128)(2,1)S(1)} collective-permute-done((bf16[128,2048]{1,0:T(8,128)(2,1)S(1)}, bf16[128,2048]{1,0:T(8,128)(2,1)S(1)}, u32[]{:S(2)}, u32[]{:S(2)}) %collective-permute-start.4) | collective-permute-done | bytes 524320 | tf_op jit(solution)/shard_map/ppermute | solution.py:442
  25.2 1.2 %collective-permute-done.5 = bf16[96,2048]{1,0:T(8,128)(2,1)S(1)} collective-permute-done((bf16[96,2048]{1,0:T(8,128)(2,1)S(1)}, bf16[96,2048]{1,0:T(8,128)(2,1)S(1)}, u32[]{:S(2)}, u32[]{:S(2)}) %collective-permute-start.5) | collective-permute-done | bytes 393248 | tf_op jit(solution)/shard_map/ppermute | solution.py:536
  26.5 0.1 add_convert_fusion.1.after
  26.6 0.6 %collective-permute-start.9 = (bf16[96,2048]{1,0:T(8,128)(2,1)S(1)}, bf16[96,2048]{1,0:T(8,128)(2,1)S(1)}, u32[]{:S(2)}, u32[]{:S(2)}) collective-permute-start(bf16[96,2048]{1,0:T(8,128)(2,1)S(1)} %add_convert_fusion.1.after), channel_id=1, source_target_pairs={{0,2},{1,3},{2,0},{3,1},{4,6},{5,7},{6,4},{7,5},{8,10},{9,11},{10,... | collective-permute-start | bytes 1179656 | tf_op jit(solution)/shard_map/ppermute | solution.py:442
  27.1 1.6 %collective-permute-start.6 = (bf16[8,512]{1,0:T(8,128)(2,1)S(1)}, bf16[8,512]{1,0:T(8,128)(2,1)S(1)}, u32[]{:S(2)}, u32[]{:S(2)}) collective-permute-start(bf16[8,512]{1,0:T(8,128)(2,1)S(1)} %get-tuple-element.46), channel_id=1, source_target_pairs={{0,4},{4,0},{8,12},{12,8},{1,5},{5,1},{9,13},{13,9},{2,6},{6,2},{1... | collective-permute-start | bytes 24584 | tf_op jit(solution)/shard_map/ppermute | solution.py:537
  28.7 2.6 %collective-permute-start.7 = (bf16[8,512]{1,0:T(8,128)(2,1)S(1)}, bf16[8,512]{1,0:T(8,128)(2,1)S(1)}, u32[]{:S(2)}, u32[]{:S(2)}) collective-permute-start(bf16[8,512]{1,0:T(8,128)(2,1)S(1)} %get-tuple-element.47), channel_id=1, source_target_pairs={{0,8},{4,12},{8,0},{12,4},{1,9},{5,13},{9,1},{13,5},{2,10},{6,14},... | collective-permute-start | bytes 24584 | tf_op jit(solution)/shard_map/ppermute | solution.py:537
  31.3 0.2 collective-permute-start.8
  31.5 1.1 %own_columns.1 = (f32[224,2048]{1,0:T(8,128)S(1)}, bf16[224,1024]{1,0:T(8,128)(2,1)S(1)}, bf16[224,1024]{1,0:T(8,128)(2,1)S(1)}) custom-call(bf16[2,512,2048]{2,1,0:T(8,128)(2,1)S(1)} %get-tuple-element.34.near_weight, bf16[128,512]{1,0:T(8,128)(2,1)S(1)} %get-tuple-element.37.first, bf16[96,512]{1,0:T(8,128)(2,1)S(1)} %get-tuple-element.38.second, ...), custom_call_target="tpu_custom_call" | custom-call | flops 1 | bytes 1 | tf_op jit(solution)/shard_map/own_columns/pallas_call | solution.py:544
  32.7 0.0 collective-permute-done.6.refs_0_
  32.7 0.6 %collective-permute-done.7.refs_1_ = bf16[8,512]{1,0:T(8,128)(2,1)S(1)} collective-permute-done((bf16[8,512]{1,0:T(8,128)(2,1)S(1)}, bf16[8,512]{1,0:T(8,128)(2,1)S(1)}, u32[]{:S(2)}, u32[]{:S(2)}) %collective-permute-start.7) | collective-permute-done | bytes 8224 | tf_op jit(solution)/shard_map/ppermute | solution.py:537
  33.3 3.5 %collective-permute-done.8.refs_2_ = bf16[8,512]{1,0:T(8,128)(2,1)S(1)} collective-permute-done((bf16[8,512]{1,0:T(8,128)(2,1)S(1)}, bf16[8,512]{1,0:T(8,128)(2,1)S(1)}, u32[]{:S(2)}, u32[]{:S(2)}) %collective-permute-start.8) | collective-permute-done | bytes 8224 | tf_op jit(solution)/shard_map/ppermute | solution.py:537
  36.8 2.3 %last_rows.1 = (f32[64,2048]{1,0:T(8,128)S(1)}, bf16[64,2048]{1,0:T(8,128)(2,1)S(1)}) custom-call(s32[4,12]{1,0:T(4,128)} %bitcast.12, bf16[2,512,2048]{2,1,0:T(8,128)(2,1)S(1)} %get-tuple-element.34.near_weight, bf16[512,4096]{1,0:T(8,128)(2,1)S(1)} %get-tuple-element.35.far_weight, bf16[1,8,512]{2,1,0:T(8,128)(2,1)S(1)} %get-tuple-element.36.extra, ...), custom_call_target="tpu_custom_call" | custom-call | flops 1 | bytes 1 | tf_op jit(solution)/shard_map/last_rows/pallas_call | solution.py:559
  39.0 0.0 collective-permute-start.10
  39.0 0.5 %collective-permute-start.12 = (bf16[224,1024]{1,0:T(8,128)(2,1)S(1)}, bf16[224,1024]{1,0:T(8,128)(2,1)S(1)}, u32[]{:S(2)}, u32[]{:S(2)}) collective-permute-start(bf16[224,1024]{1,0:T(8,128)(2,1)S(1)} %get-tuple-element.51), channel_id=1, source_target_pairs={{0,1},{1,0},{2,3},{3,2},{4,5},{5,4},{6,7},{7,6},{8,9},{9,8},{10,11... | collective-permute-start | bytes 1376264 | tf_op jit(solution)/shard_map/ppermute | solution.py:557
  39.5 0.1 collective-permute-start.13
  39.6 0.0 collective-permute-done.9.refs_1_.refs_3_
  39.6 1.0 %collective-permute-done.10.mate = bf16[64,2048]{1,0:T(8,128)(2,1)S(1)} collective-permute-done((bf16[64,2048]{1,0:T(8,128)(2,1)S(1)}, bf16[64,2048]{1,0:T(8,128)(2,1)S(1)}, u32[]{:S(2)}, u32[]{:S(2)}) %collective-permute-start.10) | collective-permute-done | bytes 262176 | tf_op jit(solution)/shard_map/ppermute | solution.py:572
  40.6 1.2 %collective-permute-start.11 = (bf16[32,2048]{1,0:T(8,128)(2,1)S(1)}, bf16[32,2048]{1,0:T(8,128)(2,1)S(1)}, u32[]{:S(2)}, u32[]{:S(2)}) collective-permute-start(bf16[32,2048]{1,0:T(8,128)(2,1)S(1)} %fusion), channel_id=1, source_target_pairs={{0,2},{1,3},{2,0},{3,1},{4,6},{5,7},{6,4},{7,5},{8,10},{9,11},{10,... | collective-permute-start | bytes 393224 | tf_op jit(solution)/shard_map/ppermute | solution.py:442
  41.8 0.0 collective-permute-done.12.refs_0_
  41.8 0.1 collective-permute-done.13.refs_1_
  41.9 1.9 %sum_early.1.refs_1_ = bf16[32,8,2048]{2,1,0:T(8,128)(2,1)} custom-call(s32[4,12]{1,0:T(4,128)} %bitcast.13, f32[224,2048]{1,0:T(8,128)S(1)} %get-tuple-element.45.after.keep, bf16[224,1024]{1,0:T(8,128)(2,1)S(1)} %collective-permute-done.12.refs_0_, bf16[224,1024]{1,0:T(8,128)(2,1)S(1)} %collective-permute-done.13.refs_1_, ...), custom_call_target="tpu_custom_call" | custom-call | flops 1 | bytes 1 | tf_op jit(solution)/shard_map/sum_early/pallas_call | solution.py:579
  43.7 2.5 %collective-permute-done.11.refs_0_ = bf16[32,2048]{1,0:T(8,128)(2,1)S(1)} collective-permute-done((bf16[32,2048]{1,0:T(8,128)(2,1)S(1)}, bf16[32,2048]{1,0:T(8,128)(2,1)S(1)}, u32[]{:S(2)}, u32[]{:S(2)}) %collective-permute-start.11) | collective-permute-done | bytes 131104 | tf_op jit(solution)/shard_map/ppermute | solution.py:442
  46.2 1.4 %sum_last.1 = bf16[32,8,2048]{2,1,0:T(8,128)(2,1)} custom-call(s32[4,12]{1,0:T(4,128)} %bitcast.14, f32[64,2048]{1,0:T(8,128)S(1)} %hold.3.keep, bf16[64,2048]{1,0:T(8,128)(2,1)S(1)} %collective-permute-done.10.mate, bf16[32,2048]{1,0:T(8,128)(2,1)S(1)} %collective-permute-done.11.refs_0_, ...), custom_call_target="tpu_custom_call", output_to_operand_aliasing={{}: (4, {})} | custom-call | flops 1 | bytes 1 | tf_op jit(solution)/shard_map/sum_last/pallas_call | solution.py:594
  (3 shorter events, 0.0 us)
Async XLA Ops:
  7.9 2.1 %collective-permute-start = (bf16[128,2048]{1,0:T(8,128)(2,1)S(1)}, bf16[128,2048]{1,0:T(8,128)(2,1)S(1)}, u32[]{:S(2)}, u32[]{:S(2)}) collective-permute-start(bf16[128,2048]{1,0:T(8,128)(2,1)S(1)} %get-tuple-element.33), channel_id=1, source_target_pairs={{0,1},{1,0},{2,3},{3,2},{4,5},{5,4},{6,7},{7,6},{8,9},{9,8},{10,11... | collective-permute-start | bytes 1572872 | tf_op jit(solution)/shard_map/ppermute | solution.py:504
  10.1 15.2 %collective-permute-start.4 = (bf16[128,2048]{1,0:T(8,128)(2,1)S(1)}, bf16[128,2048]{1,0:T(8,128)(2,1)S(1)}, u32[]{:S(2)}, u32[]{:S(2)}) collective-permute-start(bf16[128,2048]{1,0:T(8,128)(2,1)S(1)} %add_convert_fusion.after), channel_id=1, source_target_pairs={{0,2},{1,3},{2,0},{3,1},{4,6},{5,7},{6,4},{7,5},{8,10},{9,11},{10,... | collective-permute-start | bytes 1572872 | tf_op jit(solution)/shard_map/ppermute | solution.py:442
  13.0 9.3 %collective-permute-start.1 = (bf16[8,768]{1,0:T(8,128)(2,1)S(1)}, bf16[8,768]{1,0:T(8,128)(2,1)S(1)}, u32[]{:S(2)}, u32[]{:S(2)}) collective-permute-start(bf16[8,768]{1,0:T(8,128)(2,1)S(1)} %get-tuple-element.40), channel_id=1, source_target_pairs={{0,4},{4,0},{8,12},{12,8},{1,5},{5,1},{9,13},{13,9},{2,6},{6,2},{1... | collective-permute-start | bytes 36872 | tf_op jit(solution)/shard_map/ppermute | solution.py:507
  14.6 7.7 %collective-permute-start.2 = (bf16[8,768]{1,0:T(8,128)(2,1)S(1)}, bf16[8,768]{1,0:T(8,128)(2,1)S(1)}, u32[]{:S(2)}, u32[]{:S(2)}) collective-permute-start(bf16[8,768]{1,0:T(8,128)(2,1)S(1)} %get-tuple-element.41), channel_id=1, source_target_pairs={{0,8},{4,12},{8,0},{12,4},{1,9},{5,13},{9,1},{13,5},{2,10},{6,14},... | collective-permute-start | bytes 36872 | tf_op jit(solution)/shard_map/ppermute | solution.py:507
  17.2 5.5 %collective-permute-start.3 = (bf16[8,768]{1,0:T(8,128)(2,1)S(1)}, bf16[8,768]{1,0:T(8,128)(2,1)S(1)}, u32[]{:S(2)}, u32[]{:S(2)}) collective-permute-start(bf16[8,768]{1,0:T(8,128)(2,1)S(1)} %get-tuple-element.42), channel_id=1, source_target_pairs={{0,12},{4,8},{8,4},{12,0},{1,13},{5,9},{9,5},{13,1},{2,14},{6,10},... | collective-permute-start | bytes 36872 | tf_op jit(solution)/shard_map/ppermute | solution.py:507
  24.7 1.8 %collective-permute-start.5 = (bf16[96,2048]{1,0:T(8,128)(2,1)S(1)}, bf16[96,2048]{1,0:T(8,128)(2,1)S(1)}, u32[]{:S(2)}, u32[]{:S(2)}) collective-permute-start(bf16[96,2048]{1,0:T(8,128)(2,1)S(1)} %get-tuple-element.44), channel_id=1, source_target_pairs={{0,1},{1,0},{2,3},{3,2},{4,5},{5,4},{6,7},{7,6},{8,9},{9,8},{10,11... | collective-permute-start | bytes 1179656 | tf_op jit(solution)/shard_map/ppermute | solution.py:536
  26.6 13.0 %collective-permute-start.9 = (bf16[96,2048]{1,0:T(8,128)(2,1)S(1)}, bf16[96,2048]{1,0:T(8,128)(2,1)S(1)}, u32[]{:S(2)}, u32[]{:S(2)}) collective-permute-start(bf16[96,2048]{1,0:T(8,128)(2,1)S(1)} %add_convert_fusion.1.after), channel_id=1, source_target_pairs={{0,2},{1,3},{2,0},{3,1},{4,6},{5,7},{6,4},{7,5},{8,10},{9,11},{10,... | collective-permute-start | bytes 1179656 | tf_op jit(solution)/shard_map/ppermute | solution.py:442
  27.1 5.5 %collective-permute-start.6 = (bf16[8,512]{1,0:T(8,128)(2,1)S(1)}, bf16[8,512]{1,0:T(8,128)(2,1)S(1)}, u32[]{:S(2)}, u32[]{:S(2)}) collective-permute-start(bf16[8,512]{1,0:T(8,128)(2,1)S(1)} %get-tuple-element.46), channel_id=1, source_target_pairs={{0,4},{4,0},{8,12},{12,8},{1,5},{5,1},{9,13},{13,9},{2,6},{6,2},{1... | collective-permute-start | bytes 24584 | tf_op jit(solution)/shard_map/ppermute | solution.py:537
  28.7 4.5 %collective-permute-start.7 = (bf16[8,512]{1,0:T(8,128)(2,1)S(1)}, bf16[8,512]{1,0:T(8,128)(2,1)S(1)}, u32[]{:S(2)}, u32[]{:S(2)}) collective-permute-start(bf16[8,512]{1,0:T(8,128)(2,1)S(1)} %get-tuple-element.47), channel_id=1, source_target_pairs={{0,8},{4,12},{8,0},{12,4},{1,9},{5,13},{9,1},{13,5},{2,10},{6,14},... | collective-permute-start | bytes 24584 | tf_op jit(solution)/shard_map/ppermute | solution.py:537
  31.3 5.4 %collective-permute-start.8 = (bf16[8,512]{1,0:T(8,128)(2,1)S(1)}, bf16[8,512]{1,0:T(8,128)(2,1)S(1)}, u32[]{:S(2)}, u32[]{:S(2)}) collective-permute-start(bf16[8,512]{1,0:T(8,128)(2,1)S(1)} %get-tuple-element.48), channel_id=1, source_target_pairs={{0,12},{4,8},{8,4},{12,0},{1,13},{5,9},{9,5},{13,1},{2,14},{6,10},... | collective-permute-start | bytes 24584 | tf_op jit(solution)/shard_map/ppermute | solution.py:537
  39.0 1.6 %collective-permute-start.10 = (bf16[64,2048]{1,0:T(8,128)(2,1)S(1)}, bf16[64,2048]{1,0:T(8,128)(2,1)S(1)}, u32[]{:S(2)}, u32[]{:S(2)}) collective-permute-start(bf16[64,2048]{1,0:T(8,128)(2,1)S(1)} %get-tuple-element.50), channel_id=1, source_target_pairs={{0,1},{1,0},{2,3},{3,2},{4,5},{5,4},{6,7},{7,6},{8,9},{9,8},{10,11... | collective-permute-start | bytes 786440 | tf_op jit(solution)/shard_map/ppermute | solution.py:572
  39.0 2.8 %collective-permute-start.12 = (bf16[224,1024]{1,0:T(8,128)(2,1)S(1)}, bf16[224,1024]{1,0:T(8,128)(2,1)S(1)}, u32[]{:S(2)}, u32[]{:S(2)}) collective-permute-start(bf16[224,1024]{1,0:T(8,128)(2,1)S(1)} %get-tuple-element.51), channel_id=1, source_target_pairs={{0,1},{1,0},{2,3},{3,2},{4,5},{5,4},{6,7},{7,6},{8,9},{9,8},{10,11... | collective-permute-start | bytes 1376264 | tf_op jit(solution)/shard_map/ppermute | solution.py:557
  39.5 2.3 %collective-permute-start.13 = (bf16[224,1024]{1,0:T(8,128)(2,1)S(1)}, bf16[224,1024]{1,0:T(8,128)(2,1)S(1)}, u32[]{:S(2)}, u32[]{:S(2)}) collective-permute-start(bf16[224,1024]{1,0:T(8,128)(2,1)S(1)} %get-tuple-element.52), channel_id=1, source_target_pairs={{0,1},{1,0},{2,3},{3,2},{4,5},{5,4},{6,7},{7,6},{8,9},{9,8},{10,11... | collective-permute-start | bytes 1376264 | tf_op jit(solution)/shard_map/ppermute | solution.py:557
  40.6 5.6 %collective-permute-start.11 = (bf16[32,2048]{1,0:T(8,128)(2,1)S(1)}, bf16[32,2048]{1,0:T(8,128)(2,1)S(1)}, u32[]{:S(2)}, u32[]{:S(2)}) collective-permute-start(bf16[32,2048]{1,0:T(8,128)(2,1)S(1)} %fusion), channel_id=1, source_target_pairs={{0,2},{1,3},{2,0},{3,1},{4,6},{5,7},{6,4},{7,5},{8,10},{9,11},{10,... | collective-permute-start | bytes 393224 | tf_op jit(solution)/shard_map/ppermute | solution.py:442
where the time goes:
time: 47.9 us; the launch traced here: 47.6 us
  Pallas kernels  21.4 us (45%)
  starting transfers between devices  14.7 us (31%)
  waiting for transfers between devices  11.2 us (23%)
    pallas_call x1, Pallas kernels, on_device(): pl.pallas_call(functools.partial(first_kernel, inst_count, rounds), out_s...  7.89 us
    pallas_call x1, Pallas kernels, on_device(): pl.pallas_call(functools.partial(second_kernel, inst_count, first_count),...  4.86 us
    ppermute x3, starting transfers between devices, send_far(): lax.ppermute(part, 'tp', [(t, (t + 2 * d) % tp_count) for t in range(tp_c...  4.75 us
    ppermute x3, starting transfers between devices, on_device(): lax.ppermute(answer, 'inst', pairs[k])  4.39 us
    ppermute x3, starting transfers between devices, on_device(): lax.ppermute(pack, 'inst', pairs[k])  4.39 us
    ppermute x3, waiting for transfers between devices, on_device(): lax.ppermute(answer, 'inst', pairs[k])  4.09 us
    ppermute x3, waiting for transfers between devices, on_device(): mate = lax.ppermute(send, 'tp', swap)  3.72 us
    ppermute x3, waiting for transfers between devices, send_far(): lax.ppermute(part, 'tp', [(t, (t + 2 * d) % tp_count) for t in range(tp_c...  2.94 us
  transfers between devices with their start and end apart: 14, of which 9 were waited for; matrix products, arithmetic and copies ran while one was open for 0% of the time, Pallas kernels for 25%

commit v1 on v0

--- a/solution.py
+++ b/solution.py
@@ -9,8 +9,9 @@
 
 LOG2E = 1.4426950408889634
 MASKED = -1e30
-GROUP = 6
+GROUP = 8
 NEVER = 2**30
+PIECES = 2
 
 VMEM = pl.BlockSpec(memory_space=pltpu.VMEM)
 SMEM = pl.BlockSpec(memory_space=pltpu.SMEM)
@@ -158,23 +159,29 @@
 
 
 def away_kernel(
-    inst_count, rounds, lengths, migration, pages, second, far_weight, *refs
+    inst_count, rounds, lengths, page_table, migration, pool, second, weight, *refs
 ):
     count = len(rounds)
-    received, answers, (keep, send) = refs[:count], refs[count : 2 * count], refs[2 * count :]
-    _, page_count, page_len, _ = pages.shape
+    received, answers = refs[:count], refs[count : 2 * count]
+    keep, send, buffer, sems = refs[2 * count :]
+    page_count, slot_count = page_table.shape
     step_count, width = answers[0].shape
-    first = lax.axis_index("inst") * (lengths.shape[0] // inst_count)
+    first = lax.axis_index("inst") * slot_count
+    slots = [away_slot(migration, inst_count, k) for k in rounds]
+    for i, slot in enumerate(slots):
+        page_copies(pool, buffer, sems, page_table, i, slot)
+    project_far(second, weight, keep, send)
+    for i in range(count):
+        wait_copies(pool, buffer, sems, i)
     result = attend_group(
         [ref[:, :width].astype(jnp.float32) for ref in received],
         [ref[:, width:].astype(jnp.float32) for ref in received],
-        [[pages.at[i, j] for j in range(page_count)] for i in range(count)],
-        [lengths[first + away_slot(migration, inst_count, k)] * page_len for k in rounds],
+        [[buffer.at[i, j] for j in range(page_count)] for i in range(count)],
+        [lengths[first + slot] * pool.shape[1] for slot in slots],
         step_count,
     )
     for answer, rows in zip(answers, result):
         answer[...] = rows.astype(answer.dtype)
-    project_far(second, far_weight, keep, send)
 
 
 def project(rows, weight, first, columns, target, row_offset=0, offset=0):
@@ -187,18 +194,19 @@
         ).astype(target.dtype)
 
 
-def project_far(attended, far_weight, keep, send):
+def project_far(attended, weight, keep, send, stacked=False):
     core = lax.rem(lax.axis_index("tp"), 2)
+    chip = lax.axis_index("tp") // 2
     chips = lax.axis_size("tp") // 2
-    columns = far_weight.shape[1] // (2 * chips - 2)
+    columns = weight.shape[1] // (2 * chips)
     for target, side in ((send, 1 - core), (keep, core)):
-        for d in range(chips - 1):
-            first = (2 * d + side) * columns
-            project(attended, far_weight, first, columns, target, 0, d * columns)
-
-
-def attend_slots(slots, lengths, queries, new_tokens, pages, wait=lambda i: None):
-    page_count, page_len = pages.shape[1:3]
+        for d in range(1, chips):
+            first = (2 * lax.rem(chip + d, chips) + side) * columns
+            row, column = ((d - 1) * attended.shape[0], 0) if stacked else (0, (d - 1) * columns)
+            project(attended, weight, first, columns, target, row, column)
+
+
+def attend_slots(slots, lengths, queries, new_tokens, pages_of, page_len, wait=lambda i: None):
     first = lax.axis_index("inst") * queries.shape[0]
     rows = []
     for base in range(0, len(slots), GROUP):
@@ -208,7 +216,7 @@
         rows += attend_group(
             [queries[slots[i]].astype(jnp.float32) for i in items],
             [new_tokens[slots[i]].astype(jnp.float32) for i in items],
-            [[pages.at[i, j] for j in range(page_count)] for i in items],
+            [pages_of(i) for i in items],
             [lengths[first + slots[i]] * page_len for i in items],
             queries.shape[1],
         )
@@ -225,14 +233,11 @@
 
 
 def first_kernel(
-    inst_count, rounds, migration, lengths, page_table, queries_in, new_in, pool, weight,
-    attended, keep, send, far_weight, queries, new_tokens, second_pages, away_pages, *refs,
+    inst_count, rounds, migration, lengths, page_table, queries_in, new_in, pool,
+    attended, queries, new_tokens, *refs,
 ):
     packs = dict(zip(rounds, refs))
-    buffer, small_sems, first_sems, second_sems, away_sems, weight_sems = refs[len(rounds) :]
-    own_tp = lax.axis_index("tp")
-    chips = lax.axis_size("tp") // 2
-    pair_columns = weight.shape[1] // chips
+    buffer, small_sems, page_sems = refs[len(rounds) :]
     slot_count, step_count, _ = queries.shape
     small = [
         pltpu.make_async_copy(queries_in, queries, small_sems.at[0]),
@@ -241,94 +246,51 @@
     for copy in small:
         copy.start()
     arrivals, _ = arrivals_of(migration, inst_count)
-    count = attended.shape[0] // step_count
-    total = count + second_pages.shape[0]
-    slots = [slot_at(position, arrivals, slot_count) for position in range(total)]
-    for i in range(count):
-        page_copies(pool, buffer, first_sems, page_table, i, slots[i])
-
-    def weight_copy(d):
-        chip = lax.rem(own_tp // 2 + d, chips)
-        start = pl.multiple_of(chip * pair_columns, pair_columns)
-        return pltpu.make_async_copy(
-            weight.at[:, pl.ds(start, pair_columns)],
-            far_weight.at[:, pl.ds((d - 1) * pair_columns, pair_columns)],
-            weight_sems.at[d - 1],
-        )
-
-    for d in range(1, chips):
-        weight_copy(d).start()
-    for i, slot in enumerate(slots[count:]):
-        page_copies(pool, second_pages, second_sems, page_table, i, slot)
-    for i, k in enumerate(rounds):
-        slot = away_slot(migration, inst_count, k)
-        page_copies(pool, away_pages, away_sems, page_table, i, slot)
+    slots = [
+        slot_at(position, arrivals, slot_count)
+        for position in range(attended.shape[0] // step_count)
+    ]
+    for i, slot in enumerate(slots):
+        page_copies(pool, buffer, page_sems, page_table, i, slot)
     for copy in small:
         copy.wait()
     pack_rows(inst_count, migration, queries, new_tokens, packs)
-    store_rows(
-        attend_slots(
-            slots[:count], lengths, queries, new_tokens, buffer,
-            lambda i: wait_copies(pool, buffer, first_sems, i),
-        ),
-        attended,
-    )
-    for d in range(1, chips):
-        weight_copy(d).wait()
-    project_far(attended, far_weight, keep, send)
-    for i in range(total - count):
-        wait_copies(pool, second_pages, second_sems, i)
-    for i in range(len(rounds)):
-        wait_copies(pool, away_pages, away_sems, i)
+    rows = attend_slots(
+        slots, lengths, queries, new_tokens,
+        lambda i: [buffer.at[i, j] for j in range(buffer.shape[1])],
+        buffer.shape[2],
+        lambda i: wait_copies(pool, buffer, page_sems, i),
+    )
+    store_rows(rows, attended)
+
+
+def far_kernel(attended, weight, keep, send):
+    project_far(attended, weight, keep, send)
 
 
 def second_kernel(
-    inst_count, first, migration, lengths, queries, new_tokens, pages, weight, after,
-    attended, extra, near_weight, sems,
+    inst_count, first, migration, lengths, page_table, queries, new_tokens, pool, after,
+    attended, extra,
 ):
     slot_count, step_count, _ = queries.shape
-    core = lax.rem(lax.axis_index("tp"), 2)
-    chip = lax.axis_index("tp") // 2
-    columns = near_weight.shape[2]
-    copies = []
-    for n, side in enumerate((1 - core, core)):
-        start = pl.multiple_of((chip * 2 + side) * columns, columns)
-        copies.append(
-            pltpu.make_async_copy(
-                weight.at[:, pl.ds(start, columns)], near_weight.at[n], sems.at[n]
-            )
-        )
-        copies[n].start()
+    count = attended.shape[0] // step_count
     arrivals, _ = arrivals_of(migration, inst_count)
-    slots = [slot_at(first + i, arrivals, slot_count) for i in range(pages.shape[0])]
-    rows = attend_slots(slots, lengths, queries, new_tokens, pages)
-    count = attended.shape[0] // step_count
+    slots = [
+        slot_at(first + i, arrivals, slot_count) for i in range(count + extra.shape[0])
+    ]
+    rows = attend_slots(
+        slots, lengths, queries, new_tokens,
+        lambda i: [pool.at[page_table[j, slots[i]]] for j in range(page_table.shape[0])],
+        pool.shape[1],
+    )
     store_rows(rows[:count], attended)
     for i, row in enumerate(rows[count:]):
         extra[i] = row.astype(extra.dtype)
-    for copy in copies:
-        copy.wait()
-
-
-def own_kernel(near_weight, first, second, after, keep, *refs):
-    sends, rows = refs[:-1], refs[-1]
-    rows[: first.shape[0], :] = first[...]
-    rows[first.shape[0] :, :] = second[...]
-    at = 0
-    for send in sends:
-        project(rows, near_weight.at[0], at, send.shape[1], send)
-        at += send.shape[1]
-    project(rows, near_weight.at[1], 0, keep.shape[1], keep)
-
-
-def last_rows_kernel(
-    inst_count, rounds, migration, near_weight, far_weight, extra, after, *refs
-):
-    answers, (keep, send, rows) = refs[:-3], refs[-3:]
-    core = lax.rem(lax.axis_index("tp"), 2)
-    chips = lax.axis_size("tp") // 2
+
+
+def last_rows_kernel(inst_count, rounds, migration, weight, extra, *refs):
+    answers, (rows, keep, send) = refs[:-3], refs[-3:]
     me = lax.axis_index("inst")
-    columns = keep.shape[1]
     _, sources = arrivals_of(migration, inst_count)
     last = [extra[i].astype(jnp.float32) for i in range(extra.shape[0])]
     given = [answer[...].astype(jnp.float32) for answer in answers]
@@ -337,12 +299,24 @@
         for k, answer in zip(rounds[1:], given[1:]):
             row = jnp.where(source == peer_of(me, k, inst_count), answer, row)
         last.append(row)
-    size = rows.shape[0]
     store_rows(last, rows)
-    for n, (target, side) in enumerate(((send, 1 - core), (keep, core))):
-        for d in range(chips - 1):
-            project(rows, far_weight, (2 * d + side) * columns, columns, target, d * size)
-        project(rows, near_weight.at[n], 0, columns, target, (chips - 1) * size)
+    project_far(rows, weight, keep, send, stacked=True)
+
+
+def own_kernel(weight, first, second, last, after, keep, *refs):
+    sends, rows = refs[:-1], refs[-1]
+    core = lax.rem(lax.axis_index("tp"), 2)
+    pair = lax.axis_index("tp") // 2 * 2
+    columns = keep.shape[1]
+    at = 0
+    for part in (first, second, last):
+        rows[at : at + part.shape[0], :] = part[...]
+        at += part.shape[0]
+    at = 0
+    for send in sends:
+        project(rows, weight, (pair + 1 - core) * columns + at, send.shape[1], send)
+        at += send.shape[1]
+    project(rows, weight, (pair + core) * columns, columns, keep)
 
 
 def sum_kernel(inst_count, chunks, piece_count, migration, keep, *refs):
@@ -377,20 +351,25 @@
     pltpu.make_async_copy(staged, out.at[pl.ds(0, staged.shape[0])], sem.at[0]).wait()
 
 
-def last_kernel(inst_count, first, migration, keep, mate, *refs):
-    parts, (out, staged, sem) = refs[:-4], refs[-3:]
+def last_kernel(inst_count, first, piece_count, migration, keep, *refs):
+    mates, parts, (out, staged, sem) = refs[:piece_count], refs[piece_count:-4], refs[-3:]
     step_count = out.shape[1]
     pair = 2 * step_count
+    width = mates[0].shape[1]
     size = parts[0].shape[0]
     arrivals, _ = arrivals_of(migration, inst_count)
     for at in range(0, size, pair):
         own = keep.shape[0] - size + at
-        total = keep[own : own + pair, :] + mate[own : own + pair, :].astype(jnp.float32)
-        for part in parts:
-            total = total + part[at : at + pair, :].astype(jnp.float32)
-        total = total.astype(jnp.bfloat16)
-        for half in range(2):
-            staged[at // step_count + half] = total[half * step_count : (half + 1) * step_count]
+        for m, mate in enumerate(mates):
+            columns = slice(m * width, (m + 1) * width)
+            total = keep[own : own + pair, columns] + mate[own : own + pair, :].astype(jnp.float32)
+            for part in parts:
+                total = total + part[at : at + pair, columns].astype(jnp.float32)
+            total = total.astype(jnp.bfloat16)
+            for half in range(2):
+                staged[at // step_count + half, :, columns] = total[
+                    half * step_count : (half + 1) * step_count
+                ]
     scatter_rows(staged, out, arrivals, first, sem)
 
 
@@ -411,10 +390,10 @@
     step_count = row_count // slot_count
     queries = in_hbm(queries.reshape(slot_count, step_count, width))
     new_tokens = in_hbm(new_kv[0].reshape(slot_count, step_count, new_kv.shape[2]))
-    pool = in_hbm(kv_pool[0])
+    pool = kv_pool[0]
     columns = out_weight.shape[1] // tp_count
     incoming = migration.shape[0] // inst_count
-    weight = in_hbm(out_weight)
+    weight = in_vmem(out_weight)
     lengths = in_hbm(lengths)
     page_table = in_hbm(page_table.T)
     migration = in_hbm(migration.T)
@@ -425,17 +404,17 @@
     swap = [(t, t ^ 1) for t in range(tp_count)]
     far = (chips - 1) * columns
 
-    def hold(value, until):
+    def hold(values, until):
         return pl.pallas_call(
             lambda *refs: None,
-            out_shape=pltpu.VMEM(value.shape, value.dtype),
-            in_specs=[ANY] * (1 + len(until)),
-            out_specs=ANY,
-            input_output_aliases={0: 0},
+            out_shape=[pltpu.VMEM(value.shape, value.dtype) for value in values],
+            in_specs=[ANY] * (len(values) + len(until)),
+            out_specs=[ANY] * len(values),
+            input_output_aliases={i: i for i in range(len(values))},
             compiler_params=pltpu.CompilerParams(vmem_limit_bytes=2**20),
             cost_estimate=light,
             name="hold",
-        )(in_vmem(value), *until)
+        )(*[in_vmem(value) for value in values], *until)
 
     def send_far(summed):
         return [
@@ -471,140 +450,124 @@
         if any(peer_of(i, k, inst_count) != i for i in range(inst_count))
     ]
     pairs = {k: [(i, peer_of(i, k, inst_count)) for i in range(inst_count)] for k in rounds}
-    rest_count = second_count + extra_count
-    (
-        first, keep, send, far_weight, queries, new_tokens, second_pages, away_pages, *packs
-    ) = pl.pallas_call(
+    first, queries, new_tokens, *packs = pl.pallas_call(
         functools.partial(first_kernel, inst_count, rounds),
         out_shape=[
             rows_shape(first_count),
-            *chunk_shapes(first_count),
-            pltpu.VMEM((width, 2 * far), bf16),
             pltpu.VMEM(queries.shape, bf16),
             pltpu.VMEM(new_tokens.shape, bf16),
-            page_shape(rest_count),
-            page_shape(len(rounds)),
         ]
         + [shape((step_count, width + new_tokens.shape[2]), bf16)] * len(rounds),
-        in_specs=[SMEM, SMEM, SMEM, ANY, ANY, ANY, ANY],
-        out_specs=[VMEM] * (8 + len(rounds)),
-        scratch_shapes=[
-            page_shape(first_count),
-            dma((2,)),
-            dma((first_count,)),
-            dma((rest_count,)),
-            dma((len(rounds),)),
-            dma((chips - 1,)),
-        ],
+        in_specs=[SMEM, SMEM, SMEM, ANY, ANY, ANY],
+        out_specs=[VMEM] * (3 + len(rounds)),
+        scratch_shapes=[page_shape(first_count), dma((2,)), dma((first_count,))],
         compiler_params=limit,
         cost_estimate=light,
         name="attend_first",
-    )(migration, lengths, page_table, queries, new_tokens, pool, weight)
-    far_weight = in_vmem(far_weight)
+    )(migration, lengths, page_table, queries, new_tokens, in_hbm(pool))
+    first, queries, new_tokens = in_vmem(first), in_vmem(queries), in_vmem(new_tokens)
+    keep, send = pl.pallas_call(
+        far_kernel,
+        out_shape=chunk_shapes(first_count),
+        in_specs=[VMEM] * 2,
+        out_specs=[VMEM] * 2,
+        compiler_params=limit,
+        cost_estimate=light,
+        name="far_first",
+    )(first, weight)
     mate = lax.ppermute(send, "tp", swap)
     summed = (keep + mate.astype(f32)).astype(bf16)
     arrived_first = send_far(split_far(summed))
+    packs = hold(packs, [summed])
     received = [lax.ppermute(pack, "inst", pairs[k]) for k, pack in zip(rounds, packs)]
 
-    second, extra, near_weight = pl.pallas_call(
+    second, extra = pl.pallas_call(
         functools.partial(second_kernel, inst_count, first_count),
         out_shape=[
             rows_shape(second_count),
             pltpu.VMEM((extra_count, step_count, width), bf16),
-            pltpu.VMEM((2, width, columns), bf16),
         ],
-        in_specs=[SMEM, SMEM, VMEM, VMEM, VMEM, ANY, ANY],
-        out_specs=[VMEM] * 3,
-        scratch_shapes=[dma((2,))],
+        in_specs=[SMEM, SMEM, SMEM, VMEM, VMEM, VMEM, ANY],
+        out_specs=[VMEM] * 2,
         compiler_params=limit,
         cost_estimate=light,
         name="attend_second",
-    )(
-        migration, lengths, in_vmem(queries), in_vmem(new_tokens), in_vmem(second_pages), weight,
-        summed,
-    )
-    second, near_weight = in_vmem(second), in_vmem(near_weight)
+    )(migration, lengths, page_table, queries, new_tokens, in_vmem(pool), summed)
+    second = in_vmem(second)
     *answers, keep, send = pl.pallas_call(
         functools.partial(away_kernel, inst_count, rounds),
         out_shape=[shape((step_count, width), bf16)] * len(rounds) + chunk_shapes(second_count),
-        in_specs=[SMEM, SMEM] + [VMEM] * (3 + len(rounds)),
+        in_specs=[SMEM, SMEM, SMEM, ANY] + [VMEM] * (2 + len(rounds)),
         out_specs=[VMEM] * (2 + len(rounds)),
+        scratch_shapes=[page_shape(len(rounds)), dma((len(rounds),))],
         compiler_params=limit,
         cost_estimate=light,
         name="attend_away",
-    )(lengths, migration, in_vmem(away_pages), second, far_weight, *received)
+    )(lengths, page_table, migration, in_hbm(pool), second, weight, *received)
     mate = lax.ppermute(send, "tp", swap)
     answers = [lax.ppermute(answer, "inst", pairs[k]) for k, answer in zip(rounds, answers)]
-    keep = hold(keep, arrived_first)
+    (keep,) = hold([keep], arrived_first)
     summed = (keep + mate.astype(f32)).astype(bf16)
     arrived_second = send_far(split_far(summed))
 
-    early_rows = (first_count + second_count) * step_count
-    pieces = 2
-    early_keep, *early_sends = pl.pallas_call(
+    last, keep, send = pl.pallas_call(
+        functools.partial(last_rows_kernel, inst_count, rounds),
+        out_shape=[
+            rows_shape(last_count),
+            pltpu.VMEM((last_rows * (chips - 1), columns), f32),
+            pltpu.VMEM((last_rows * (chips - 1), columns), bf16),
+        ],
+        in_specs=[SMEM] + [VMEM] * (2 + len(rounds)),
+        out_specs=[VMEM] * 3,
+        compiler_params=limit,
+        cost_estimate=light,
+        name="last_rows",
+    )(migration, weight, in_vmem(extra), *answers)
+    mate = lax.ppermute(send, "tp", swap)
+    own_keep, *own_sends = pl.pallas_call(
         own_kernel,
         out_shape=[
-            pltpu.VMEM((early_rows, columns), f32),
-            *[pltpu.VMEM((early_rows, columns // pieces), bf16)] * pieces,
+            pltpu.VMEM((row_count, columns), f32),
+            *[pltpu.VMEM((row_count, columns // PIECES), bf16)] * PIECES,
         ],
-        in_specs=[VMEM, VMEM, VMEM, ANY],
-        out_specs=[VMEM] * (1 + pieces),
-        scratch_shapes=[pltpu.VMEM((early_rows, width), bf16)],
+        in_specs=[VMEM] * 4 + [ANY],
+        out_specs=[VMEM] * (1 + PIECES),
+        scratch_shapes=[pltpu.VMEM((row_count, width), bf16)],
         compiler_params=limit,
         cost_estimate=light,
         name="own_columns",
-    )(near_weight, in_vmem(first), second, summed)
-    early_mates = [lax.ppermute(early_send, "tp", swap) for early_send in early_sends]
-
-    keep, send = pl.pallas_call(
-        functools.partial(last_rows_kernel, inst_count, rounds),
-        out_shape=[
-            pltpu.VMEM((last_rows * chips, columns), f32),
-            pltpu.VMEM((last_rows * chips, columns), bf16),
-        ],
-        in_specs=[SMEM] + [VMEM] * 3 + [ANY] + [VMEM] * len(rounds),
-        out_specs=[VMEM] * 2,
-        scratch_shapes=[pltpu.VMEM((last_rows, width), bf16)],
-        compiler_params=limit,
-        cost_estimate=light,
-        name="last_rows",
-    )(migration, near_weight, far_weight, in_vmem(extra), early_keep, *answers)
-    mate = lax.ppermute(send, "tp", swap)
-    keep = hold(keep, arrived_second)
-    summed = (keep[:-last_rows] + mate[:-last_rows].astype(f32)).astype(bf16)
+    )(weight, first, second, in_vmem(last), summed)
+    own_keep = in_vmem(own_keep)
+    own_mates = [lax.ppermute(own_send, "tp", swap) for own_send in own_sends]
+    (keep,) = hold([keep], [*arrived_second, own_keep])
+    summed = (keep + mate.astype(f32)).astype(bf16)
     arrived_last = send_far([summed[d * last_rows : (d + 1) * last_rows] for d in range(chips - 1)])
 
     early = slot_count - last_count
     out_shape = (slot_count, step_count, columns)
     out = pl.pallas_call(
         functools.partial(
-            sum_kernel, inst_count, [first_count * step_count, second_count * step_count], pieces
+            sum_kernel, inst_count, [first_count * step_count, second_count * step_count], PIECES
         ),
         out_shape=pltpu.HBM(out_shape, bf16),
-        in_specs=[SMEM] + [VMEM] * (1 + pieces + 2 * (chips - 1)),
+        in_specs=[SMEM] + [VMEM] * (1 + PIECES + 2 * (chips - 1)),
         out_specs=ANY,
-        scratch_shapes=[
-            pltpu.VMEM((early, step_count, columns), bf16),
-            pltpu.SemaphoreType.DMA((1,)),
-        ],
+        scratch_shapes=[pltpu.VMEM((early, step_count, columns), bf16), dma((1,))],
         compiler_params=limit,
         cost_estimate=light,
         name="sum_early",
-    )(migration, in_vmem(early_keep), *early_mates, *arrived_first, *arrived_second)
+    )(migration, own_keep, *own_mates, *arrived_first, *arrived_second)
     out = pl.pallas_call(
-        functools.partial(last_kernel, inst_count, early),
+        functools.partial(last_kernel, inst_count, early, PIECES),
         out_shape=pltpu.HBM(out_shape, bf16),
-        in_specs=[SMEM] + [VMEM] * (chips + 1) + [ANY],
+        in_specs=[SMEM] + [VMEM] * (PIECES + chips) + [ANY],
         out_specs=ANY,
-        scratch_shapes=[
-            pltpu.VMEM((last_count, step_count, columns), bf16),
-            pltpu.SemaphoreType.DMA((1,)),
-        ],
-        input_output_aliases={2 + chips: 0},
+        scratch_shapes=[pltpu.VMEM((last_count, step_count, columns), bf16), dma((1,))],
+        input_output_aliases={PIECES + chips + 1: 0},
         compiler_params=limit,
         cost_estimate=light,
         name="sum_last",
-    )(migration, in_vmem(keep), mate, *arrived_last, out)
+    )(migration, own_keep, *own_mates, *arrived_last, out)
     return out.reshape(row_count, columns)
 
 

time: 47.9 us -> 46.5 us (0.971)
  Pallas kernels: 21.4 us -> 18.4 us
  waiting for transfers between devices: 11.2 us -> 13.4 us
  starting transfers between devices: 14.7 us -> 14.1 us
    pallas_call x1, Pallas kernels: 4.86 us -> 2.47 us  [on_device(): pl.pallas_call(functools.partial(second_kernel, inst_count, first_count),...]
    ppermute x3, waiting for transfers between devices: 0.39 us -> 2.76 us  [on_device(): lax.ppermute(pack, 'inst', pairs[k])]
    pallas_call x1, Pallas kernels: 7.89 us -> 5.65 us  [on_device(): pl.pallas_call(functools.partial(first_kernel, inst_count, rounds), out_s...]
    ppermute x2, waiting for transfers between devices: 0.07 us -> 1.58 us  [on_device(): own_mates = [lax.ppermute(own_send, 'tp', swap) for own_send in own_sends]]
    pallas_call x1, Pallas kernels: 2 us -> 3.32 us  [on_device(): pl.pallas_call(functools.partial(away_kernel, inst_count, rounds), out_sh...]
    ppermute x3, waiting for transfers between devices: 2.94 us -> 1.88 us  [send_far(): lax.ppermute(part, 'tp', [(t, (t + 2 * d) % tp_count) for t in range(tp_c...]
    pallas_call x4 -> x6, Pallas kernels: 2.53 us -> 3.55 us  [the longest x1 1.4 us: on_device(): pl.pallas_call(functools.partial(last_kernel, inst_count, early, PIECES),...]
    pallas_call x1, Pallas kernels: 2.26 us -> 1.55 us  [on_device(): pl.pallas_call(functools.partial(last_rows_kernel, inst_count, rounds), o...]
  transfers between devices with their start and end apart: 14 -> 14, of which waited for: 9 -> 8; matrix products, arithmetic and copies ran while one was open for 0% -> 0% of each run, Pallas kernels for 25% -> 23%
where the time goes in v1:
time: 46.5 us; the launch traced here: 46.2 us
  Pallas kernels  18.4 us (40%)
  starting transfers between devices  14.1 us (30%)
  waiting for transfers between devices  13.4 us (29%)
    pallas_call x1, Pallas kernels, on_device(): pl.pallas_call(functools.partial(first_kernel, inst_count, rounds), out_s...  5.65 us
    ppermute x3, starting transfers between devices, on_device(): lax.ppermute(pack, 'inst', pairs[k])  4.39 us
    ppermute x3, starting transfers between devices, on_device(): lax.ppermute(answer, 'inst', pairs[k])  4.39 us
    ppermute x3, starting transfers between devices, send_far(): lax.ppermute(part, 'tp', [(t, (t + 2 * d) % tp_count) for t in range(tp_c...  4.13 us
    ppermute x3, waiting for transfers between devices, on_device(): lax.ppermute(answer, 'inst', pairs[k])  3.9 us
    pallas_call x1, Pallas kernels, on_device(): pl.pallas_call(functools.partial(away_kernel, inst_count, rounds), out_sh...  3.32 us
    ppermute x3, waiting for transfers between devices, on_device(): mate = lax.ppermute(send, 'tp', swap)  3.23 us
    ppermute x3, waiting for transfers between devices, on_device(): lax.ppermute(pack, 'inst', pairs[k])  2.76 us
  transfers between devices with their start and end apart: 14, of which 8 were waited for; matrix products, arithmetic and copies ran while one was open for 0% of the time, Pallas kernels for 23%

profile of v1, /device:TPU:0, one launch (start us, length us, event | category | flops | bytes accessed | tf_op | source)
XLA Modules:
  0.0 46.2 jit_solution(16097339826288807294)
XLA Ops:
  0.0 0.0 copy-start
  0.0 0.0 copy-start.1
  0.0 5.6 %attend_first.1 = (bf16[128,512]{1,0:T(8,128)(2,1)S(1)}, bf16[32,8,512]{2,1,0:T(8,128)(2,1)S(1)}, bf16[32,8,256]{2,1,0:T(8,128)(2,1)S(1)}, bf16[8,768]{1,0:T(8,1...) custom-call(s32[4,12]{1,0:T(4,128)} %bitcast.11, s32[128]{0:T(128)} %lengths.5, s32[4,32]{1,0:T(4,128)} %bitcast.17, ...), custom_call_target="tpu_custom_call" | custom-call | flops 1 | bytes 1 | tf_op jit(solution)/shard_map/attend_first/pallas_call | solution.py:453
  5.7 0.0 copy-done
  5.7 0.8 %far_first.1 = (f32[128,2048]{1,0:T(8,128)S(1)}, bf16[128,2048]{1,0:T(8,128)(2,1)S(1)}) custom-call(bf16[128,512]{1,0:T(8,128)(2,1)S(1)} %get-tuple-element.29.attended.first, bf16[512,8192]{1,0:T(8,128)(2,1)S(1)} %copy-done), custom_call_target="tpu_custom_call" | custom-call | flops 1 | bytes 1 | tf_op jit(solution)/shard_map/far_first/pallas_call | solution.py:469
  6.5 0.5 %collective-permute-start = (bf16[128,2048]{1,0:T(8,128)(2,1)S(1)}, bf16[128,2048]{1,0:T(8,128)(2,1)S(1)}, u32[]{:S(2)}, u32[]{:S(2)}) collective-permute-start(bf16[128,2048]{1,0:T(8,128)(2,1)S(1)} %get-tuple-element.33), channel_id=1, source_target_pairs={{0,1},{1,0},{2,3},{3,2},{4,5},{5,4},{6,7},{7,6},{8,9},{9,8},{10,11... | collective-permute-start | bytes 1572872 | tf_op jit(solution)/shard_map/ppermute | solution.py:478
  7.0 1.5 %collective-permute-done = bf16[128,2048]{1,0:T(8,128)(2,1)S(1)} collective-permute-done((bf16[128,2048]{1,0:T(8,128)(2,1)S(1)}, bf16[128,2048]{1,0:T(8,128)(2,1)S(1)}, u32[]{:S(2)}, u32[]{:S(2)}) %collective-permute-start) | collective-permute-done | bytes 524320 | tf_op jit(solution)/shard_map/ppermute | solution.py:478
  8.5 0.1 add_convert_fusion.after.refs_3_
  8.7 3.0 %collective-permute-start.7 = (bf16[128,2048]{1,0:T(8,128)(2,1)S(1)}, bf16[128,2048]{1,0:T(8,128)(2,1)S(1)}, u32[]{:S(2)}, u32[]{:S(2)}) collective-permute-start(bf16[128,2048]{1,0:T(8,128)(2,1)S(1)} %add_convert_fusion.after.refs_3_), channel_id=1, source_target_pairs={{0,2},{1,3},{2,0},{3,1},{4,6},{5,7},{6,4},{7,5},{8,10},{9,11},{10,... | collective-permute-start | bytes 1572872 | tf_op jit(solution)/shard_map/ppermute | solution.py:421
  11.6 1.6 %collective-permute-start.1 = (bf16[8,768]{1,0:T(8,128)(2,1)S(1)}, bf16[8,768]{1,0:T(8,128)(2,1)S(1)}, u32[]{:S(2)}, u32[]{:S(2)}) collective-permute-start(bf16[8,768]{1,0:T(8,128)(2,1)S(1)} %get-tuple-element.39), channel_id=1, source_target_pairs={{0,4},{4,0},{8,12},{12,8},{1,5},{5,1},{9,13},{13,9},{2,6},{6,2},{1... | collective-permute-start | bytes 36872 | tf_op jit(solution)/shard_map/ppermute | solution.py:482
  13.2 2.6 %collective-permute-start.2 = (bf16[8,768]{1,0:T(8,128)(2,1)S(1)}, bf16[8,768]{1,0:T(8,128)(2,1)S(1)}, u32[]{:S(2)}, u32[]{:S(2)}) collective-permute-start(bf16[8,768]{1,0:T(8,128)(2,1)S(1)} %get-tuple-element.40), channel_id=1, source_target_pairs={{0,8},{4,12},{8,0},{12,4},{1,9},{5,13},{9,1},{13,5},{2,10},{6,14},... | collective-permute-start | bytes 36872 | tf_op jit(solution)/shard_map/ppermute | solution.py:482
  15.8 0.3 collective-permute-start.3
  16.0 0.0 copy-done.1
  16.0 2.5 %attend_second.1 = (bf16[96,512]{1,0:T(8,128)(2,1)S(1)}, bf16[1,8,512]{2,1,0:T(8,128)(2,1)S(1)}) custom-call(s32[4,12]{1,0:T(4,128)} %bitcast.12, s32[128]{0:T(128)} %lengths.5, s32[4,32]{1,0:T(4,128)} %bitcast.18, bf16[32,8,512]{2,1,0:T(8,128)(2,1)S(1)} %get-tuple-element.30.queries, bf16[32,8,256]{2,1,0:T(8,128)(2,1)S(1)} %get-tuple-element.31.new_tokens, ...), custom_call_target="tpu_custom_call" | custom-call | flops 1 | bytes 1 | tf_op jit(solution)/shard_map/attend_second/pallas_call | solution.py:484
  18.5 0.0 collective-permute-done.1.refs_0_
  18.5 0.0 collective-permute-done.2.refs_1_
  18.5 2.8 %collective-permute-done.3.refs_2_ = bf16[8,768]{1,0:T(8,128)(2,1)S(1)} collective-permute-done((bf16[8,768]{1,0:T(8,128)(2,1)S(1)}, bf16[8,768]{1,0:T(8,128)(2,1)S(1)}, u32[]{:S(2)}, u32[]{:S(2)}) %collective-permute-start.3) | collective-permute-done | bytes 12320 | tf_op jit(solution)/shard_map/ppermute | solution.py:482
  21.2 3.3 %attend_away.1 = (bf16[8,512]{1,0:T(8,128)(2,1)S(1)}, bf16[8,512]{1,0:T(8,128)(2,1)S(1)}, bf16[8,512]{1,0:T(8,128)(2,1)S(1)}, f32[96,2048]{1,0:T(8,128)S(1)}, bf16[96,2048]{1,0:T(8,128)(2,1)S(1)}) custom-call(s32[128]{0:T(128)} %lengths.5, s32[4,32]{1,0:T(4,128)} %bitcast.19, s32[4,12]{1,0:T(4,128)} %bitcast.13, bf16[128,128,256]{2,1,0:T(8,128)(2,1)} %bitcast.7, ...), custom_call_target="tpu_custom_call" | custom-call | flops 1 | bytes 1 | tf_op jit(solution)/shard_map/attend_away/pallas_call | solution.py:497
  24.6 0.1 collective-permute-start.8
  24.6 0.0 collective-permute-done.7.refs_1_.refs_2_
  24.7 1.7 %collective-permute-done.8 = bf16[96,2048]{1,0:T(8,128)(2,1)S(1)} collective-permute-done((bf16[96,2048]{1,0:T(8,128)(2,1)S(1)}, bf16[96,2048]{1,0:T(8,128)(2,1)S(1)}, u32[]{:S(2)}, u32[]{:S(2)}) %collective-permute-start.8) | collective-permute-done | bytes 393248 | tf_op jit(solution)/shard_map/ppermute | solution.py:507
  26.4 0.1 add_convert_fusion.1.after
  26.5 0.6 %collective-permute-start.11 = (bf16[96,2048]{1,0:T(8,128)(2,1)S(1)}, bf16[96,2048]{1,0:T(8,128)(2,1)S(1)}, u32[]{:S(2)}, u32[]{:S(2)}) collective-permute-start(bf16[96,2048]{1,0:T(8,128)(2,1)S(1)} %add_convert_fusion.1.after), channel_id=1, source_target_pairs={{0,2},{1,3},{2,0},{3,1},{4,6},{5,7},{6,4},{7,5},{8,10},{9,11},{10,... | collective-permute-start | bytes 1179656 | tf_op jit(solution)/shard_map/ppermute | solution.py:421
  27.0 0.3 collective-permute-start.4
  27.3 2.6 %collective-permute-start.5 = (bf16[8,512]{1,0:T(8,128)(2,1)S(1)}, bf16[8,512]{1,0:T(8,128)(2,1)S(1)}, u32[]{:S(2)}, u32[]{:S(2)}) collective-permute-start(bf16[8,512]{1,0:T(8,128)(2,1)S(1)} %get-tuple-element.43), channel_id=1, source_target_pairs={{0,8},{4,12},{8,0},{12,4},{1,9},{5,13},{9,1},{13,5},{2,10},{6,14},... | collective-permute-start | bytes 24584 | tf_op jit(solution)/shard_map/ppermute | solution.py:508
  29.9 1.5 %collective-permute-start.6 = (bf16[8,512]{1,0:T(8,128)(2,1)S(1)}, bf16[8,512]{1,0:T(8,128)(2,1)S(1)}, u32[]{:S(2)}, u32[]{:S(2)}) collective-permute-start(bf16[8,512]{1,0:T(8,128)(2,1)S(1)} %get-tuple-element.44), channel_id=1, source_target_pairs={{0,12},{4,8},{8,4},{12,0},{1,13},{5,9},{9,5},{13,1},{2,14},{6,10},... | collective-permute-start | bytes 24584 | tf_op jit(solution)/shard_map/ppermute | solution.py:508
  31.4 0.0 collective-permute-done.4.refs_0_
  31.4 0.4 collective-permute-done.5.refs_1_
  31.9 3.5 %collective-permute-done.6.refs_2_ = bf16[8,512]{1,0:T(8,128)(2,1)S(1)} collective-permute-done((bf16[8,512]{1,0:T(8,128)(2,1)S(1)}, bf16[8,512]{1,0:T(8,128)(2,1)S(1)}, u32[]{:S(2)}, u32[]{:S(2)}) %collective-permute-start.6) | collective-permute-done | bytes 8224 | tf_op jit(solution)/shard_map/ppermute | solution.py:508
  35.3 1.5 %last_rows.1 = (bf16[32,512]{1,0:T(8,128)(2,1)S(1)}, f32[32,2048]{1,0:T(8,128)S(1)}, bf16[32,2048]{1,0:T(8,128)(2,1)S(1)}) custom-call(s32[4,12]{1,0:T(4,128)} %bitcast.14, bf16[512,8192]{1,0:T(8,128)(2,1)S(1)} %copy-done, bf16[1,8,512]{2,1,0:T(8,128)(2,1)S(1)} %get-tuple-element.35.extra, bf16[8,512]{1,0:T(8,128)(2,1)S(1)} %collective-permute-done.4.refs_0_, ...), custom_call_target="tpu_custom_call" | custom-call | flops 1 | bytes 1 | tf_op jit(solution)/shard_map/last_rows/pallas_call | solution.py:513
  36.9 0.0 collective-permute-start.12
  36.9 1.3 %own_columns.1 = (f32[256,2048]{1,0:T(8,128)S(1)}, bf16[256,1024]{1,0:T(8,128)(2,1)S(1)}, bf16[256,1024]{1,0:T(8,128)(2,1)S(1)}) custom-call(bf16[512,8192]{1,0:T(8,128)(2,1)S(1)} %copy-done, bf16[128,512]{1,0:T(8,128)(2,1)S(1)} %get-tuple-element.29.attended.first, bf16[96,512]{1,0:T(8,128)(2,1)S(1)} %get-tuple-element.34.second, ...), custom_call_target="tpu_custom_call" | custom-call | flops 1 | bytes 1 | tf_op jit(solution)/shard_map/own_columns/pallas_call | solution.py:527
  38.2 0.6 %collective-permute-start.9 = (bf16[256,1024]{1,0:T(8,128)(2,1)S(1)}, bf16[256,1024]{1,0:T(8,128)(2,1)S(1)}, u32[]{:S(2)}, u32[]{:S(2)}) collective-permute-start(bf16[256,1024]{1,0:T(8,128)(2,1)S(1)} %get-tuple-element.49), channel_id=1, source_target_pairs={{0,1},{1,0},{2,3},{3,2},{4,5},{5,4},{6,7},{7,6},{8,9},{9,8},{10,11... | collective-permute-start | bytes 1572872 | tf_op jit(solution)/shard_map/ppermute | solution.py:541
  38.8 0.1 collective-permute-start.10
  38.9 0.0 collective-permute-done.11.refs_1_.refs_3_
  38.9 0.0 collective-permute-done.12
  38.9 0.6 %collective-permute-start.13 = (bf16[32,2048]{1,0:T(8,128)(2,1)S(1)}, bf16[32,2048]{1,0:T(8,128)(2,1)S(1)}, u32[]{:S(2)}, u32[]{:S(2)}) collective-permute-start(bf16[32,2048]{1,0:T(8,128)(2,1)S(1)} %add_convert_fusion.2), channel_id=1, source_target_pairs={{0,2},{1,3},{2,0},{3,1},{4,6},{5,7},{6,4},{7,5},{8,10},{9,11},{10,... | collective-permute-start | bytes 393224 | tf_op jit(solution)/shard_map/ppermute | solution.py:421
  39.5 0.8 %collective-permute-done.9.refs_0_ = bf16[256,1024]{1,0:T(8,128)(2,1)S(1)} collective-permute-done((bf16[256,1024]{1,0:T(8,128)(2,1)S(1)}, bf16[256,1024]{1,0:T(8,128)(2,1)S(1)}, u32[]{:S(2)}, u32[]{:S(2)}) %collective-permute-start.9) | collective-permute-done | bytes 524320 | tf_op jit(solution)/shard_map/ppermute | solution.py:541
  40.3 0.7 %collective-permute-done.10.refs_1_ = bf16[256,1024]{1,0:T(8,128)(2,1)S(1)} collective-permute-done((bf16[256,1024]{1,0:T(8,128)(2,1)S(1)}, bf16[256,1024]{1,0:T(8,128)(2,1)S(1)}, u32[]{:S(2)}, u32[]{:S(2)}) %collective-permute-start.10) | collective-permute-done | bytes 524320 | tf_op jit(solution)/shard_map/ppermute | solution.py:541
  41.1 1.9 %sum_early.1.refs_3_ = bf16[32,8,2048]{2,1,0:T(8,128)(2,1)} custom-call(s32[4,12]{1,0:T(4,128)} %bitcast.15, f32[256,2048]{1,0:T(8,128)S(1)} %get-tuple-element.48.refs_2_.keep, bf16[256,1024]{1,0:T(8,128)(2,1)S(1)} %collective-permute-done.9.refs_0_, bf16[256,1024]{1,0:T(8,128)(2,1)S(1)} %collective-permute-done.10.refs_1_, ...), custom_call_target="tpu_custom_call" | custom-call | flops 1 | bytes 1 | tf_op jit(solution)/shard_map/sum_early/pallas_call | solution.py:548
  43.0 1.9 %collective-permute-done.13.refs_2_ = bf16[32,2048]{1,0:T(8,128)(2,1)S(1)} collective-permute-done((bf16[32,2048]{1,0:T(8,128)(2,1)S(1)}, bf16[32,2048]{1,0:T(8,128)(2,1)S(1)}, u32[]{:S(2)}, u32[]{:S(2)}) %collective-permute-start.13) | collective-permute-done | bytes 131104 | tf_op jit(solution)/shard_map/ppermute | solution.py:421
  44.8 1.4 %sum_last.1 = bf16[32,8,2048]{2,1,0:T(8,128)(2,1)} custom-call(s32[4,12]{1,0:T(4,128)} %bitcast.16, f32[256,2048]{1,0:T(8,128)S(1)} %get-tuple-element.48.refs_2_.keep, bf16[256,1024]{1,0:T(8,128)(2,1)S(1)} %collective-permute-done.9.refs_0_, bf16[256,1024]{1,0:T(8,128)(2,1)S(1)} %collective-permute-done.10.refs_1_, ...), custom_call_target="tpu_custom_call", output_to_operand_aliasing={{}: (5, {})} | custom-call | flops 1 | bytes 1 | tf_op jit(solution)/shard_map/sum_last/pallas_call | solution.py:560
  (4 shorter events, 0.0 us)
Async XLA Ops:
  0.0 5.7 %copy-start = (bf16[512,8192]{1,0:T(8,128)(2,1)S(1)}, bf16[512,8192]{1,0:T(8,128)(2,1)}, u32[]{:S(2)}) copy-start(bf16[512,8192]{1,0:T(8,128)(2,1)} %weight.7) | copy-start | bytes 25165828
  0.0 16.0 %copy-start.1 = (bf16[1,128,128,256]{3,2,1,0:T(8,128)(2,1)S(1)}, bf16[1,128,128,256]{3,2,1,0:T(8,128)(2,1)}, u32[]{:S(2)}) copy-start(bf16[1,128,128,256]{3,2,1,0:T(8,128)(2,1)} %param.9) | copy-start | bytes 25165828
  6.5 2.1 %collective-permute-start = (bf16[128,2048]{1,0:T(8,128)(2,1)S(1)}, bf16[128,2048]{1,0:T(8,128)(2,1)S(1)}, u32[]{:S(2)}, u32[]{:S(2)}) collective-permute-start(bf16[128,2048]{1,0:T(8,128)(2,1)S(1)} %get-tuple-element.33), channel_id=1, source_target_pairs={{0,1},{1,0},{2,3},{3,2},{4,5},{5,4},{6,7},{7,6},{8,9},{9,8},{10,11... | collective-permute-start | bytes 1572872 | tf_op jit(solution)/shard_map/ppermute | solution.py:478
  8.7 16.0 %collective-permute-start.7 = (bf16[128,2048]{1,0:T(8,128)(2,1)S(1)}, bf16[128,2048]{1,0:T(8,128)(2,1)S(1)}, u32[]{:S(2)}, u32[]{:S(2)}) collective-permute-start(bf16[128,2048]{1,0:T(8,128)(2,1)S(1)} %add_convert_fusion.after.refs_3_), channel_id=1, source_target_pairs={{0,2},{1,3},{2,0},{3,1},{4,6},{5,7},{6,4},{7,5},{8,10},{9,11},{10,... | collective-permute-start | bytes 1572872 | tf_op jit(solution)/shard_map/ppermute | solution.py:421
  11.6 6.9 %collective-permute-start.1 = (bf16[8,768]{1,0:T(8,128)(2,1)S(1)}, bf16[8,768]{1,0:T(8,128)(2,1)S(1)}, u32[]{:S(2)}, u32[]{:S(2)}) collective-permute-start(bf16[8,768]{1,0:T(8,128)(2,1)S(1)} %get-tuple-element.39), channel_id=1, source_target_pairs={{0,4},{4,0},{8,12},{12,8},{1,5},{5,1},{9,13},{13,9},{2,6},{6,2},{1... | collective-permute-start | bytes 36872 | tf_op jit(solution)/shard_map/ppermute | solution.py:482
  13.2 5.3 %collective-permute-start.2 = (bf16[8,768]{1,0:T(8,128)(2,1)S(1)}, bf16[8,768]{1,0:T(8,128)(2,1)S(1)}, u32[]{:S(2)}, u32[]{:S(2)}) collective-permute-start(bf16[8,768]{1,0:T(8,128)(2,1)S(1)} %get-tuple-element.40), channel_id=1, source_target_pairs={{0,8},{4,12},{8,0},{12,4},{1,9},{5,13},{9,1},{13,5},{2,10},{6,14},... | collective-permute-start | bytes 36872 | tf_op jit(solution)/shard_map/ppermute | solution.py:482
  15.8 5.5 %collective-permute-start.3 = (bf16[8,768]{1,0:T(8,128)(2,1)S(1)}, bf16[8,768]{1,0:T(8,128)(2,1)S(1)}, u32[]{:S(2)}, u32[]{:S(2)}) collective-permute-start(bf16[8,768]{1,0:T(8,128)(2,1)S(1)} %get-tuple-element.41), channel_id=1, source_target_pairs={{0,12},{4,8},{8,4},{12,0},{1,13},{5,9},{9,5},{13,1},{2,14},{6,10},... | collective-permute-start | bytes 36872 | tf_op jit(solution)/shard_map/ppermute | solution.py:482
  24.6 1.8 %collective-permute-start.8 = (bf16[96,2048]{1,0:T(8,128)(2,1)S(1)}, bf16[96,2048]{1,0:T(8,128)(2,1)S(1)}, u32[]{:S(2)}, u32[]{:S(2)}) collective-permute-start(bf16[96,2048]{1,0:T(8,128)(2,1)S(1)} %get-tuple-element.47), channel_id=1, source_target_pairs={{0,1},{1,0},{2,3},{3,2},{4,5},{5,4},{6,7},{7,6},{8,9},{9,8},{10,11... | collective-permute-start | bytes 1179656 | tf_op jit(solution)/shard_map/ppermute | solution.py:507
  26.5 12.4 %collective-permute-start.11 = (bf16[96,2048]{1,0:T(8,128)(2,1)S(1)}, bf16[96,2048]{1,0:T(8,128)(2,1)S(1)}, u32[]{:S(2)}, u32[]{:S(2)}) collective-permute-start(bf16[96,2048]{1,0:T(8,128)(2,1)S(1)} %add_convert_fusion.1.after), channel_id=1, source_target_pairs={{0,2},{1,3},{2,0},{3,1},{4,6},{5,7},{6,4},{7,5},{8,10},{9,11},{10,... | collective-permute-start | bytes 1179656 | tf_op jit(solution)/shard_map/ppermute | solution.py:421
  27.0 4.4 %collective-permute-start.4 = (bf16[8,512]{1,0:T(8,128)(2,1)S(1)}, bf16[8,512]{1,0:T(8,128)(2,1)S(1)}, u32[]{:S(2)}, u32[]{:S(2)}) collective-permute-start(bf16[8,512]{1,0:T(8,128)(2,1)S(1)} %get-tuple-element.42), channel_id=1, source_target_pairs={{0,4},{4,0},{8,12},{12,8},{1,5},{5,1},{9,13},{13,9},{2,6},{6,2},{1... | collective-permute-start | bytes 24584 | tf_op jit(solution)/shard_map/ppermute | solution.py:508
  27.3 4.5 %collective-permute-start.5 = (bf16[8,512]{1,0:T(8,128)(2,1)S(1)}, bf16[8,512]{1,0:T(8,128)(2,1)S(1)}, u32[]{:S(2)}, u32[]{:S(2)}) collective-permute-start(bf16[8,512]{1,0:T(8,128)(2,1)S(1)} %get-tuple-element.43), channel_id=1, source_target_pairs={{0,8},{4,12},{8,0},{12,4},{1,9},{5,13},{9,1},{13,5},{2,10},{6,14},... | collective-permute-start | bytes 24584 | tf_op jit(solution)/shard_map/ppermute | solution.py:508
  29.9 5.4 %collective-permute-start.6 = (bf16[8,512]{1,0:T(8,128)(2,1)S(1)}, bf16[8,512]{1,0:T(8,128)(2,1)S(1)}, u32[]{:S(2)}, u32[]{:S(2)}) collective-permute-start(bf16[8,512]{1,0:T(8,128)(2,1)S(1)} %get-tuple-element.44), channel_id=1, source_target_pairs={{0,12},{4,8},{8,4},{12,0},{1,13},{5,9},{9,5},{13,1},{2,14},{6,10},... | collective-permute-start | bytes 24584 | tf_op jit(solution)/shard_map/ppermute | solution.py:508
  36.9 2.0 %collective-permute-start.12 = (bf16[32,2048]{1,0:T(8,128)(2,1)S(1)}, bf16[32,2048]{1,0:T(8,128)(2,1)S(1)}, u32[]{:S(2)}, u32[]{:S(2)}) collective-permute-start(bf16[32,2048]{1,0:T(8,128)(2,1)S(1)} %get-tuple-element.52), channel_id=1, source_target_pairs={{0,1},{1,0},{2,3},{3,2},{4,5},{5,4},{6,7},{7,6},{8,9},{9,8},{10,11... | collective-permute-start | bytes 393224 | tf_op jit(solution)/shard_map/ppermute | solution.py:526
  38.2 2.1 %collective-permute-start.9 = (bf16[256,1024]{1,0:T(8,128)(2,1)S(1)}, bf16[256,1024]{1,0:T(8,128)(2,1)S(1)}, u32[]{:S(2)}, u32[]{:S(2)}) collective-permute-start(bf16[256,1024]{1,0:T(8,128)(2,1)S(1)} %get-tuple-element.49), channel_id=1, source_target_pairs={{0,1},{1,0},{2,3},{3,2},{4,5},{5,4},{6,7},{7,6},{8,9},{9,8},{10,11... | collective-permute-start | bytes 1572872 | tf_op jit(solution)/shard_map/ppermute | solution.py:541
  38.8 2.3 %collective-permute-start.10 = (bf16[256,1024]{1,0:T(8,128)(2,1)S(1)}, bf16[256,1024]{1,0:T(8,128)(2,1)S(1)}, u32[]{:S(2)}, u32[]{:S(2)}) collective-permute-start(bf16[256,1024]{1,0:T(8,128)(2,1)S(1)} %get-tuple-element.50), channel_id=1, source_target_pairs={{0,1},{1,0},{2,3},{3,2},{4,5},{5,4},{6,7},{7,6},{8,9},{9,8},{10,11... | collective-permute-start | bytes 1572872 | tf_op jit(solution)/shard_map/ppermute | solution.py:541
  38.9 5.9 %collective-permute-start.13 = (bf16[32,2048]{1,0:T(8,128)(2,1)S(1)}, bf16[32,2048]{1,0:T(8,128)(2,1)S(1)}, u32[]{:S(2)}, u32[]{:S(2)}) collective-permute-start(bf16[32,2048]{1,0:T(8,128)(2,1)S(1)} %add_convert_fusion.2), channel_id=1, source_target_pairs={{0,2},{1,3},{2,0},{3,1},{4,6},{5,7},{6,4},{7,5},{8,10},{9,11},{10,... | collective-permute-start | bytes 393224 | tf_op jit(solution)/shard_map/ppermute | solution.py:421

commit v2 on v1

--- a/solution.py
+++ b/solution.py
@@ -11,7 +11,7 @@
 MASKED = -1e30
 GROUP = 8
 NEVER = 2**30
-PIECES = 2
+PIECES = 4
 
 VMEM = pl.BlockSpec(memory_space=pltpu.VMEM)
 SMEM = pl.BlockSpec(memory_space=pltpu.SMEM)
@@ -158,43 +158,33 @@
     return route_of(migration, me, peer_of(me, k, inst_count), False)
 
 
-def away_kernel(
-    inst_count, rounds, lengths, page_table, migration, pool, second, weight, *refs
-):
-    count = len(rounds)
-    received, answers = refs[:count], refs[count : 2 * count]
-    keep, send, buffer, sems = refs[2 * count :]
-    page_count, slot_count = page_table.shape
+def away_kernel(inst_count, rounds, lengths, migration, pages, *refs):
+    received, answers = refs[: len(rounds)], refs[len(rounds) :]
+    _, page_count, page_len, _ = pages.shape
     step_count, width = answers[0].shape
-    first = lax.axis_index("inst") * slot_count
-    slots = [away_slot(migration, inst_count, k) for k in rounds]
-    for i, slot in enumerate(slots):
-        page_copies(pool, buffer, sems, page_table, i, slot)
-    project_far(second, weight, keep, send)
-    for i in range(count):
-        wait_copies(pool, buffer, sems, i)
+    first = lax.axis_index("inst") * (lengths.shape[0] // inst_count)
     result = attend_group(
         [ref[:, :width].astype(jnp.float32) for ref in received],
         [ref[:, width:].astype(jnp.float32) for ref in received],
-        [[buffer.at[i, j] for j in range(page_count)] for i in range(count)],
-        [lengths[first + slot] * pool.shape[1] for slot in slots],
+        [[pages.at[i, j] for j in range(page_count)] for i in range(len(rounds))],
+        [lengths[first + away_slot(migration, inst_count, k)] * page_len for k in rounds],
         step_count,
     )
     for answer, rows in zip(answers, result):
         answer[...] = rows.astype(answer.dtype)
 
 
-def project(rows, weight, first, columns, target, row_offset=0, offset=0):
+def project(rows, weight, first, columns, target, offset=0):
     tile = min(512, columns)
     rows = rows[...]
     for j in range(0, columns, tile):
         start = pl.multiple_of(first + j, tile)
-        target[row_offset : row_offset + rows.shape[0], offset + j : offset + j + tile] = jnp.dot(
+        target[:, offset + j : offset + j + tile] = jnp.dot(
             rows, weight[:, pl.ds(start, tile)], preferred_element_type=jnp.float32
         ).astype(target.dtype)
 
 
-def project_far(attended, weight, keep, send, stacked=False):
+def project_far(attended, weight, keep, send):
     core = lax.rem(lax.axis_index("tp"), 2)
     chip = lax.axis_index("tp") // 2
     chips = lax.axis_size("tp") // 2
@@ -202,8 +192,7 @@
     for target, side in ((send, 1 - core), (keep, core)):
         for d in range(1, chips):
             first = (2 * lax.rem(chip + d, chips) + side) * columns
-            row, column = ((d - 1) * attended.shape[0], 0) if stacked else (0, (d - 1) * columns)
-            project(attended, weight, first, columns, target, row, column)
+            project(attended, weight, first, columns, target, (d - 1) * columns)
 
 
 def attend_slots(slots, lengths, queries, new_tokens, pages_of, page_len, wait=lambda i: None):
@@ -269,49 +258,48 @@
 
 
 def second_kernel(
-    inst_count, first, migration, lengths, page_table, queries, new_tokens, pool, after,
-    attended, extra,
+    inst_count, rounds, first, migration, lengths, page_table, queries, new_tokens, pool, after,
+    attended, away_pages, sems,
 ):
     slot_count, step_count, _ = queries.shape
-    count = attended.shape[0] // step_count
+    for i, k in enumerate(rounds):
+        slot = away_slot(migration, inst_count, k)
+        page_copies(pool, away_pages, sems, page_table, i, slot)
     arrivals, _ = arrivals_of(migration, inst_count)
-    slots = [
-        slot_at(first + i, arrivals, slot_count) for i in range(count + extra.shape[0])
-    ]
+    slots = [slot_at(first + i, arrivals, slot_count) for i in range(attended.shape[0])]
     rows = attend_slots(
         slots, lengths, queries, new_tokens,
         lambda i: [pool.at[page_table[j, slots[i]]] for j in range(page_table.shape[0])],
         pool.shape[1],
     )
-    store_rows(rows[:count], attended)
-    for i, row in enumerate(rows[count:]):
-        extra[i] = row.astype(extra.dtype)
-
-
-def last_rows_kernel(inst_count, rounds, migration, weight, extra, *refs):
+    for i, row in enumerate(rows):
+        attended[i] = row.astype(attended.dtype)
+    for i in range(len(rounds)):
+        wait_copies(pool, away_pages, sems, i)
+
+
+def far_second_kernel(inst_count, rounds, migration, weight, attended, *refs):
     answers, (rows, keep, send) = refs[:-3], refs[-3:]
     me = lax.axis_index("inst")
     _, sources = arrivals_of(migration, inst_count)
-    last = [extra[i].astype(jnp.float32) for i in range(extra.shape[0])]
+    parts = [attended[i].astype(jnp.float32) for i in range(attended.shape[0])]
     given = [answer[...].astype(jnp.float32) for answer in answers]
     for source in sources:
-        row = given[0]
+        part = given[0]
         for k, answer in zip(rounds[1:], given[1:]):
-            row = jnp.where(source == peer_of(me, k, inst_count), answer, row)
-        last.append(row)
-    store_rows(last, rows)
-    project_far(rows, weight, keep, send, stacked=True)
-
-
-def own_kernel(weight, first, second, last, after, keep, *refs):
+            part = jnp.where(source == peer_of(me, k, inst_count), answer, part)
+        parts.append(part)
+    store_rows(parts, rows)
+    project_far(rows, weight, keep, send)
+
+
+def own_kernel(weight, first, second, after, keep, *refs):
     sends, rows = refs[:-1], refs[-1]
     core = lax.rem(lax.axis_index("tp"), 2)
     pair = lax.axis_index("tp") // 2 * 2
     columns = keep.shape[1]
-    at = 0
-    for part in (first, second, last):
-        rows[at : at + part.shape[0], :] = part[...]
-        at += part.shape[0]
+    rows[: first.shape[0], :] = first[...]
+    rows[first.shape[0] :, :] = second[...]
     at = 0
     for send in sends:
         project(rows, weight, (pair + 1 - core) * columns + at, send.shape[1], send)
@@ -319,47 +307,16 @@
     project(rows, weight, (pair + core) * columns, columns, keep)
 
 
-def sum_kernel(inst_count, chunks, piece_count, migration, keep, *refs):
-    mates, parts, (out, staged, sem) = refs[:piece_count], refs[piece_count:-3], refs[-3:]
+def sum_kernel(inst_count, first, piece_count, migration, keep, *refs):
+    mates, parts = refs[:piece_count], refs[piece_count:-3]
+    out, staged, sem = refs[-3:]
+    parts = parts[: lax.axis_size("tp") // 2 - 1]
     slot_count, step_count, _ = out.shape
     pair = 2 * step_count
     width = mates[0].shape[1]
     arrivals, _ = arrivals_of(migration, inst_count)
-    share = len(parts) // len(chunks)
-    at = 0
-    for n, chunk in enumerate(chunks):
-        for base in range(0, chunk, pair):
-            for m, mate in enumerate(mates):
-                columns = slice(m * width, (m + 1) * width)
-                total = keep[at : at + pair, columns] + mate[at : at + pair, :].astype(jnp.float32)
-                for part in parts[n * share : (n + 1) * share]:
-                    total = total + part[base : base + pair, columns].astype(jnp.float32)
-                total = total.astype(jnp.bfloat16)
-                for half in range(2):
-                    staged[at // step_count + half, :, columns] = total[
-                        half * step_count : (half + 1) * step_count
-                    ]
-            at += pair
-    scatter_rows(staged, out, arrivals, 0, sem)
-
-
-def scatter_rows(staged, out, arrivals, first, sem):
-    slot_count = out.shape[0]
-    for i in range(staged.shape[0]):
-        slot = slot_at(first + i, arrivals, slot_count)
-        pltpu.make_async_copy(staged.at[i], out.at[slot], sem.at[0]).start()
-    pltpu.make_async_copy(staged, out.at[pl.ds(0, staged.shape[0])], sem.at[0]).wait()
-
-
-def last_kernel(inst_count, first, piece_count, migration, keep, *refs):
-    mates, parts, (out, staged, sem) = refs[:piece_count], refs[piece_count:-4], refs[-3:]
-    step_count = out.shape[1]
-    pair = 2 * step_count
-    width = mates[0].shape[1]
-    size = parts[0].shape[0]
-    arrivals, _ = arrivals_of(migration, inst_count)
-    for at in range(0, size, pair):
-        own = keep.shape[0] - size + at
+    for at in range(0, staged.shape[0] * step_count, pair):
+        own = first * step_count + at
         for m, mate in enumerate(mates):
             columns = slice(m * width, (m + 1) * width)
             total = keep[own : own + pair, columns] + mate[own : own + pair, :].astype(jnp.float32)
@@ -370,7 +327,10 @@
                 staged[at // step_count + half, :, columns] = total[
                     half * step_count : (half + 1) * step_count
                 ]
-    scatter_rows(staged, out, arrivals, first, sem)
+    for i in range(staged.shape[0]):
+        slot = slot_at(first + i, arrivals, slot_count)
+        pltpu.make_async_copy(staged.at[i], out.at[slot], sem.at[0]).start()
+    pltpu.make_async_copy(staged, out.at[pl.ds(0, staged.shape[0])], sem.at[0]).wait()
 
 
 def in_hbm(value):
@@ -434,11 +394,8 @@
     def rows_shape(count):
         return pltpu.VMEM((count * step_count, width), bf16)
 
-    last_count = incoming + incoming % 2
-    extra_count = last_count - incoming
-    first_count = slot_count // 4 * 2
-    second_count = slot_count - first_count - last_count
-    last_rows = last_count * step_count
+    first_count = slot_count // 16 * 10
+    second_count = slot_count - first_count
 
     def page_shape(count):
         return pltpu.VMEM((count, page_count, *pool.shape[1:]), bf16)
@@ -481,93 +438,81 @@
     packs = hold(packs, [summed])
     received = [lax.ppermute(pack, "inst", pairs[k]) for k, pack in zip(rounds, packs)]
 
-    second, extra = pl.pallas_call(
-        functools.partial(second_kernel, inst_count, first_count),
+    attended, away_pages = pl.pallas_call(
+        functools.partial(second_kernel, inst_count, rounds, first_count),
         out_shape=[
-            rows_shape(second_count),
-            pltpu.VMEM((extra_count, step_count, width), bf16),
+            pltpu.VMEM((second_count - incoming, step_count, width), bf16),
+            page_shape(len(rounds)),
         ],
         in_specs=[SMEM, SMEM, SMEM, VMEM, VMEM, VMEM, ANY],
         out_specs=[VMEM] * 2,
+        scratch_shapes=[dma((len(rounds),))],
         compiler_params=limit,
         cost_estimate=light,
         name="attend_second",
-    )(migration, lengths, page_table, queries, new_tokens, in_vmem(pool), summed)
-    second = in_vmem(second)
-    *answers, keep, send = pl.pallas_call(
+    )(
+        migration, lengths, page_table, queries, new_tokens, in_vmem(pool), summed,
+    )
+    attended = in_vmem(attended)
+    answers = pl.pallas_call(
         functools.partial(away_kernel, inst_count, rounds),
-        out_shape=[shape((step_count, width), bf16)] * len(rounds) + chunk_shapes(second_count),
-        in_specs=[SMEM, SMEM, SMEM, ANY] + [VMEM] * (2 + len(rounds)),
-        out_specs=[VMEM] * (2 + len(rounds)),
-        scratch_shapes=[page_shape(len(rounds)), dma((len(rounds),))],
+        out_shape=[shape((step_count, width), bf16)] * len(rounds),
+        in_specs=[SMEM, SMEM] + [VMEM] * (1 + len(rounds)),
+        out_specs=[VMEM] * len(rounds),
         compiler_params=limit,
         cost_estimate=light,
         name="attend_away",
-    )(lengths, page_table, migration, in_hbm(pool), second, weight, *received)
-    mate = lax.ppermute(send, "tp", swap)
+    )(lengths, migration, in_vmem(away_pages), *received)
     answers = [lax.ppermute(answer, "inst", pairs[k]) for k, answer in zip(rounds, answers)]
-    (keep,) = hold([keep], arrived_first)
-    summed = (keep + mate.astype(f32)).astype(bf16)
-    arrived_second = send_far(split_far(summed))
-
-    last, keep, send = pl.pallas_call(
-        functools.partial(last_rows_kernel, inst_count, rounds),
-        out_shape=[
-            rows_shape(last_count),
-            pltpu.VMEM((last_rows * (chips - 1), columns), f32),
-            pltpu.VMEM((last_rows * (chips - 1), columns), bf16),
-        ],
+    second, keep, send = pl.pallas_call(
+        functools.partial(far_second_kernel, inst_count, rounds),
+        out_shape=[rows_shape(second_count), *chunk_shapes(second_count)],
         in_specs=[SMEM] + [VMEM] * (2 + len(rounds)),
         out_specs=[VMEM] * 3,
         compiler_params=limit,
         cost_estimate=light,
-        name="last_rows",
-    )(migration, weight, in_vmem(extra), *answers)
+        name="far_second",
+    )(migration, weight, attended, *answers)
     mate = lax.ppermute(send, "tp", swap)
+    (keep,) = hold([keep], arrived_first)
+    summed = (keep + mate.astype(f32)).astype(bf16)
+    arrived_second = send_far(split_far(summed))
     own_keep, *own_sends = pl.pallas_call(
         own_kernel,
         out_shape=[
             pltpu.VMEM((row_count, columns), f32),
             *[pltpu.VMEM((row_count, columns // PIECES), bf16)] * PIECES,
         ],
-        in_specs=[VMEM] * 4 + [ANY],
+        in_specs=[VMEM] * 3 + [ANY],
         out_specs=[VMEM] * (1 + PIECES),
         scratch_shapes=[pltpu.VMEM((row_count, width), bf16)],
         compiler_params=limit,
         cost_estimate=light,
         name="own_columns",
-    )(weight, first, second, in_vmem(last), summed)
+    )(weight, first, in_vmem(second), summed)
     own_keep = in_vmem(own_keep)
     own_mates = [lax.ppermute(own_send, "tp", swap) for own_send in own_sends]
-    (keep,) = hold([keep], [*arrived_second, own_keep])
-    summed = (keep + mate.astype(f32)).astype(bf16)
-    arrived_last = send_far([summed[d * last_rows : (d + 1) * last_rows] for d in range(chips - 1)])
-
-    early = slot_count - last_count
-    out_shape = (slot_count, step_count, columns)
-    out = pl.pallas_call(
-        functools.partial(
-            sum_kernel, inst_count, [first_count * step_count, second_count * step_count], PIECES
-        ),
-        out_shape=pltpu.HBM(out_shape, bf16),
-        in_specs=[SMEM] + [VMEM] * (1 + PIECES + 2 * (chips - 1)),
-        out_specs=ANY,
-        scratch_shapes=[pltpu.VMEM((early, step_count, columns), bf16), dma((1,))],
-        compiler_params=limit,
-        cost_estimate=light,
-        name="sum_early",
-    )(migration, own_keep, *own_mates, *arrived_first, *arrived_second)
-    out = pl.pallas_call(
-        functools.partial(last_kernel, inst_count, early, PIECES),
-        out_shape=pltpu.HBM(out_shape, bf16),
-        in_specs=[SMEM] + [VMEM] * (PIECES + chips) + [ANY],
-        out_specs=ANY,
-        scratch_shapes=[pltpu.VMEM((last_count, step_count, columns), bf16), dma((1,))],
-        input_output_aliases={PIECES + chips + 1: 0},
-        compiler_params=limit,
-        cost_estimate=light,
-        name="sum_last",
-    )(migration, own_keep, *own_mates, *arrived_last, out)
+
+    out = []
+    for start, count, arrived in (
+        (0, first_count, arrived_first),
+        (first_count, second_count, arrived_second),
+    ):
+        operands = [migration, own_keep, *own_mates, *arrived]
+        out = [
+            pl.pallas_call(
+                functools.partial(sum_kernel, inst_count, start, PIECES),
+                out_shape=pltpu.HBM((slot_count, step_count, columns), bf16),
+                in_specs=[SMEM] + [VMEM] * (len(operands) - 1) + [ANY] * len(out),
+                out_specs=ANY,
+                scratch_shapes=[pltpu.VMEM((count, step_count, columns), bf16), dma((1,))],
+                input_output_aliases={len(operands): 0} if out else {},
+                compiler_params=limit,
+                cost_estimate=light,
+                name="sum_chunk",
+            )(*operands, *out)
+        ]
+    (out,) = out
     return out.reshape(row_count, columns)
 
 

time: 46.5 us -> 48.4 us (1.041)
  waiting for transfers between devices: 13.4 us -> 15.2 us
    ppermute x3 -> x2, waiting for transfers between devices: 1.88 us -> 4.88 us  [send_far(): lax.ppermute(part, 'tp', [(t, (t + 2 * d) % tp_count) for t in range(tp_c...]
    pallas_call x1, Pallas kernels: 3.32 us -> 1.36 us  [on_device(): pl.pallas_call(functools.partial(away_kernel, inst_count, rounds), out_sh...]
    pallas_call x1, Pallas kernels: 5.65 us -> 6.78 us  [on_device(): pl.pallas_call(functools.partial(first_kernel, inst_count, rounds), out_s...]
    pallas_call x4, Pallas kernels: 7.28 us -> 8.15 us  [the longest x1 3.33 us: on_device(): pl.pallas_call(functools.partial(second_kernel, inst_count, rounds, first...]
    ppermute x3, waiting for transfers between devices: 2.76 us -> 1.91 us  [on_device(): lax.ppermute(pack, 'inst', pairs[k])]
    ppermute x3 -> x2, starting transfers between devices: 4.13 us -> 3.52 us  [send_far(): lax.ppermute(part, 'tp', [(t, (t + 2 * d) % tp_count) for t in range(tp_c...]
    ppermute x3, waiting for transfers between devices: 3.9 us -> 3.33 us  [on_device(): lax.ppermute(answer, 'inst', pairs[k])]
    ppermute x2 -> x4, starting transfers between devices: 0.64 us -> 1.08 us  [on_device(): own_mates = [lax.ppermute(own_send, 'tp', swap) for own_send in own_sends]]
  transfers between devices with their start and end apart: 14 -> 14, of which waited for: 8 -> 10; matrix products, arithmetic and copies ran while one was open for 0% -> 0% of each run, Pallas kernels for 23% -> 19%
where the time goes in v2:
time: 48.4 us; the launch traced here: 48.1 us
  Pallas kernels  18.5 us (38%)
  waiting for transfers between devices  15.2 us (31%)
  starting transfers between devices  14 us (29%)
    pallas_call x1, Pallas kernels, on_device(): pl.pallas_call(functools.partial(first_kernel, inst_count, rounds), out_s...  6.78 us
    ppermute x2, waiting for transfers between devices, send_far(): lax.ppermute(part, 'tp', [(t, (t + 2 * d) % tp_count) for t in range(tp_c...  4.88 us
    ppermute x3, starting transfers between devices, on_device(): lax.ppermute(answer, 'inst', pairs[k])  4.43 us
    ppermute x3, starting transfers between devices, on_device(): lax.ppermute(pack, 'inst', pairs[k])  4.39 us
    ppermute x2, starting transfers between devices, send_far(): lax.ppermute(part, 'tp', [(t, (t + 2 * d) % tp_count) for t in range(tp_c...  3.52 us
    ppermute x2, waiting for transfers between devices, on_device(): mate = lax.ppermute(send, 'tp', swap)  3.41 us
    ppermute x3, waiting for transfers between devices, on_device(): lax.ppermute(answer, 'inst', pairs[k])  3.33 us
    pallas_call x1, Pallas kernels, on_device(): pl.pallas_call(functools.partial(second_kernel, inst_count, rounds, first...  3.33 us
  transfers between devices with their start and end apart: 14, of which 10 were waited for; matrix products, arithmetic and copies ran while one was open for 0% of the time, Pallas kernels for 19%

profile of v2, /device:TPU:0, one launch (start us, length us, event | category | flops | bytes accessed | tf_op | source)
XLA Modules:
  0.0 48.1 jit_solution(8367721435859417195)
XLA Ops:
  0.0 0.0 copy-start
  0.0 6.8 %attend_first.1 = (bf16[160,512]{1,0:T(8,128)(2,1)S(1)}, bf16[32,8,512]{2,1,0:T(8,128)(2,1)S(1)}, bf16[32,8,256]{2,1,0:T(8,128)(2,1)S(1)}, bf16[8,768]{1,0:T(8,1...) custom-call(s32[4,12]{1,0:T(4,128)} %bitcast.10, s32[128]{0:T(128)} %lengths.5, s32[4,32]{1,0:T(4,128)} %bitcast.16, ...), custom_call_target="tpu_custom_call" | custom-call | flops 1 | bytes 1 | tf_op jit(solution)/shard_map/attend_first/pallas_call | solution.py:410
  6.8 0.0 copy-done
  6.8 0.0 copy-start.1
  6.8 0.9 %far_first.1 = (f32[160,2048]{1,0:T(8,128)S(1)}, bf16[160,2048]{1,0:T(8,128)(2,1)S(1)}) custom-call(bf16[160,512]{1,0:T(8,128)(2,1)S(1)} %get-tuple-element.29.attended.first, bf16[512,8192]{1,0:T(8,128)(2,1)S(1)} %copy-done), custom_call_target="tpu_custom_call" | custom-call | flops 1 | bytes 1 | tf_op jit(solution)/shard_map/far_first/pallas_call | solution.py:426
  7.7 0.5 %collective-permute-start = (bf16[160,2048]{1,0:T(8,128)(2,1)S(1)}, bf16[160,2048]{1,0:T(8,128)(2,1)S(1)}, u32[]{:S(2)}, u32[]{:S(2)}) collective-permute-start(bf16[160,2048]{1,0:T(8,128)(2,1)S(1)} %get-tuple-element.33), channel_id=1, source_target_pairs={{0,1},{1,0},{2,3},{3,2},{4,5},{5,4},{6,7},{7,6},{8,9},{9,8},{10,11... | collective-permute-start | bytes 1966088 | tf_op jit(solution)/shard_map/ppermute | solution.py:435
  8.3 1.7 %collective-permute-done = bf16[160,2048]{1,0:T(8,128)(2,1)S(1)} collective-permute-done((bf16[160,2048]{1,0:T(8,128)(2,1)S(1)}, bf16[160,2048]{1,0:T(8,128)(2,1)S(1)}, u32[]{:S(2)}, u32[]{:S(2)}) %collective-permute-start) | collective-permute-done | bytes 655392 | tf_op jit(solution)/shard_map/ppermute | solution.py:435
  10.0 0.2 add_convert_fusion.after.refs_3_
  10.2 2.9 %collective-permute-start.7 = (bf16[160,2048]{1,0:T(8,128)(2,1)S(1)}, bf16[160,2048]{1,0:T(8,128)(2,1)S(1)}, u32[]{:S(2)}, u32[]{:S(2)}) collective-permute-start(bf16[160,2048]{1,0:T(8,128)(2,1)S(1)} %add_convert_fusion.after.refs_3_), channel_id=1, source_target_pairs={{0,2},{1,3},{2,0},{3,1},{4,6},{5,7},{6,4},{7,5},{8,10},{9,11},{10,... | collective-permute-start | bytes 1966088 | tf_op jit(solution)/shard_map/ppermute | solution.py:381
  13.1 1.6 %collective-permute-start.1 = (bf16[8,768]{1,0:T(8,128)(2,1)S(1)}, bf16[8,768]{1,0:T(8,128)(2,1)S(1)}, u32[]{:S(2)}, u32[]{:S(2)}) collective-permute-start(bf16[8,768]{1,0:T(8,128)(2,1)S(1)} %get-tuple-element.39), channel_id=1, source_target_pairs={{0,4},{4,0},{8,12},{12,8},{1,5},{5,1},{9,13},{13,9},{2,6},{6,2},{1... | collective-permute-start | bytes 36872 | tf_op jit(solution)/shard_map/ppermute | solution.py:439
  14.7 2.6 %collective-permute-start.2 = (bf16[8,768]{1,0:T(8,128)(2,1)S(1)}, bf16[8,768]{1,0:T(8,128)(2,1)S(1)}, u32[]{:S(2)}, u32[]{:S(2)}) collective-permute-start(bf16[8,768]{1,0:T(8,128)(2,1)S(1)} %get-tuple-element.40), channel_id=1, source_target_pairs={{0,8},{4,12},{8,0},{12,4},{1,9},{5,13},{9,1},{13,5},{2,10},{6,14},... | collective-permute-start | bytes 36872 | tf_op jit(solution)/shard_map/ppermute | solution.py:439
  17.3 0.2 collective-permute-start.3
  17.5 0.0 copy-done.1
  17.5 3.3 %attend_second.1 = (bf16[9,8,512]{2,1,0:T(8,128)(2,1)S(1)}, bf16[3,4,128,256]{3,2,1,0:T(8,128)(2,1)S(1)}) custom-call(s32[4,12]{1,0:T(4,128)} %bitcast.11, s32[128]{0:T(128)} %lengths.5, s32[4,32]{1,0:T(4,128)} %bitcast.17, bf16[32,8,512]{2,1,0:T(8,128)(2,1)S(1)} %get-tuple-element.30.queries, bf16[32,8,256]{2,1,0:T(8,128)(2,1)S(1)} %get-tuple-element.31.new_tokens, ...), custom_call_target="tpu_custom_call" | custom-call | flops 1 | bytes 1 | tf_op jit(solution)/shard_map/attend_second/pallas_call | solution.py:441
  20.8 0.0 collective-permute-done.1.refs_0_
  20.9 0.0 collective-permute-done.2.refs_1_
  20.9 1.9 %collective-permute-done.3.refs_2_ = bf16[8,768]{1,0:T(8,128)(2,1)S(1)} collective-permute-done((bf16[8,768]{1,0:T(8,128)(2,1)S(1)}, bf16[8,768]{1,0:T(8,128)(2,1)S(1)}, u32[]{:S(2)}, u32[]{:S(2)}) %collective-permute-start.3) | collective-permute-done | bytes 12320 | tf_op jit(solution)/shard_map/ppermute | solution.py:439
  22.8 1.4 %attend_away.1 = (bf16[8,512]{1,0:T(8,128)(2,1)S(1)}, bf16[8,512]{1,0:T(8,128)(2,1)S(1)}, bf16[8,512]{1,0:T(8,128)(2,1)S(1)}) custom-call(s32[128]{0:T(128)} %lengths.5, s32[4,12]{1,0:T(4,128)} %bitcast.12, bf16[3,4,128,256]{3,2,1,0:T(8,128)(2,1)S(1)} %get-tuple-element.35.pages, bf16[8,768]{1,0:T(8,128)(2,1)S(1)} %collective-permute-done.1.refs_0_, ...), custom_call_target="tpu_custom_call" | custom-call | flops 1 | bytes 1 | tf_op jit(solution)/shard_map/attend_away/pallas_call | solution.py:457
  24.1 0.1 collective-permute-start.4
  24.2 2.3 %collective-permute-start.5 = (bf16[8,512]{1,0:T(8,128)(2,1)S(1)}, bf16[8,512]{1,0:T(8,128)(2,1)S(1)}, u32[]{:S(2)}, u32[]{:S(2)}) collective-permute-start(bf16[8,512]{1,0:T(8,128)(2,1)S(1)} %get-tuple-element.43), channel_id=1, source_target_pairs={{0,8},{4,12},{8,0},{12,4},{1,9},{5,13},{9,1},{13,5},{2,10},{6,14},... | collective-permute-start | bytes 24584 | tf_op jit(solution)/shard_map/ppermute | solution.py:466
  26.5 2.1 %collective-permute-start.6 = (bf16[8,512]{1,0:T(8,128)(2,1)S(1)}, bf16[8,512]{1,0:T(8,128)(2,1)S(1)}, u32[]{:S(2)}, u32[]{:S(2)}) collective-permute-start(bf16[8,512]{1,0:T(8,128)(2,1)S(1)} %get-tuple-element.44), channel_id=1, source_target_pairs={{0,12},{4,8},{8,4},{12,0},{1,13},{5,9},{9,5},{13,1},{2,14},{6,10},... | collective-permute-start | bytes 24584 | tf_op jit(solution)/shard_map/ppermute | solution.py:466
  28.6 0.0 collective-permute-done.4.refs_0_
  28.6 0.2 collective-permute-done.5.refs_1_
  28.8 3.1 %collective-permute-done.6.refs_2_ = bf16[8,512]{1,0:T(8,128)(2,1)S(1)} collective-permute-done((bf16[8,512]{1,0:T(8,128)(2,1)S(1)}, bf16[8,512]{1,0:T(8,128)(2,1)S(1)}, u32[]{:S(2)}, u32[]{:S(2)}) %collective-permute-start.6) | collective-permute-done | bytes 8224 | tf_op jit(solution)/shard_map/ppermute | solution.py:466
  31.9 1.5 %far_second.1 = (bf16[96,512]{1,0:T(8,128)(2,1)S(1)}, f32[96,2048]{1,0:T(8,128)S(1)}, bf16[96,2048]{1,0:T(8,128)(2,1)S(1)}) custom-call(s32[4,12]{1,0:T(4,128)} %bitcast.13, bf16[512,8192]{1,0:T(8,128)(2,1)S(1)} %copy-done, bf16[9,8,512]{2,1,0:T(8,128)(2,1)S(1)} %get-tuple-element.34.attended, bf16[8,512]{1,0:T(8,128)(2,1)S(1)} %collective-permute-done.4.refs_0_, ...), custom_call_target="tpu_custom_call" | custom-call | flops 1 | bytes 1 | tf_op jit(solution)/shard_map/far_second/pallas_call | solution.py:467
  33.4 0.1 collective-permute-start.8
  33.5 0.0 collective-permute-done.7.refs_1_.refs_4_
  33.5 1.7 %collective-permute-done.8 = bf16[96,2048]{1,0:T(8,128)(2,1)S(1)} collective-permute-done((bf16[96,2048]{1,0:T(8,128)(2,1)S(1)}, bf16[96,2048]{1,0:T(8,128)(2,1)S(1)}, u32[]{:S(2)}, u32[]{:S(2)}) %collective-permute-start.8) | collective-permute-done | bytes 393248 | tf_op jit(solution)/shard_map/ppermute | solution.py:476
  35.2 0.1 add_convert_fusion.1.after
  35.3 0.6 %collective-permute-start.13 = (bf16[96,2048]{1,0:T(8,128)(2,1)S(1)}, bf16[96,2048]{1,0:T(8,128)(2,1)S(1)}, u32[]{:S(2)}, u32[]{:S(2)}) collective-permute-start(bf16[96,2048]{1,0:T(8,128)(2,1)S(1)} %add_convert_fusion.1.after), channel_id=1, source_target_pairs={{0,2},{1,3},{2,0},{3,1},{4,6},{5,7},{6,4},{7,5},{8,10},{9,11},{10,... | collective-permute-start | bytes 1179656 | tf_op jit(solution)/shard_map/ppermute | solution.py:381
  35.9 1.3 %own_columns.1 = (f32[256,2048]{1,0:T(8,128)S(1)}, bf16[256,512]{1,0:T(8,128)(2,1)S(1)}, bf16[256,512]{1,0:T(8,128)(2,1)S(1)}, bf16[256,512]{1,0:T(8,128)(2,1)S(1)}, bf16[256,512]{1,0:T(8,128)(2,1)S(1)}) custom-call(bf16[512,8192]{1,0:T(8,128)(2,1)S(1)} %copy-done, bf16[160,512]{1,0:T(8,128)(2,1)S(1)} %get-tuple-element.29.attended.first, ...), custom_call_target="tpu_custom_call" | custom-call | flops 1 | bytes 1 | tf_op jit(solution)/shard_map/own_columns/pallas_call | solution.py:480
  37.2 0.1 collective-permute-start.9
  37.3 0.5 %collective-permute-start.10 = (bf16[256,512]{1,0:T(8,128)(2,1)S(1)}, bf16[256,512]{1,0:T(8,128)(2,1)S(1)}, u32[]{:S(2)}, u32[]{:S(2)}) collective-permute-start(bf16[256,512]{1,0:T(8,128)(2,1)S(1)} %get-tuple-element.50), channel_id=1, source_target_pairs={{0,1},{1,0},{2,3},{3,2},{4,5},{5,4},{6,7},{7,6},{8,9},{9,8},{10,11... | collective-permute-start | bytes 786440 | tf_op jit(solution)/shard_map/ppermute | solution.py:494
  37.8 0.1 collective-permute-start.11
  37.9 0.4 collective-permute-start.12
  38.3 0.5 %collective-permute-done.9.refs_0_ = bf16[256,512]{1,0:T(8,128)(2,1)S(1)} collective-permute-done((bf16[256,512]{1,0:T(8,128)(2,1)S(1)}, bf16[256,512]{1,0:T(8,128)(2,1)S(1)}, u32[]{:S(2)}, u32[]{:S(2)}) %collective-permute-start.9) | collective-permute-done | bytes 262176 | tf_op jit(solution)/shard_map/ppermute | solution.py:494
  38.8 0.4 collective-permute-done.10.refs_1_
  39.2 0.4 collective-permute-done.11.refs_2_
  39.6 0.4 collective-permute-done.12.refs_3_
  39.9 1.7 %sum_chunk.2.refs_5_ = bf16[32,8,2048]{2,1,0:T(8,128)(2,1)} custom-call(s32[4,12]{1,0:T(4,128)} %bitcast.14, f32[256,2048]{1,0:T(8,128)S(1)} %get-tuple-element.48.keep, bf16[256,512]{1,0:T(8,128)(2,1)S(1)} %collective-permute-done.9.refs_0_, bf16[256,512]{1,0:T(8,128)(2,1)S(1)} %collective-permute-done.10.refs_1_, ...), custom_call_target="tpu_custom_call" | custom-call | flops 1 | bytes 1 | tf_op jit(solution)/shard_map/sum_chunk/pallas_call | solution.py:503
  41.7 4.9 %collective-permute-done.13.refs_4_ = bf16[96,2048]{1,0:T(8,128)(2,1)S(1)} collective-permute-done((bf16[96,2048]{1,0:T(8,128)(2,1)S(1)}, bf16[96,2048]{1,0:T(8,128)(2,1)S(1)}, u32[]{:S(2)}, u32[]{:S(2)}) %collective-permute-start.13) | collective-permute-done | bytes 393248 | tf_op jit(solution)/shard_map/ppermute | solution.py:381
  46.5 1.6 %sum_chunk.3 = bf16[32,8,2048]{2,1,0:T(8,128)(2,1)} custom-call(s32[4,12]{1,0:T(4,128)} %bitcast.15, f32[256,2048]{1,0:T(8,128)S(1)} %get-tuple-element.48.keep, bf16[256,512]{1,0:T(8,128)(2,1)S(1)} %collective-permute-done.9.refs_0_, bf16[256,512]{1,0:T(8,128)(2,1)S(1)} %collective-permute-done.10.refs_1_, ...), custom_call_target="tpu_custom_call", output_to_operand_aliasing={{}: (7, {})} | custom-call | flops 1 | bytes 1 | tf_op jit(solution)/shard_map/sum_chunk/pallas_call | solution.py:503
  (2 shorter events, 0.0 us)
Async XLA Ops:
  0.0 6.8 %copy-start = (bf16[512,8192]{1,0:T(8,128)(2,1)S(1)}, bf16[512,8192]{1,0:T(8,128)(2,1)}, u32[]{:S(2)}) copy-start(bf16[512,8192]{1,0:T(8,128)(2,1)} %weight.5) | copy-start | bytes 25165828
  6.8 10.7 %copy-start.1 = (bf16[1,128,128,256]{3,2,1,0:T(8,128)(2,1)S(1)}, bf16[1,128,128,256]{3,2,1,0:T(8,128)(2,1)}, u32[]{:S(2)}) copy-start(bf16[1,128,128,256]{3,2,1,0:T(8,128)(2,1)} %param.9) | copy-start | bytes 25165828
  7.7 2.2 %collective-permute-start = (bf16[160,2048]{1,0:T(8,128)(2,1)S(1)}, bf16[160,2048]{1,0:T(8,128)(2,1)S(1)}, u32[]{:S(2)}, u32[]{:S(2)}) collective-permute-start(bf16[160,2048]{1,0:T(8,128)(2,1)S(1)} %get-tuple-element.33), channel_id=1, source_target_pairs={{0,1},{1,0},{2,3},{3,2},{4,5},{5,4},{6,7},{7,6},{8,9},{9,8},{10,11... | collective-permute-start | bytes 1966088 | tf_op jit(solution)/shard_map/ppermute | solution.py:435
  10.2 23.4 %collective-permute-start.7 = (bf16[160,2048]{1,0:T(8,128)(2,1)S(1)}, bf16[160,2048]{1,0:T(8,128)(2,1)S(1)}, u32[]{:S(2)}, u32[]{:S(2)}) collective-permute-start(bf16[160,2048]{1,0:T(8,128)(2,1)S(1)} %add_convert_fusion.after.refs_3_), channel_id=1, source_target_pairs={{0,2},{1,3},{2,0},{3,1},{4,6},{5,7},{6,4},{7,5},{8,10},{9,11},{10,... | collective-permute-start | bytes 1966088 | tf_op jit(solution)/shard_map/ppermute | solution.py:381
  13.1 7.7 %collective-permute-start.1 = (bf16[8,768]{1,0:T(8,128)(2,1)S(1)}, bf16[8,768]{1,0:T(8,128)(2,1)S(1)}, u32[]{:S(2)}, u32[]{:S(2)}) collective-permute-start(bf16[8,768]{1,0:T(8,128)(2,1)S(1)} %get-tuple-element.39), channel_id=1, source_target_pairs={{0,4},{4,0},{8,12},{12,8},{1,5},{5,1},{9,13},{13,9},{2,6},{6,2},{1... | collective-permute-start | bytes 36872 | tf_op jit(solution)/shard_map/ppermute | solution.py:439
  14.7 6.2 %collective-permute-start.2 = (bf16[8,768]{1,0:T(8,128)(2,1)S(1)}, bf16[8,768]{1,0:T(8,128)(2,1)S(1)}, u32[]{:S(2)}, u32[]{:S(2)}) collective-permute-start(bf16[8,768]{1,0:T(8,128)(2,1)S(1)} %get-tuple-element.40), channel_id=1, source_target_pairs={{0,8},{4,12},{8,0},{12,4},{1,9},{5,13},{9,1},{13,5},{2,10},{6,14},... | collective-permute-start | bytes 36872 | tf_op jit(solution)/shard_map/ppermute | solution.py:439
  17.3 5.5 %collective-permute-start.3 = (bf16[8,768]{1,0:T(8,128)(2,1)S(1)}, bf16[8,768]{1,0:T(8,128)(2,1)S(1)}, u32[]{:S(2)}, u32[]{:S(2)}) collective-permute-start(bf16[8,768]{1,0:T(8,128)(2,1)S(1)} %get-tuple-element.41), channel_id=1, source_target_pairs={{0,12},{4,8},{8,4},{12,0},{1,13},{5,9},{9,5},{13,1},{2,14},{6,10},... | collective-permute-start | bytes 36872 | tf_op jit(solution)/shard_map/ppermute | solution.py:439
  24.1 4.4 %collective-permute-start.4 = (bf16[8,512]{1,0:T(8,128)(2,1)S(1)}, bf16[8,512]{1,0:T(8,128)(2,1)S(1)}, u32[]{:S(2)}, u32[]{:S(2)}) collective-permute-start(bf16[8,512]{1,0:T(8,128)(2,1)S(1)} %get-tuple-element.42), channel_id=1, source_target_pairs={{0,4},{4,0},{8,12},{12,8},{1,5},{5,1},{9,13},{13,9},{2,6},{6,2},{1... | collective-permute-start | bytes 24584 | tf_op jit(solution)/shard_map/ppermute | solution.py:466
  24.2 4.6 %collective-permute-start.5 = (bf16[8,512]{1,0:T(8,128)(2,1)S(1)}, bf16[8,512]{1,0:T(8,128)(2,1)S(1)}, u32[]{:S(2)}, u32[]{:S(2)}) collective-permute-start(bf16[8,512]{1,0:T(8,128)(2,1)S(1)} %get-tuple-element.43), channel_id=1, source_target_pairs={{0,8},{4,12},{8,0},{12,4},{1,9},{5,13},{9,1},{13,5},{2,10},{6,14},... | collective-permute-start | bytes 24584 | tf_op jit(solution)/shard_map/ppermute | solution.py:466
  26.5 5.4 %collective-permute-start.6 = (bf16[8,512]{1,0:T(8,128)(2,1)S(1)}, bf16[8,512]{1,0:T(8,128)(2,1)S(1)}, u32[]{:S(2)}, u32[]{:S(2)}) collective-permute-start(bf16[8,512]{1,0:T(8,128)(2,1)S(1)} %get-tuple-element.44), channel_id=1, source_target_pairs={{0,12},{4,8},{8,4},{12,0},{1,13},{5,9},{9,5},{13,1},{2,14},{6,10},... | collective-permute-start | bytes 24584 | tf_op jit(solution)/shard_map/ppermute | solution.py:466
  33.4 1.8 %collective-permute-start.8 = (bf16[96,2048]{1,0:T(8,128)(2,1)S(1)}, bf16[96,2048]{1,0:T(8,128)(2,1)S(1)}, u32[]{:S(2)}, u32[]{:S(2)}) collective-permute-start(bf16[96,2048]{1,0:T(8,128)(2,1)S(1)} %get-tuple-element.47), channel_id=1, source_target_pairs={{0,1},{1,0},{2,3},{3,2},{4,5},{5,4},{6,7},{7,6},{8,9},{9,8},{10,11... | collective-permute-start | bytes 1179656 | tf_op jit(solution)/shard_map/ppermute | solution.py:476
  35.3 11.2 %collective-permute-start.13 = (bf16[96,2048]{1,0:T(8,128)(2,1)S(1)}, bf16[96,2048]{1,0:T(8,128)(2,1)S(1)}, u32[]{:S(2)}, u32[]{:S(2)}) collective-permute-start(bf16[96,2048]{1,0:T(8,128)(2,1)S(1)} %add_convert_fusion.1.after), channel_id=1, source_target_pairs={{0,2},{1,3},{2,0},{3,1},{4,6},{5,7},{6,4},{7,5},{8,10},{9,11},{10,... | collective-permute-start | bytes 1179656 | tf_op jit(solution)/shard_map/ppermute | solution.py:381
  37.2 1.6 %collective-permute-start.9 = (bf16[256,512]{1,0:T(8,128)(2,1)S(1)}, bf16[256,512]{1,0:T(8,128)(2,1)S(1)}, u32[]{:S(2)}, u32[]{:S(2)}) collective-permute-start(bf16[256,512]{1,0:T(8,128)(2,1)S(1)} %get-tuple-element.49), channel_id=1, source_target_pairs={{0,1},{1,0},{2,3},{3,2},{4,5},{5,4},{6,7},{7,6},{8,9},{9,8},{10,11... | collective-permute-start | bytes 786440 | tf_op jit(solution)/shard_map/ppermute | solution.py:494
  37.3 1.9 %collective-permute-start.10 = (bf16[256,512]{1,0:T(8,128)(2,1)S(1)}, bf16[256,512]{1,0:T(8,128)(2,1)S(1)}, u32[]{:S(2)}, u32[]{:S(2)}) collective-permute-start(bf16[256,512]{1,0:T(8,128)(2,1)S(1)} %get-tuple-element.50), channel_id=1, source_target_pairs={{0,1},{1,0},{2,3},{3,2},{4,5},{5,4},{6,7},{7,6},{8,9},{9,8},{10,11... | collective-permute-start | bytes 786440 | tf_op jit(solution)/shard_map/ppermute | solution.py:494
  37.8 1.8 %collective-permute-start.11 = (bf16[256,512]{1,0:T(8,128)(2,1)S(1)}, bf16[256,512]{1,0:T(8,128)(2,1)S(1)}, u32[]{:S(2)}, u32[]{:S(2)}) collective-permute-start(bf16[256,512]{1,0:T(8,128)(2,1)S(1)} %get-tuple-element.51), channel_id=1, source_target_pairs={{0,1},{1,0},{2,3},{3,2},{4,5},{5,4},{6,7},{7,6},{8,9},{9,8},{10,11... | collective-permute-start | bytes 786440 | tf_op jit(solution)/shard_map/ppermute | solution.py:494
  37.9 2.1 %collective-permute-start.12 = (bf16[256,512]{1,0:T(8,128)(2,1)S(1)}, bf16[256,512]{1,0:T(8,128)(2,1)S(1)}, u32[]{:S(2)}, u32[]{:S(2)}) collective-permute-start(bf16[256,512]{1,0:T(8,128)(2,1)S(1)} %get-tuple-element.52), channel_id=1, source_target_pairs={{0,1},{1,0},{2,3},{3,2},{4,5},{5,4},{6,7},{7,6},{8,9},{9,8},{10,11... | collective-permute-start | bytes 786440 | tf_op jit(solution)/shard_map/ppermute | solution.py:494

commit v3 on v1

--- a/solution.py
+++ b/solution.py
@@ -436,7 +436,7 @@
 
     last_count = incoming + incoming % 2
     extra_count = last_count - incoming
-    first_count = slot_count // 4 * 2
+    first_count = slot_count // 16 * 9 // 2 * 2
     second_count = slot_count - first_count - last_count
     last_rows = last_count * step_count
 
@@ -506,7 +506,7 @@
     )(lengths, page_table, migration, in_hbm(pool), second, weight, *received)
     mate = lax.ppermute(send, "tp", swap)
     answers = [lax.ppermute(answer, "inst", pairs[k]) for k, answer in zip(rounds, answers)]
-    (keep,) = hold([keep], arrived_first)
+    (keep,) = hold([keep], [*arrived_first, *answers])
     summed = (keep + mate.astype(f32)).astype(bf16)
     arrived_second = send_far(split_far(summed))
 

time: 46.5 us -> 47.8 us (1.028)
  Pallas kernels: 18.4 us -> 19.1 us
    ppermute x3, waiting for transfers between devices: 1.88 us -> 6.95 us  [send_far(): lax.ppermute(part, 'tp', [(t, (t + 2 * d) % tp_count) for t in range(tp_c...]
    ppermute x3, waiting for transfers between devices: 3.23 us -> 1.64 us  [on_device(): mate = lax.ppermute(send, 'tp', swap)]
    ppermute x2, waiting for transfers between devices: 1.58 us -> 0.01 us  [on_device(): own_mates = [lax.ppermute(own_send, 'tp', swap) for own_send in own_sends]]
    ppermute x3, waiting for transfers between devices: 3.9 us -> 2.35 us  [on_device(): lax.ppermute(answer, 'inst', pairs[k])]
    pallas_call x1, Pallas kernels: 5.65 us -> 6.51 us  [on_device(): pl.pallas_call(functools.partial(first_kernel, inst_count, rounds), out_s...]
  transfers between devices with their start and end apart: 14 -> 14, of which waited for: 8 -> 6; matrix products, arithmetic and copies ran while one was open for 0% -> 0% of each run, Pallas kernels for 23% -> 22%
where the time goes in v3:
time: 47.8 us; the launch traced here: 47.5 us
  Pallas kernels  19.1 us (40%)
  starting transfers between devices  14.2 us (30%)
  waiting for transfers between devices  13.8 us (29%)
    ppermute x3, waiting for transfers between devices, send_far(): lax.ppermute(part, 'tp', [(t, (t + 2 * d) % tp_count) for t in range(tp_c...  6.95 us
    pallas_call x1, Pallas kernels, on_device(): pl.pallas_call(functools.partial(first_kernel, inst_count, rounds), out_s...  6.51 us
    ppermute x3, starting transfers between devices, on_device(): lax.ppermute(answer, 'inst', pairs[k])  4.44 us
    ppermute x3, starting transfers between devices, on_device(): lax.ppermute(pack, 'inst', pairs[k])  4.39 us
    ppermute x3, starting transfers between devices, send_far(): lax.ppermute(part, 'tp', [(t, (t + 2 * d) % tp_count) for t in range(tp_c...  4.1 us
    pallas_call x1, Pallas kernels, on_device(): pl.pallas_call(functools.partial(away_kernel, inst_count, rounds), out_sh...  3.36 us
    ppermute x3, waiting for transfers between devices, on_device(): lax.ppermute(pack, 'inst', pairs[k])  2.91 us
    ppermute x3, waiting for transfers between devices, on_device(): lax.ppermute(answer, 'inst', pairs[k])  2.35 us
  transfers between devices with their start and end apart: 14, of which 6 were waited for; matrix products, arithmetic and copies ran while one was open for 0% of the time, Pallas kernels for 22%

profile of v3, /device:TPU:0, one launch (start us, length us, event | category | flops | bytes accessed | tf_op | source)
XLA Modules:
  0.0 47.5 jit_solution(6995539474278682547)
XLA Ops:
  0.0 0.0 copy-start
  0.0 6.5 %attend_first.1 = (bf16[144,512]{1,0:T(8,128)(2,1)S(1)}, bf16[32,8,512]{2,1,0:T(8,128)(2,1)S(1)}, bf16[32,8,256]{2,1,0:T(8,128)(2,1)S(1)}, bf16[8,768]{1,0:T(8,1...) custom-call(s32[4,12]{1,0:T(4,128)} %bitcast.11, s32[128]{0:T(128)} %lengths.5, s32[4,32]{1,0:T(4,128)} %bitcast.17, ...), custom_call_target="tpu_custom_call" | custom-call | flops 1 | bytes 1 | tf_op jit(solution)/shard_map/attend_first/pallas_call | solution.py:453
  6.5 0.0 copy-done
  6.5 0.0 copy-start.1
  6.5 0.8 %far_first.1 = (f32[144,2048]{1,0:T(8,128)S(1)}, bf16[144,2048]{1,0:T(8,128)(2,1)S(1)}) custom-call(bf16[144,512]{1,0:T(8,128)(2,1)S(1)} %get-tuple-element.29.attended.first, bf16[512,8192]{1,0:T(8,128)(2,1)S(1)} %copy-done), custom_call_target="tpu_custom_call" | custom-call | flops 1 | bytes 1 | tf_op jit(solution)/shard_map/far_first/pallas_call | solution.py:469
  7.3 0.5 %collective-permute-start = (bf16[144,2048]{1,0:T(8,128)(2,1)S(1)}, bf16[144,2048]{1,0:T(8,128)(2,1)S(1)}, u32[]{:S(2)}, u32[]{:S(2)}) collective-permute-start(bf16[144,2048]{1,0:T(8,128)(2,1)S(1)} %get-tuple-element.33), channel_id=1, source_target_pairs={{0,1},{1,0},{2,3},{3,2},{4,5},{5,4},{6,7},{7,6},{8,9},{9,8},{10,11... | collective-permute-start | bytes 1769480 | tf_op jit(solution)/shard_map/ppermute | solution.py:478
  7.9 1.6 %collective-permute-done = bf16[144,2048]{1,0:T(8,128)(2,1)S(1)} collective-permute-done((bf16[144,2048]{1,0:T(8,128)(2,1)S(1)}, bf16[144,2048]{1,0:T(8,128)(2,1)S(1)}, u32[]{:S(2)}, u32[]{:S(2)}) %collective-permute-start) | collective-permute-done | bytes 589856 | tf_op jit(solution)/shard_map/ppermute | solution.py:478
  9.5 0.1 add_convert_fusion.after.refs_3_
  9.6 3.0 %collective-permute-start.7 = (bf16[144,2048]{1,0:T(8,128)(2,1)S(1)}, bf16[144,2048]{1,0:T(8,128)(2,1)S(1)}, u32[]{:S(2)}, u32[]{:S(2)}) collective-permute-start(bf16[144,2048]{1,0:T(8,128)(2,1)S(1)} %add_convert_fusion.after.refs_3_), channel_id=1, source_target_pairs={{0,2},{1,3},{2,0},{3,1},{4,6},{5,7},{6,4},{7,5},{8,10},{9,11},{10,... | collective-permute-start | bytes 1769480 | tf_op jit(solution)/shard_map/ppermute | solution.py:421
  12.6 1.6 %collective-permute-start.1 = (bf16[8,768]{1,0:T(8,128)(2,1)S(1)}, bf16[8,768]{1,0:T(8,128)(2,1)S(1)}, u32[]{:S(2)}, u32[]{:S(2)}) collective-permute-start(bf16[8,768]{1,0:T(8,128)(2,1)S(1)} %get-tuple-element.39), channel_id=1, source_target_pairs={{0,4},{4,0},{8,12},{12,8},{1,5},{5,1},{9,13},{13,9},{2,6},{6,2},{1... | collective-permute-start | bytes 36872 | tf_op jit(solution)/shard_map/ppermute | solution.py:482
  14.1 2.6 %collective-permute-start.2 = (bf16[8,768]{1,0:T(8,128)(2,1)S(1)}, bf16[8,768]{1,0:T(8,128)(2,1)S(1)}, u32[]{:S(2)}, u32[]{:S(2)}) collective-permute-start(bf16[8,768]{1,0:T(8,128)(2,1)S(1)} %get-tuple-element.40), channel_id=1, source_target_pairs={{0,8},{4,12},{8,0},{12,4},{1,9},{5,13},{9,1},{13,5},{2,10},{6,14},... | collective-permute-start | bytes 36872 | tf_op jit(solution)/shard_map/ppermute | solution.py:482
  16.7 0.2 collective-permute-start.3
  17.0 0.0 copy-done.1
  17.0 2.3 %attend_second.1 = (bf16[80,512]{1,0:T(8,128)(2,1)S(1)}, bf16[1,8,512]{2,1,0:T(8,128)(2,1)S(1)}) custom-call(s32[4,12]{1,0:T(4,128)} %bitcast.12, s32[128]{0:T(128)} %lengths.5, s32[4,32]{1,0:T(4,128)} %bitcast.18, bf16[32,8,512]{2,1,0:T(8,128)(2,1)S(1)} %get-tuple-element.30.queries, bf16[32,8,256]{2,1,0:T(8,128)(2,1)S(1)} %get-tuple-element.31.new_tokens, ...), custom_call_target="tpu_custom_call" | custom-call | flops 1 | bytes 1 | tf_op jit(solution)/shard_map/attend_second/pallas_call | solution.py:484
  19.3 0.0 collective-permute-done.1.refs_0_
  19.3 0.0 collective-permute-done.2.refs_1_
  19.3 2.9 %collective-permute-done.3.refs_2_ = bf16[8,768]{1,0:T(8,128)(2,1)S(1)} collective-permute-done((bf16[8,768]{1,0:T(8,128)(2,1)S(1)}, bf16[8,768]{1,0:T(8,128)(2,1)S(1)}, u32[]{:S(2)}, u32[]{:S(2)}) %collective-permute-start.3) | collective-permute-done | bytes 12320 | tf_op jit(solution)/shard_map/ppermute | solution.py:482
  22.2 3.4 %attend_away.1 = (bf16[8,512]{1,0:T(8,128)(2,1)S(1)}, bf16[8,512]{1,0:T(8,128)(2,1)S(1)}, bf16[8,512]{1,0:T(8,128)(2,1)S(1)}, f32[80,2048]{1,0:T(8,128)S(1)}, bf16[80,2048]{1,0:T(8,128)(2,1)S(1)}) custom-call(s32[128]{0:T(128)} %lengths.5, s32[4,32]{1,0:T(4,128)} %bitcast.19, s32[4,12]{1,0:T(4,128)} %bitcast.13, bf16[128,128,256]{2,1,0:T(8,128)(2,1)} %bitcast.7, ...), custom_call_target="tpu_custom_call" | custom-call | flops 1 | bytes 1 | tf_op jit(solution)/shard_map/attend_away/pallas_call | solution.py:497
  25.6 0.1 collective-permute-start.8
  25.7 0.1 collective-permute-start.4
  25.8 1.3 %collective-permute-start.5 = (bf16[8,512]{1,0:T(8,128)(2,1)S(1)}, bf16[8,512]{1,0:T(8,128)(2,1)S(1)}, u32[]{:S(2)}, u32[]{:S(2)}) collective-permute-start(bf16[8,512]{1,0:T(8,128)(2,1)S(1)} %get-tuple-element.43), channel_id=1, source_target_pairs={{0,8},{4,12},{8,0},{12,4},{1,9},{5,13},{9,1},{13,5},{2,10},{6,14},... | collective-permute-start | bytes 24584 | tf_op jit(solution)/shard_map/ppermute | solution.py:508
  27.0 3.1 %collective-permute-start.6 = (bf16[8,512]{1,0:T(8,128)(2,1)S(1)}, bf16[8,512]{1,0:T(8,128)(2,1)S(1)}, u32[]{:S(2)}, u32[]{:S(2)}) collective-permute-start(bf16[8,512]{1,0:T(8,128)(2,1)S(1)} %get-tuple-element.44), channel_id=1, source_target_pairs={{0,12},{4,8},{8,4},{12,0},{1,13},{5,9},{9,5},{13,1},{2,14},{6,10},... | collective-permute-start | bytes 24584 | tf_op jit(solution)/shard_map/ppermute | solution.py:508
  30.1 0.0 collective-permute-done.4.refs_0_.refs_2_
  30.1 0.2 collective-permute-done.5.refs_1_.refs_3_
  30.4 2.1 %collective-permute-done.6.refs_2_.refs_4_ = bf16[8,512]{1,0:T(8,128)(2,1)S(1)} collective-permute-done((bf16[8,512]{1,0:T(8,128)(2,1)S(1)}, bf16[8,512]{1,0:T(8,128)(2,1)S(1)}, u32[]{:S(2)}, u32[]{:S(2)}) %collective-permute-start.6) | collective-permute-done | bytes 8224 | tf_op jit(solution)/shard_map/ppermute | solution.py:508
  32.5 0.0 collective-permute-done.7.refs_1_.refs_2_
  32.5 0.0 collective-permute-done.8
  32.5 0.1 add_convert_fusion.1.after
  32.6 0.6 %collective-permute-start.11 = (bf16[80,2048]{1,0:T(8,128)(2,1)S(1)}, bf16[80,2048]{1,0:T(8,128)(2,1)S(1)}, u32[]{:S(2)}, u32[]{:S(2)}) collective-permute-start(bf16[80,2048]{1,0:T(8,128)(2,1)S(1)} %add_convert_fusion.1.after), channel_id=1, source_target_pairs={{0,2},{1,3},{2,0},{3,1},{4,6},{5,7},{6,4},{7,5},{8,10},{9,11},{10,... | collective-permute-start | bytes 983048 | tf_op jit(solution)/shard_map/ppermute | solution.py:421
  33.1 1.5 %last_rows.1 = (bf16[32,512]{1,0:T(8,128)(2,1)S(1)}, f32[32,2048]{1,0:T(8,128)S(1)}, bf16[32,2048]{1,0:T(8,128)(2,1)S(1)}) custom-call(s32[4,12]{1,0:T(4,128)} %bitcast.14, bf16[512,8192]{1,0:T(8,128)(2,1)S(1)} %copy-done, bf16[1,8,512]{2,1,0:T(8,128)(2,1)S(1)} %get-tuple-element.35.extra, bf16[8,512]{1,0:T(8,128)(2,1)S(1)} %collective-permute-done.4.refs_0_.refs_2_, ...), custom_call_target="tpu_custom_call" | custom-call | flops 1 | bytes 1 | tf_op jit(solution)/shard_map/last_rows/pallas_call | solution.py:513
  34.7 0.0 collective-permute-start.12
  34.7 1.3 %own_columns.1 = (f32[256,2048]{1,0:T(8,128)S(1)}, bf16[256,1024]{1,0:T(8,128)(2,1)S(1)}, bf16[256,1024]{1,0:T(8,128)(2,1)S(1)}) custom-call(bf16[512,8192]{1,0:T(8,128)(2,1)S(1)} %copy-done, bf16[144,512]{1,0:T(8,128)(2,1)S(1)} %get-tuple-element.29.attended.first, bf16[80,512]{1,0:T(8,128)(2,1)S(1)} %get-tuple-element.34.second, ...), custom_call_target="tpu_custom_call" | custom-call | flops 1 | bytes 1 | tf_op jit(solution)/shard_map/own_columns/pallas_call | solution.py:527
  36.0 0.6 %collective-permute-start.9 = (bf16[256,1024]{1,0:T(8,128)(2,1)S(1)}, bf16[256,1024]{1,0:T(8,128)(2,1)S(1)}, u32[]{:S(2)}, u32[]{:S(2)}) collective-permute-start(bf16[256,1024]{1,0:T(8,128)(2,1)S(1)} %get-tuple-element.49), channel_id=1, source_target_pairs={{0,1},{1,0},{2,3},{3,2},{4,5},{5,4},{6,7},{7,6},{8,9},{9,8},{10,11... | collective-permute-start | bytes 1572872 | tf_op jit(solution)/shard_map/ppermute | solution.py:541
  36.5 0.1 collective-permute-start.10
  36.6 4.4 %collective-permute-done.11.refs_1_.refs_3_ = bf16[80,2048]{1,0:T(8,128)(2,1)S(1)} collective-permute-done((bf16[80,2048]{1,0:T(8,128)(2,1)S(1)}, bf16[80,2048]{1,0:T(8,128)(2,1)S(1)}, u32[]{:S(2)}, u32[]{:S(2)}) %collective-permute-start.11) | collective-permute-done | bytes 327712 | tf_op jit(solution)/shard_map/ppermute | solution.py:421
  41.0 0.0 collective-permute-done.12
  41.0 0.6 %collective-permute-start.13 = (bf16[32,2048]{1,0:T(8,128)(2,1)S(1)}, bf16[32,2048]{1,0:T(8,128)(2,1)S(1)}, u32[]{:S(2)}, u32[]{:S(2)}) collective-permute-start(bf16[32,2048]{1,0:T(8,128)(2,1)S(1)} %add_convert_fusion.2), channel_id=1, source_target_pairs={{0,2},{1,3},{2,0},{3,1},{4,6},{5,7},{6,4},{7,5},{8,10},{9,11},{10,... | collective-permute-start | bytes 393224 | tf_op jit(solution)/shard_map/ppermute | solution.py:421
  41.6 0.0 collective-permute-done.9.refs_0_
  41.6 0.0 collective-permute-done.10.refs_1_
  41.6 1.9 %sum_early.1.refs_3_ = bf16[32,8,2048]{2,1,0:T(8,128)(2,1)} custom-call(s32[4,12]{1,0:T(4,128)} %bitcast.15, f32[256,2048]{1,0:T(8,128)S(1)} %get-tuple-element.48.refs_2_.keep, bf16[256,1024]{1,0:T(8,128)(2,1)S(1)} %collective-permute-done.9.refs_0_, bf16[256,1024]{1,0:T(8,128)(2,1)S(1)} %collective-permute-done.10.refs_1_, ...), custom_call_target="tpu_custom_call" | custom-call | flops 1 | bytes 1 | tf_op jit(solution)/shard_map/sum_early/pallas_call | solution.py:548
  43.5 2.6 %collective-permute-done.13.refs_2_ = bf16[32,2048]{1,0:T(8,128)(2,1)S(1)} collective-permute-done((bf16[32,2048]{1,0:T(8,128)(2,1)S(1)}, bf16[32,2048]{1,0:T(8,128)(2,1)S(1)}, u32[]{:S(2)}, u32[]{:S(2)}) %collective-permute-start.13) | collective-permute-done | bytes 131104 | tf_op jit(solution)/shard_map/ppermute | solution.py:421
  46.1 1.4 %sum_last.1 = bf16[32,8,2048]{2,1,0:T(8,128)(2,1)} custom-call(s32[4,12]{1,0:T(4,128)} %bitcast.16, f32[256,2048]{1,0:T(8,128)S(1)} %get-tuple-element.48.refs_2_.keep, bf16[256,1024]{1,0:T(8,128)(2,1)S(1)} %collective-permute-done.9.refs_0_, bf16[256,1024]{1,0:T(8,128)(2,1)S(1)} %collective-permute-done.10.refs_1_, ...), custom_call_target="tpu_custom_call", output_to_operand_aliasing={{}: (5, {})} | custom-call | flops 1 | bytes 1 | tf_op jit(solution)/shard_map/sum_last/pallas_call | solution.py:560
  (4 shorter events, 0.0 us)
Async XLA Ops:
  0.0 6.5 %copy-start = (bf16[512,8192]{1,0:T(8,128)(2,1)S(1)}, bf16[512,8192]{1,0:T(8,128)(2,1)}, u32[]{:S(2)}) copy-start(bf16[512,8192]{1,0:T(8,128)(2,1)} %weight.7) | copy-start | bytes 25165828
  6.5 10.4 %copy-start.1 = (bf16[1,128,128,256]{3,2,1,0:T(8,128)(2,1)S(1)}, bf16[1,128,128,256]{3,2,1,0:T(8,128)(2,1)}, u32[]{:S(2)}) copy-start(bf16[1,128,128,256]{3,2,1,0:T(8,128)(2,1)} %param.9) | copy-start | bytes 25165828
  7.3 2.1 %collective-permute-start = (bf16[144,2048]{1,0:T(8,128)(2,1)S(1)}, bf16[144,2048]{1,0:T(8,128)(2,1)S(1)}, u32[]{:S(2)}, u32[]{:S(2)}) collective-permute-start(bf16[144,2048]{1,0:T(8,128)(2,1)S(1)} %get-tuple-element.33), channel_id=1, source_target_pairs={{0,1},{1,0},{2,3},{3,2},{4,5},{5,4},{6,7},{7,6},{8,9},{9,8},{10,11... | collective-permute-start | bytes 1769480 | tf_op jit(solution)/shard_map/ppermute | solution.py:478
  9.6 22.9 %collective-permute-start.7 = (bf16[144,2048]{1,0:T(8,128)(2,1)S(1)}, bf16[144,2048]{1,0:T(8,128)(2,1)S(1)}, u32[]{:S(2)}, u32[]{:S(2)}) collective-permute-start(bf16[144,2048]{1,0:T(8,128)(2,1)S(1)} %add_convert_fusion.after.refs_3_), channel_id=1, source_target_pairs={{0,2},{1,3},{2,0},{3,1},{4,6},{5,7},{6,4},{7,5},{8,10},{9,11},{10,... | collective-permute-start | bytes 1769480 | tf_op jit(solution)/shard_map/ppermute | solution.py:421
  12.6 6.7 %collective-permute-start.1 = (bf16[8,768]{1,0:T(8,128)(2,1)S(1)}, bf16[8,768]{1,0:T(8,128)(2,1)S(1)}, u32[]{:S(2)}, u32[]{:S(2)}) collective-permute-start(bf16[8,768]{1,0:T(8,128)(2,1)S(1)} %get-tuple-element.39), channel_id=1, source_target_pairs={{0,4},{4,0},{8,12},{12,8},{1,5},{5,1},{9,13},{13,9},{2,6},{6,2},{1... | collective-permute-start | bytes 36872 | tf_op jit(solution)/shard_map/ppermute | solution.py:482
  14.1 5.2 %collective-permute-start.2 = (bf16[8,768]{1,0:T(8,128)(2,1)S(1)}, bf16[8,768]{1,0:T(8,128)(2,1)S(1)}, u32[]{:S(2)}, u32[]{:S(2)}) collective-permute-start(bf16[8,768]{1,0:T(8,128)(2,1)S(1)} %get-tuple-element.40), channel_id=1, source_target_pairs={{0,8},{4,12},{8,0},{12,4},{1,9},{5,13},{9,1},{13,5},{2,10},{6,14},... | collective-permute-start | bytes 36872 | tf_op jit(solution)/shard_map/ppermute | solution.py:482
  16.7 5.5 %collective-permute-start.3 = (bf16[8,768]{1,0:T(8,128)(2,1)S(1)}, bf16[8,768]{1,0:T(8,128)(2,1)S(1)}, u32[]{:S(2)}, u32[]{:S(2)}) collective-permute-start(bf16[8,768]{1,0:T(8,128)(2,1)S(1)} %get-tuple-element.41), channel_id=1, source_target_pairs={{0,12},{4,8},{8,4},{12,0},{1,13},{5,9},{9,5},{13,1},{2,14},{6,10},... | collective-permute-start | bytes 36872 | tf_op jit(solution)/shard_map/ppermute | solution.py:482
  25.6 6.9 %collective-permute-start.8 = (bf16[80,2048]{1,0:T(8,128)(2,1)S(1)}, bf16[80,2048]{1,0:T(8,128)(2,1)S(1)}, u32[]{:S(2)}, u32[]{:S(2)}) collective-permute-start(bf16[80,2048]{1,0:T(8,128)(2,1)S(1)} %get-tuple-element.47), channel_id=1, source_target_pairs={{0,1},{1,0},{2,3},{3,2},{4,5},{5,4},{6,7},{7,6},{8,9},{9,8},{10,11... | collective-permute-start | bytes 983048 | tf_op jit(solution)/shard_map/ppermute | solution.py:507
  25.7 4.5 %collective-permute-start.4 = (bf16[8,512]{1,0:T(8,128)(2,1)S(1)}, bf16[8,512]{1,0:T(8,128)(2,1)S(1)}, u32[]{:S(2)}, u32[]{:S(2)}) collective-permute-start(bf16[8,512]{1,0:T(8,128)(2,1)S(1)} %get-tuple-element.42), channel_id=1, source_target_pairs={{0,4},{4,0},{8,12},{12,8},{1,5},{5,1},{9,13},{13,9},{2,6},{6,2},{1... | collective-permute-start | bytes 24584 | tf_op jit(solution)/shard_map/ppermute | solution.py:508
  25.8 4.6 %collective-permute-start.5 = (bf16[8,512]{1,0:T(8,128)(2,1)S(1)}, bf16[8,512]{1,0:T(8,128)(2,1)S(1)}, u32[]{:S(2)}, u32[]{:S(2)}) collective-permute-start(bf16[8,512]{1,0:T(8,128)(2,1)S(1)} %get-tuple-element.43), channel_id=1, source_target_pairs={{0,8},{4,12},{8,0},{12,4},{1,9},{5,13},{9,1},{13,5},{2,10},{6,14},... | collective-permute-start | bytes 24584 | tf_op jit(solution)/shard_map/ppermute | solution.py:508
  27.0 5.4 %collective-permute-start.6 = (bf16[8,512]{1,0:T(8,128)(2,1)S(1)}, bf16[8,512]{1,0:T(8,128)(2,1)S(1)}, u32[]{:S(2)}, u32[]{:S(2)}) collective-permute-start(bf16[8,512]{1,0:T(8,128)(2,1)S(1)} %get-tuple-element.44), channel_id=1, source_target_pairs={{0,12},{4,8},{8,4},{12,0},{1,13},{5,9},{9,5},{13,1},{2,14},{6,10},... | collective-permute-start | bytes 24584 | tf_op jit(solution)/shard_map/ppermute | solution.py:508
  32.6 8.4 %collective-permute-start.11 = (bf16[80,2048]{1,0:T(8,128)(2,1)S(1)}, bf16[80,2048]{1,0:T(8,128)(2,1)S(1)}, u32[]{:S(2)}, u32[]{:S(2)}) collective-permute-start(bf16[80,2048]{1,0:T(8,128)(2,1)S(1)} %add_convert_fusion.1.after), channel_id=1, source_target_pairs={{0,2},{1,3},{2,0},{3,1},{4,6},{5,7},{6,4},{7,5},{8,10},{9,11},{10,... | collective-permute-start | bytes 983048 | tf_op jit(solution)/shard_map/ppermute | solution.py:421
  34.7 6.3 %collective-permute-start.12 = (bf16[32,2048]{1,0:T(8,128)(2,1)S(1)}, bf16[32,2048]{1,0:T(8,128)(2,1)S(1)}, u32[]{:S(2)}, u32[]{:S(2)}) collective-permute-start(bf16[32,2048]{1,0:T(8,128)(2,1)S(1)} %get-tuple-element.52), channel_id=1, source_target_pairs={{0,1},{1,0},{2,3},{3,2},{4,5},{5,4},{6,7},{7,6},{8,9},{9,8},{10,11... | collective-permute-start | bytes 393224 | tf_op jit(solution)/shard_map/ppermute | solution.py:526
  36.0 5.6 %collective-permute-start.9 = (bf16[256,1024]{1,0:T(8,128)(2,1)S(1)}, bf16[256,1024]{1,0:T(8,128)(2,1)S(1)}, u32[]{:S(2)}, u32[]{:S(2)}) collective-permute-start(bf16[256,1024]{1,0:T(8,128)(2,1)S(1)} %get-tuple-element.49), channel_id=1, source_target_pairs={{0,1},{1,0},{2,3},{3,2},{4,5},{5,4},{6,7},{7,6},{8,9},{9,8},{10,11... | collective-permute-start | bytes 1572872 | tf_op jit(solution)/shard_map/ppermute | solution.py:541
  36.5 5.1 %collective-permute-start.10 = (bf16[256,1024]{1,0:T(8,128)(2,1)S(1)}, bf16[256,1024]{1,0:T(8,128)(2,1)S(1)}, u32[]{:S(2)}, u32[]{:S(2)}) collective-permute-start(bf16[256,1024]{1,0:T(8,128)(2,1)S(1)} %get-tuple-element.50), channel_id=1, source_target_pairs={{0,1},{1,0},{2,3},{3,2},{4,5},{5,4},{6,7},{7,6},{8,9},{9,8},{10,11... | collective-permute-start | bytes 1572872 | tf_op jit(solution)/shard_map/ppermute | solution.py:541
  41.0 5.0 %collective-permute-start.13 = (bf16[32,2048]{1,0:T(8,128)(2,1)S(1)}, bf16[32,2048]{1,0:T(8,128)(2,1)S(1)}, u32[]{:S(2)}, u32[]{:S(2)}) collective-permute-start(bf16[32,2048]{1,0:T(8,128)(2,1)S(1)} %add_convert_fusion.2), channel_id=1, source_target_pairs={{0,2},{1,3},{2,0},{3,1},{4,6},{5,7},{6,4},{7,5},{8,10},{9,11},{10,... | collective-permute-start | bytes 393224 | tf_op jit(solution)/shard_map/ppermute | solution.py:421

commit v4 on v1

--- a/solution.py
+++ b/solution.py
@@ -9,7 +9,7 @@
 
 LOG2E = 1.4426950408889634
 MASKED = -1e30
-GROUP = 8
+GROUP = 16
 NEVER = 2**30
 PIECES = 2
 
@@ -288,8 +288,8 @@
         extra[i] = row.astype(extra.dtype)
 
 
-def last_rows_kernel(inst_count, rounds, migration, weight, extra, *refs):
-    answers, (rows, keep, send) = refs[:-3], refs[-3:]
+def last_rows_kernel(inst_count, rounds, migration, weight, extra, after, *refs):
+    answers, (keep, send, rows) = refs[:-3], refs[-3:]
     me = lax.axis_index("inst")
     _, sources = arrivals_of(migration, inst_count)
     last = [extra[i].astype(jnp.float32) for i in range(extra.shape[0])]
@@ -300,18 +300,23 @@
             row = jnp.where(source == peer_of(me, k, inst_count), answer, row)
         last.append(row)
     store_rows(last, rows)
-    project_far(rows, weight, keep, send, stacked=True)
-
-
-def own_kernel(weight, first, second, last, after, keep, *refs):
+    core = lax.rem(lax.axis_index("tp"), 2)
+    chip = lax.axis_index("tp") // 2
+    chips = lax.axis_size("tp") // 2
+    columns = keep.shape[1]
+    for target, side in ((send, 1 - core), (keep, core)):
+        for d in range(1, chips + 1):
+            first = (2 * lax.rem(chip + d, chips) + side) * columns
+            project(rows, weight, first, columns, target, (d - 1) * rows.shape[0])
+
+
+def own_kernel(weight, first, second, after, keep, *refs):
     sends, rows = refs[:-1], refs[-1]
     core = lax.rem(lax.axis_index("tp"), 2)
     pair = lax.axis_index("tp") // 2 * 2
     columns = keep.shape[1]
-    at = 0
-    for part in (first, second, last):
-        rows[at : at + part.shape[0], :] = part[...]
-        at += part.shape[0]
+    rows[: first.shape[0], :] = first[...]
+    rows[first.shape[0] :, :] = second[...]
     at = 0
     for send in sends:
         project(rows, weight, (pair + 1 - core) * columns + at, send.shape[1], send)
@@ -351,25 +356,20 @@
     pltpu.make_async_copy(staged, out.at[pl.ds(0, staged.shape[0])], sem.at[0]).wait()
 
 
-def last_kernel(inst_count, first, piece_count, migration, keep, *refs):
-    mates, parts, (out, staged, sem) = refs[:piece_count], refs[piece_count:-4], refs[-3:]
+def last_kernel(inst_count, first, migration, keep, mate, *refs):
+    parts, (out, staged, sem) = refs[:-4], refs[-3:]
     step_count = out.shape[1]
     pair = 2 * step_count
-    width = mates[0].shape[1]
     size = parts[0].shape[0]
     arrivals, _ = arrivals_of(migration, inst_count)
     for at in range(0, size, pair):
         own = keep.shape[0] - size + at
-        for m, mate in enumerate(mates):
-            columns = slice(m * width, (m + 1) * width)
-            total = keep[own : own + pair, columns] + mate[own : own + pair, :].astype(jnp.float32)
-            for part in parts:
-                total = total + part[at : at + pair, columns].astype(jnp.float32)
-            total = total.astype(jnp.bfloat16)
-            for half in range(2):
-                staged[at // step_count + half, :, columns] = total[
-                    half * step_count : (half + 1) * step_count
-                ]
+        total = keep[own : own + pair, :] + mate[own : own + pair, :].astype(jnp.float32)
+        for part in parts:
+            total = total + part[at : at + pair, :].astype(jnp.float32)
+        total = total.astype(jnp.bfloat16)
+        for half in range(2):
+            staged[at // step_count + half] = total[half * step_count : (half + 1) * step_count]
     scatter_rows(staged, out, arrivals, first, sem)
 
 
@@ -510,64 +510,72 @@
     summed = (keep + mate.astype(f32)).astype(bf16)
     arrived_second = send_far(split_far(summed))
 
-    last, keep, send = pl.pallas_call(
+    early_rows = (first_count + second_count) * step_count
+    pieces = PIECES
+    early_keep, *early_sends = pl.pallas_call(
+        own_kernel,
+        out_shape=[
+            pltpu.VMEM((early_rows, columns), f32),
+            *[pltpu.VMEM((early_rows, columns // pieces), bf16)] * pieces,
+        ],
+        in_specs=[VMEM, VMEM, VMEM, ANY],
+        out_specs=[VMEM] * (1 + pieces),
+        scratch_shapes=[pltpu.VMEM((early_rows, width), bf16)],
+        compiler_params=limit,
+        cost_estimate=light,
+        name="own_columns",
+    )(weight, first, second, summed)
+    early_mates = [lax.ppermute(early_send, "tp", swap) for early_send in early_sends]
+
+    keep, send = pl.pallas_call(
         functools.partial(last_rows_kernel, inst_count, rounds),
         out_shape=[
-            rows_shape(last_count),
-            pltpu.VMEM((last_rows * (chips - 1), columns), f32),
-            pltpu.VMEM((last_rows * (chips - 1), columns), bf16),
+            pltpu.VMEM((last_rows * chips, columns), f32),
+            pltpu.VMEM((last_rows * chips, columns), bf16),
         ],
-        in_specs=[SMEM] + [VMEM] * (2 + len(rounds)),
-        out_specs=[VMEM] * 3,
+        in_specs=[SMEM] + [VMEM] * 2 + [ANY] + [VMEM] * len(rounds),
+        out_specs=[VMEM] * 2,
+        scratch_shapes=[pltpu.VMEM((last_rows, width), bf16)],
         compiler_params=limit,
         cost_estimate=light,
         name="last_rows",
-    )(migration, weight, in_vmem(extra), *answers)
+    )(migration, weight, in_vmem(extra), early_keep, *answers)
     mate = lax.ppermute(send, "tp", swap)
-    own_keep, *own_sends = pl.pallas_call(
-        own_kernel,
-        out_shape=[
-            pltpu.VMEM((row_count, columns), f32),
-            *[pltpu.VMEM((row_count, columns // PIECES), bf16)] * PIECES,
-        ],
-        in_specs=[VMEM] * 4 + [ANY],
-        out_specs=[VMEM] * (1 + PIECES),
-        scratch_shapes=[pltpu.VMEM((row_count, width), bf16)],
-        compiler_params=limit,
-        cost_estimate=light,
-        name="own_columns",
-    )(weight, first, second, in_vmem(last), summed)
-    own_keep = in_vmem(own_keep)
-    own_mates = [lax.ppermute(own_send, "tp", swap) for own_send in own_sends]
-    (keep,) = hold([keep], [*arrived_second, own_keep])
-    summed = (keep + mate.astype(f32)).astype(bf16)
+    (keep,) = hold([keep], arrived_second)
+    summed = (keep[:-last_rows] + mate[:-last_rows].astype(f32)).astype(bf16)
     arrived_last = send_far([summed[d * last_rows : (d + 1) * last_rows] for d in range(chips - 1)])
 
     early = slot_count - last_count
     out_shape = (slot_count, step_count, columns)
     out = pl.pallas_call(
         functools.partial(
-            sum_kernel, inst_count, [first_count * step_count, second_count * step_count], PIECES
+            sum_kernel, inst_count, [first_count * step_count, second_count * step_count], pieces
         ),
         out_shape=pltpu.HBM(out_shape, bf16),
-        in_specs=[SMEM] + [VMEM] * (1 + PIECES + 2 * (chips - 1)),
+        in_specs=[SMEM] + [VMEM] * (1 + pieces + 2 * (chips - 1)),
         out_specs=ANY,
-        scratch_shapes=[pltpu.VMEM((early, step_count, columns), bf16), dma((1,))],
+        scratch_shapes=[
+            pltpu.VMEM((early, step_count, columns), bf16),
+            pltpu.SemaphoreType.DMA((1,)),
+        ],
         compiler_params=limit,
         cost_estimate=light,
         name="sum_early",
-    )(migration, own_keep, *own_mates, *arrived_first, *arrived_second)
+    )(migration, in_vmem(early_keep), *early_mates, *arrived_first, *arrived_second)
     out = pl.pallas_call(
-        functools.partial(last_kernel, inst_count, early, PIECES),
+        functools.partial(last_kernel, inst_count, early),
         out_shape=pltpu.HBM(out_shape, bf16),
-        in_specs=[SMEM] + [VMEM] * (PIECES + chips) + [ANY],
+        in_specs=[SMEM] + [VMEM] * (chips + 1) + [ANY],
         out_specs=ANY,
-        scratch_shapes=[pltpu.VMEM((last_count, step_count, columns), bf16), dma((1,))],
-        input_output_aliases={PIECES + chips + 1: 0},
+        scratch_shapes=[
+            pltpu.VMEM((last_count, step_count, columns), bf16),
+            pltpu.SemaphoreType.DMA((1,)),
+        ],
+        input_output_aliases={2 + chips: 0},
         compiler_params=limit,
         cost_estimate=light,
         name="sum_last",
-    )(migration, own_keep, *own_mates, *arrived_last, out)
+    )(migration, in_vmem(keep), mate, *arrived_last, out)
     return out.reshape(row_count, columns)
 
 

time: 46.5 us -> 46.1 us (level)
    ppermute x3, waiting for transfers between devices: 3.9 us -> 2.78 us  [on_device(): lax.ppermute(answer, 'inst', pairs[k])]
    ppermute x3, waiting for transfers between devices: 3.23 us -> 4.18 us  [on_device(): mate = lax.ppermute(send, 'tp', swap)]
    ppermute x2, waiting for transfers between devices: 1.58 us -> 0.71 us  [on_device(): lax.ppermute(early_send, 'tp', swap)]
    pallas_call x1, Pallas kernels: 1.55 us -> 2.26 us  [on_device(): pl.pallas_call(functools.partial(last_rows_kernel, inst_count, rounds), o...]
    ppermute x3, waiting for transfers between devices: 1.88 us -> 2.46 us  [send_far(): lax.ppermute(part, 'tp', [(t, (t + 2 * d) % tp_count) for t in range(tp_c...]
where the time goes in v4:
time: 46.1 us; the launch traced here: 45.8 us
  Pallas kernels  18.2 us (39%)
  starting transfers between devices  14 us (30%)
  waiting for transfers between devices  13.2 us (29%)
    pallas_call x1, Pallas kernels, on_device(): pl.pallas_call(functools.partial(first_kernel, inst_count, rounds), out_s...  5.32 us
    ppermute x3, starting transfers between devices, on_device(): lax.ppermute(answer, 'inst', pairs[k])  4.39 us
    ppermute x3, starting transfers between devices, on_device(): lax.ppermute(pack, 'inst', pairs[k])  4.39 us
    ppermute x3, waiting for transfers between devices, on_device(): mate = lax.ppermute(send, 'tp', swap)  4.18 us
    ppermute x3, starting transfers between devices, send_far(): lax.ppermute(part, 'tp', [(t, (t + 2 * d) % tp_count) for t in range(tp_c...  4.1 us
    pallas_call x1, Pallas kernels, on_device(): pl.pallas_call(functools.partial(away_kernel, inst_count, rounds), out_sh...  3.31 us
    ppermute x3, waiting for transfers between devices, on_device(): lax.ppermute(pack, 'inst', pairs[k])  3.1 us
    ppermute x3, waiting for transfers between devices, on_device(): lax.ppermute(answer, 'inst', pairs[k])  2.78 us
  transfers between devices with their start and end apart: 14, of which 8 were waited for; matrix products, arithmetic and copies ran while one was open for 0% of the time, Pallas kernels for 23%

profile of v4, /device:TPU:0, one launch (start us, length us, event | category | flops | bytes accessed | tf_op | source)
XLA Modules:
  0.0 45.8 jit_solution(9926649890435647993)
XLA Ops:
  0.0 0.0 copy-start
  0.0 0.0 copy-start.1
  0.0 5.3 %attend_first.1 = (bf16[128,512]{1,0:T(8,128)(2,1)S(1)}, bf16[32,8,512]{2,1,0:T(8,128)(2,1)S(1)}, bf16[32,8,256]{2,1,0:T(8,128)(2,1)S(1)}, bf16[8,768]{1,0:T(8,1...) custom-call(s32[4,12]{1,0:T(4,128)} %bitcast.11, s32[128]{0:T(128)} %lengths.5, s32[4,32]{1,0:T(4,128)} %bitcast.17, ...), custom_call_target="tpu_custom_call" | custom-call | flops 1 | bytes 1 | tf_op jit(solution)/shard_map/attend_first/pallas_call | solution.py:453
  5.3 0.0 copy-done
  5.3 0.7 %far_first.1 = (f32[128,2048]{1,0:T(8,128)S(1)}, bf16[128,2048]{1,0:T(8,128)(2,1)S(1)}) custom-call(bf16[128,512]{1,0:T(8,128)(2,1)S(1)} %get-tuple-element.30.attended.first, bf16[512,8192]{1,0:T(8,128)(2,1)S(1)} %copy-done), custom_call_target="tpu_custom_call" | custom-call | flops 1 | bytes 1 | tf_op jit(solution)/shard_map/far_first/pallas_call | solution.py:469
  6.1 0.5 %collective-permute-start = (bf16[128,2048]{1,0:T(8,128)(2,1)S(1)}, bf16[128,2048]{1,0:T(8,128)(2,1)S(1)}, u32[]{:S(2)}, u32[]{:S(2)}) collective-permute-start(bf16[128,2048]{1,0:T(8,128)(2,1)S(1)} %get-tuple-element.32), channel_id=1, source_target_pairs={{0,1},{1,0},{2,3},{3,2},{4,5},{5,4},{6,7},{7,6},{8,9},{9,8},{10,11... | collective-permute-start | bytes 1572872 | tf_op jit(solution)/shard_map/ppermute | solution.py:478
  6.6 1.5 %collective-permute-done = bf16[128,2048]{1,0:T(8,128)(2,1)S(1)} collective-permute-done((bf16[128,2048]{1,0:T(8,128)(2,1)S(1)}, bf16[128,2048]{1,0:T(8,128)(2,1)S(1)}, u32[]{:S(2)}, u32[]{:S(2)}) %collective-permute-start) | collective-permute-done | bytes 524320 | tf_op jit(solution)/shard_map/ppermute | solution.py:478
  8.1 0.1 add_convert_fusion.after.refs_3_
  8.3 3.0 %collective-permute-start.4 = (bf16[128,2048]{1,0:T(8,128)(2,1)S(1)}, bf16[128,2048]{1,0:T(8,128)(2,1)S(1)}, u32[]{:S(2)}, u32[]{:S(2)}) collective-permute-start(bf16[128,2048]{1,0:T(8,128)(2,1)S(1)} %add_convert_fusion.after.refs_3_), channel_id=1, source_target_pairs={{0,2},{1,3},{2,0},{3,1},{4,6},{5,7},{6,4},{7,5},{8,10},{9,11},{10,... | collective-permute-start | bytes 1572872 | tf_op jit(solution)/shard_map/ppermute | solution.py:421
  11.2 1.6 %collective-permute-start.1 = (bf16[8,768]{1,0:T(8,128)(2,1)S(1)}, bf16[8,768]{1,0:T(8,128)(2,1)S(1)}, u32[]{:S(2)}, u32[]{:S(2)}) collective-permute-start(bf16[8,768]{1,0:T(8,128)(2,1)S(1)} %get-tuple-element.38), channel_id=1, source_target_pairs={{0,4},{4,0},{8,12},{12,8},{1,5},{5,1},{9,13},{13,9},{2,6},{6,2},{1... | collective-permute-start | bytes 36872 | tf_op jit(solution)/shard_map/ppermute | solution.py:482
  12.8 2.6 %collective-permute-start.2 = (bf16[8,768]{1,0:T(8,128)(2,1)S(1)}, bf16[8,768]{1,0:T(8,128)(2,1)S(1)}, u32[]{:S(2)}, u32[]{:S(2)}) collective-permute-start(bf16[8,768]{1,0:T(8,128)(2,1)S(1)} %get-tuple-element.39), channel_id=1, source_target_pairs={{0,8},{4,12},{8,0},{12,4},{1,9},{5,13},{9,1},{13,5},{2,10},{6,14},... | collective-permute-start | bytes 36872 | tf_op jit(solution)/shard_map/ppermute | solution.py:482
  15.4 0.2 collective-permute-start.3
  15.6 0.0 copy-done.1
  15.6 2.2 %attend_second.1 = (bf16[96,512]{1,0:T(8,128)(2,1)S(1)}, bf16[1,8,512]{2,1,0:T(8,128)(2,1)S(1)}) custom-call(s32[4,12]{1,0:T(4,128)} %bitcast.12, s32[128]{0:T(128)} %lengths.5, s32[4,32]{1,0:T(4,128)} %bitcast.18, bf16[32,8,512]{2,1,0:T(8,128)(2,1)S(1)} %get-tuple-element.28.queries, bf16[32,8,256]{2,1,0:T(8,128)(2,1)S(1)} %get-tuple-element.29.new_tokens, ...), custom_call_target="tpu_custom_call" | custom-call | flops 1 | bytes 1 | tf_op jit(solution)/shard_map/attend_second/pallas_call | solution.py:484
  17.8 0.0 collective-permute-done.1.refs_0_
  17.8 0.0 collective-permute-done.2.refs_1_
  17.8 3.1 %collective-permute-done.3.refs_2_ = bf16[8,768]{1,0:T(8,128)(2,1)S(1)} collective-permute-done((bf16[8,768]{1,0:T(8,128)(2,1)S(1)}, bf16[8,768]{1,0:T(8,128)(2,1)S(1)}, u32[]{:S(2)}, u32[]{:S(2)}) %collective-permute-start.3) | collective-permute-done | bytes 12320 | tf_op jit(solution)/shard_map/ppermute | solution.py:482
  20.9 3.3 %attend_away.1 = (bf16[8,512]{1,0:T(8,128)(2,1)S(1)}, bf16[8,512]{1,0:T(8,128)(2,1)S(1)}, bf16[8,512]{1,0:T(8,128)(2,1)S(1)}, f32[96,2048]{1,0:T(8,128)S(1)}, bf16[96,2048]{1,0:T(8,128)(2,1)S(1)}) custom-call(s32[128]{0:T(128)} %lengths.5, s32[4,32]{1,0:T(4,128)} %bitcast.19, s32[4,12]{1,0:T(4,128)} %bitcast.13, bf16[128,128,256]{2,1,0:T(8,128)(2,1)} %bitcast.7, ...), custom_call_target="tpu_custom_call" | custom-call | flops 1 | bytes 1 | tf_op jit(solution)/shard_map/attend_away/pallas_call | solution.py:497
  24.2 0.1 collective-permute-start.5
  24.3 0.0 collective-permute-done.4.refs_1_.refs_2_
  24.3 1.7 %collective-permute-done.5 = bf16[96,2048]{1,0:T(8,128)(2,1)S(1)} collective-permute-done((bf16[96,2048]{1,0:T(8,128)(2,1)S(1)}, bf16[96,2048]{1,0:T(8,128)(2,1)S(1)}, u32[]{:S(2)}, u32[]{:S(2)}) %collective-permute-start.5) | collective-permute-done | bytes 393248 | tf_op jit(solution)/shard_map/ppermute | solution.py:507
  26.0 0.1 add_convert_fusion.1.after
  26.1 0.6 %collective-permute-start.9 = (bf16[96,2048]{1,0:T(8,128)(2,1)S(1)}, bf16[96,2048]{1,0:T(8,128)(2,1)S(1)}, u32[]{:S(2)}, u32[]{:S(2)}) collective-permute-start(bf16[96,2048]{1,0:T(8,128)(2,1)S(1)} %add_convert_fusion.1.after), channel_id=1, source_target_pairs={{0,2},{1,3},{2,0},{3,1},{4,6},{5,7},{6,4},{7,5},{8,10},{9,11},{10,... | collective-permute-start | bytes 1179656 | tf_op jit(solution)/shard_map/ppermute | solution.py:421
  26.7 0.3 collective-permute-start.6
  26.9 2.6 %collective-permute-start.7 = (bf16[8,512]{1,0:T(8,128)(2,1)S(1)}, bf16[8,512]{1,0:T(8,128)(2,1)S(1)}, u32[]{:S(2)}, u32[]{:S(2)}) collective-permute-start(bf16[8,512]{1,0:T(8,128)(2,1)S(1)} %get-tuple-element.45), channel_id=1, source_target_pairs={{0,8},{4,12},{8,0},{12,4},{1,9},{5,13},{9,1},{13,5},{2,10},{6,14},... | collective-permute-start | bytes 24584 | tf_op jit(solution)/shard_map/ppermute | solution.py:508
  29.5 1.5 %collective-permute-start.8 = (bf16[8,512]{1,0:T(8,128)(2,1)S(1)}, bf16[8,512]{1,0:T(8,128)(2,1)S(1)}, u32[]{:S(2)}, u32[]{:S(2)}) collective-permute-start(bf16[8,512]{1,0:T(8,128)(2,1)S(1)} %get-tuple-element.46), channel_id=1, source_target_pairs={{0,12},{4,8},{8,4},{12,0},{1,13},{5,9},{9,5},{13,1},{2,14},{6,10},... | collective-permute-start | bytes 24584 | tf_op jit(solution)/shard_map/ppermute | solution.py:508
  31.0 1.1 %own_columns.1 = (f32[224,2048]{1,0:T(8,128)S(1)}, bf16[224,1024]{1,0:T(8,128)(2,1)S(1)}, bf16[224,1024]{1,0:T(8,128)(2,1)S(1)}) custom-call(bf16[512,8192]{1,0:T(8,128)(2,1)S(1)} %copy-done, bf16[128,512]{1,0:T(8,128)(2,1)S(1)} %get-tuple-element.30.attended.first, bf16[96,512]{1,0:T(8,128)(2,1)S(1)} %get-tuple-element.34.second, ...), custom_call_target="tpu_custom_call" | custom-call | flops 1 | bytes 1 | tf_op jit(solution)/shard_map/own_columns/pallas_call | solution.py:515
  32.2 0.0 collective-permute-done.6.refs_0_
  32.2 0.0 collective-permute-done.7.refs_1_
  32.2 2.8 %collective-permute-done.8.refs_2_ = bf16[8,512]{1,0:T(8,128)(2,1)S(1)} collective-permute-done((bf16[8,512]{1,0:T(8,128)(2,1)S(1)}, bf16[8,512]{1,0:T(8,128)(2,1)S(1)}, u32[]{:S(2)}, u32[]{:S(2)}) %collective-permute-start.8) | collective-permute-done | bytes 8224 | tf_op jit(solution)/shard_map/ppermute | solution.py:508
  35.0 2.3 %last_rows.1 = (f32[64,2048]{1,0:T(8,128)S(1)}, bf16[64,2048]{1,0:T(8,128)(2,1)S(1)}) custom-call(s32[4,12]{1,0:T(4,128)} %bitcast.14, bf16[512,8192]{1,0:T(8,128)(2,1)S(1)} %copy-done, bf16[1,8,512]{2,1,0:T(8,128)(2,1)S(1)} %get-tuple-element.33.extra, f32[224,2048]{1,0:T(8,128)S(1)} %get-tuple-element.43.after.keep, ...), custom_call_target="tpu_custom_call" | custom-call | flops 1 | bytes 1 | tf_op jit(solution)/shard_map/last_rows/pallas_call | solution.py:530
  37.2 0.0 collective-permute-start.10
  37.2 0.5 %collective-permute-start.12 = (bf16[224,1024]{1,0:T(8,128)(2,1)S(1)}, bf16[224,1024]{1,0:T(8,128)(2,1)S(1)}, u32[]{:S(2)}, u32[]{:S(2)}) collective-permute-start(bf16[224,1024]{1,0:T(8,128)(2,1)S(1)} %get-tuple-element.49), channel_id=1, source_target_pairs={{0,1},{1,0},{2,3},{3,2},{4,5},{5,4},{6,7},{7,6},{8,9},{9,8},{10,11... | collective-permute-start | bytes 1376264 | tf_op jit(solution)/shard_map/ppermute | solution.py:528
  37.8 0.1 collective-permute-start.13
  37.8 0.0 collective-permute-done.9.refs_1_.refs_3_
  37.8 1.0 %collective-permute-done.10.mate = bf16[64,2048]{1,0:T(8,128)(2,1)S(1)} collective-permute-done((bf16[64,2048]{1,0:T(8,128)(2,1)S(1)}, bf16[64,2048]{1,0:T(8,128)(2,1)S(1)}, u32[]{:S(2)}, u32[]{:S(2)}) %collective-permute-start.10) | collective-permute-done | bytes 262176 | tf_op jit(solution)/shard_map/ppermute | solution.py:543
  38.8 0.6 %collective-permute-start.11 = (bf16[32,2048]{1,0:T(8,128)(2,1)S(1)}, bf16[32,2048]{1,0:T(8,128)(2,1)S(1)}, u32[]{:S(2)}, u32[]{:S(2)}) collective-permute-start(bf16[32,2048]{1,0:T(8,128)(2,1)S(1)} %fusion), channel_id=1, source_target_pairs={{0,2},{1,3},{2,0},{3,1},{4,6},{5,7},{6,4},{7,5},{8,10},{9,11},{10,... | collective-permute-start | bytes 393224 | tf_op jit(solution)/shard_map/ppermute | solution.py:421
  39.4 0.1 collective-permute-done.12.refs_0_
  39.4 0.7 %collective-permute-done.13.refs_1_ = bf16[224,1024]{1,0:T(8,128)(2,1)S(1)} collective-permute-done((bf16[224,1024]{1,0:T(8,128)(2,1)S(1)}, bf16[224,1024]{1,0:T(8,128)(2,1)S(1)}, u32[]{:S(2)}, u32[]{:S(2)}) %collective-permute-start.13) | collective-permute-done | bytes 458784 | tf_op jit(solution)/shard_map/ppermute | solution.py:528
  40.1 1.9 %sum_early.1.refs_1_ = bf16[32,8,2048]{2,1,0:T(8,128)(2,1)} custom-call(s32[4,12]{1,0:T(4,128)} %bitcast.15, f32[224,2048]{1,0:T(8,128)S(1)} %get-tuple-element.43.after.keep, bf16[224,1024]{1,0:T(8,128)(2,1)S(1)} %collective-permute-done.12.refs_0_, bf16[224,1024]{1,0:T(8,128)(2,1)S(1)} %collective-permute-done.13.refs_1_, ...), custom_call_target="tpu_custom_call" | custom-call | flops 1 | bytes 1 | tf_op jit(solution)/shard_map/sum_early/pallas_call | solution.py:550
  42.0 2.5 %collective-permute-done.11.refs_0_ = bf16[32,2048]{1,0:T(8,128)(2,1)S(1)} collective-permute-done((bf16[32,2048]{1,0:T(8,128)(2,1)S(1)}, bf16[32,2048]{1,0:T(8,128)(2,1)S(1)}, u32[]{:S(2)}, u32[]{:S(2)}) %collective-permute-start.11) | collective-permute-done | bytes 131104 | tf_op jit(solution)/shard_map/ppermute | solution.py:421
  44.4 1.4 %sum_last.1 = bf16[32,8,2048]{2,1,0:T(8,128)(2,1)} custom-call(s32[4,12]{1,0:T(4,128)} %bitcast.16, f32[64,2048]{1,0:T(8,128)S(1)} %hold.5.keep, bf16[64,2048]{1,0:T(8,128)(2,1)S(1)} %collective-permute-done.10.mate, bf16[32,2048]{1,0:T(8,128)(2,1)S(1)} %collective-permute-done.11.refs_0_, ...), custom_call_target="tpu_custom_call", output_to_operand_aliasing={{}: (4, {})} | custom-call | flops 1 | bytes 1 | tf_op jit(solution)/shard_map/sum_last/pallas_call | solution.py:565
  (4 shorter events, 0.0 us)
Async XLA Ops:
  0.0 5.3 %copy-start = (bf16[512,8192]{1,0:T(8,128)(2,1)S(1)}, bf16[512,8192]{1,0:T(8,128)(2,1)}, u32[]{:S(2)}) copy-start(bf16[512,8192]{1,0:T(8,128)(2,1)} %weight.7) | copy-start | bytes 25165828
  0.0 15.6 %copy-start.1 = (bf16[1,128,128,256]{3,2,1,0:T(8,128)(2,1)S(1)}, bf16[1,128,128,256]{3,2,1,0:T(8,128)(2,1)}, u32[]{:S(2)}) copy-start(bf16[1,128,128,256]{3,2,1,0:T(8,128)(2,1)} %param.9) | copy-start | bytes 25165828
  6.1 2.1 %collective-permute-start = (bf16[128,2048]{1,0:T(8,128)(2,1)S(1)}, bf16[128,2048]{1,0:T(8,128)(2,1)S(1)}, u32[]{:S(2)}, u32[]{:S(2)}) collective-permute-start(bf16[128,2048]{1,0:T(8,128)(2,1)S(1)} %get-tuple-element.32), channel_id=1, source_target_pairs={{0,1},{1,0},{2,3},{3,2},{4,5},{5,4},{6,7},{7,6},{8,9},{9,8},{10,11... | collective-permute-start | bytes 1572872 | tf_op jit(solution)/shard_map/ppermute | solution.py:478
  8.3 16.0 %collective-permute-start.4 = (bf16[128,2048]{1,0:T(8,128)(2,1)S(1)}, bf16[128,2048]{1,0:T(8,128)(2,1)S(1)}, u32[]{:S(2)}, u32[]{:S(2)}) collective-permute-start(bf16[128,2048]{1,0:T(8,128)(2,1)S(1)} %add_convert_fusion.after.refs_3_), channel_id=1, source_target_pairs={{0,2},{1,3},{2,0},{3,1},{4,6},{5,7},{6,4},{7,5},{8,10},{9,11},{10,... | collective-permute-start | bytes 1572872 | tf_op jit(solution)/shard_map/ppermute | solution.py:421
  11.2 6.6 %collective-permute-start.1 = (bf16[8,768]{1,0:T(8,128)(2,1)S(1)}, bf16[8,768]{1,0:T(8,128)(2,1)S(1)}, u32[]{:S(2)}, u32[]{:S(2)}) collective-permute-start(bf16[8,768]{1,0:T(8,128)(2,1)S(1)} %get-tuple-element.38), channel_id=1, source_target_pairs={{0,4},{4,0},{8,12},{12,8},{1,5},{5,1},{9,13},{13,9},{2,6},{6,2},{1... | collective-permute-start | bytes 36872 | tf_op jit(solution)/shard_map/ppermute | solution.py:482
  12.8 5.0 %collective-permute-start.2 = (bf16[8,768]{1,0:T(8,128)(2,1)S(1)}, bf16[8,768]{1,0:T(8,128)(2,1)S(1)}, u32[]{:S(2)}, u32[]{:S(2)}) collective-permute-start(bf16[8,768]{1,0:T(8,128)(2,1)S(1)} %get-tuple-element.39), channel_id=1, source_target_pairs={{0,8},{4,12},{8,0},{12,4},{1,9},{5,13},{9,1},{13,5},{2,10},{6,14},... | collective-permute-start | bytes 36872 | tf_op jit(solution)/shard_map/ppermute | solution.py:482
  15.4 5.5 %collective-permute-start.3 = (bf16[8,768]{1,0:T(8,128)(2,1)S(1)}, bf16[8,768]{1,0:T(8,128)(2,1)S(1)}, u32[]{:S(2)}, u32[]{:S(2)}) collective-permute-start(bf16[8,768]{1,0:T(8,128)(2,1)S(1)} %get-tuple-element.40), channel_id=1, source_target_pairs={{0,12},{4,8},{8,4},{12,0},{1,13},{5,9},{9,5},{13,1},{2,14},{6,10},... | collective-permute-start | bytes 36872 | tf_op jit(solution)/shard_map/ppermute | solution.py:482
  24.2 1.8 %collective-permute-start.5 = (bf16[96,2048]{1,0:T(8,128)(2,1)S(1)}, bf16[96,2048]{1,0:T(8,128)(2,1)S(1)}, u32[]{:S(2)}, u32[]{:S(2)}) collective-permute-start(bf16[96,2048]{1,0:T(8,128)(2,1)S(1)} %get-tuple-element.42), channel_id=1, source_target_pairs={{0,1},{1,0},{2,3},{3,2},{4,5},{5,4},{6,7},{7,6},{8,9},{9,8},{10,11... | collective-permute-start | bytes 1179656 | tf_op jit(solution)/shard_map/ppermute | solution.py:507
  26.1 11.7 %collective-permute-start.9 = (bf16[96,2048]{1,0:T(8,128)(2,1)S(1)}, bf16[96,2048]{1,0:T(8,128)(2,1)S(1)}, u32[]{:S(2)}, u32[]{:S(2)}) collective-permute-start(bf16[96,2048]{1,0:T(8,128)(2,1)S(1)} %add_convert_fusion.1.after), channel_id=1, source_target_pairs={{0,2},{1,3},{2,0},{3,1},{4,6},{5,7},{6,4},{7,5},{8,10},{9,11},{10,... | collective-permute-start | bytes 1179656 | tf_op jit(solution)/shard_map/ppermute | solution.py:421
  26.7 5.5 %collective-permute-start.6 = (bf16[8,512]{1,0:T(8,128)(2,1)S(1)}, bf16[8,512]{1,0:T(8,128)(2,1)S(1)}, u32[]{:S(2)}, u32[]{:S(2)}) collective-permute-start(bf16[8,512]{1,0:T(8,128)(2,1)S(1)} %get-tuple-element.44), channel_id=1, source_target_pairs={{0,4},{4,0},{8,12},{12,8},{1,5},{5,1},{9,13},{13,9},{2,6},{6,2},{1... | collective-permute-start | bytes 24584 | tf_op jit(solution)/shard_map/ppermute | solution.py:508
  26.9 5.3 %collective-permute-start.7 = (bf16[8,512]{1,0:T(8,128)(2,1)S(1)}, bf16[8,512]{1,0:T(8,128)(2,1)S(1)}, u32[]{:S(2)}, u32[]{:S(2)}) collective-permute-start(bf16[8,512]{1,0:T(8,128)(2,1)S(1)} %get-tuple-element.45), channel_id=1, source_target_pairs={{0,8},{4,12},{8,0},{12,4},{1,9},{5,13},{9,1},{13,5},{2,10},{6,14},... | collective-permute-start | bytes 24584 | tf_op jit(solution)/shard_map/ppermute | solution.py:508
  29.5 5.4 %collective-permute-start.8 = (bf16[8,512]{1,0:T(8,128)(2,1)S(1)}, bf16[8,512]{1,0:T(8,128)(2,1)S(1)}, u32[]{:S(2)}, u32[]{:S(2)}) collective-permute-start(bf16[8,512]{1,0:T(8,128)(2,1)S(1)} %get-tuple-element.46), channel_id=1, source_target_pairs={{0,12},{4,8},{8,4},{12,0},{1,13},{5,9},{9,5},{13,1},{2,14},{6,10},... | collective-permute-start | bytes 24584 | tf_op jit(solution)/shard_map/ppermute | solution.py:508
  37.2 1.6 %collective-permute-start.10 = (bf16[64,2048]{1,0:T(8,128)(2,1)S(1)}, bf16[64,2048]{1,0:T(8,128)(2,1)S(1)}, u32[]{:S(2)}, u32[]{:S(2)}) collective-permute-start(bf16[64,2048]{1,0:T(8,128)(2,1)S(1)} %get-tuple-element.48), channel_id=1, source_target_pairs={{0,1},{1,0},{2,3},{3,2},{4,5},{5,4},{6,7},{7,6},{8,9},{9,8},{10,11... | collective-permute-start | bytes 786440 | tf_op jit(solution)/shard_map/ppermute | solution.py:543
  37.2 2.2 %collective-permute-start.12 = (bf16[224,1024]{1,0:T(8,128)(2,1)S(1)}, bf16[224,1024]{1,0:T(8,128)(2,1)S(1)}, u32[]{:S(2)}, u32[]{:S(2)}) collective-permute-start(bf16[224,1024]{1,0:T(8,128)(2,1)S(1)} %get-tuple-element.49), channel_id=1, source_target_pairs={{0,1},{1,0},{2,3},{3,2},{4,5},{5,4},{6,7},{7,6},{8,9},{9,8},{10,11... | collective-permute-start | bytes 1376264 | tf_op jit(solution)/shard_map/ppermute | solution.py:528
  37.8 2.3 %collective-permute-start.13 = (bf16[224,1024]{1,0:T(8,128)(2,1)S(1)}, bf16[224,1024]{1,0:T(8,128)(2,1)S(1)}, u32[]{:S(2)}, u32[]{:S(2)}) collective-permute-start(bf16[224,1024]{1,0:T(8,128)(2,1)S(1)} %get-tuple-element.50), channel_id=1, source_target_pairs={{0,1},{1,0},{2,3},{3,2},{4,5},{5,4},{6,7},{7,6},{8,9},{9,8},{10,11... | collective-permute-start | bytes 1376264 | tf_op jit(solution)/shard_map/ppermute | solution.py:528
  38.8 5.6 %collective-permute-start.11 = (bf16[32,2048]{1,0:T(8,128)(2,1)S(1)}, bf16[32,2048]{1,0:T(8,128)(2,1)S(1)}, u32[]{:S(2)}, u32[]{:S(2)}) collective-permute-start(bf16[32,2048]{1,0:T(8,128)(2,1)S(1)} %fusion), channel_id=1, source_target_pairs={{0,2},{1,3},{2,0},{3,1},{4,6},{5,7},{6,4},{7,5},{8,10},{9,11},{10,... | collective-permute-start | bytes 393224 | tf_op jit(solution)/shard_map/ppermute | solution.py:421

commit v5 on v4

--- a/solution.py
+++ b/solution.py
@@ -289,7 +289,7 @@
 
 
 def last_rows_kernel(inst_count, rounds, migration, weight, extra, after, *refs):
-    answers, (keep, send, rows) = refs[:-3], refs[-3:]
+    answers, (rows, keep, send) = refs[:-3], refs[-3:]
     me = lax.axis_index("inst")
     _, sources = arrivals_of(migration, inst_count)
     last = [extra[i].astype(jnp.float32) for i in range(extra.shape[0])]
@@ -300,14 +300,15 @@
             row = jnp.where(source == peer_of(me, k, inst_count), answer, row)
         last.append(row)
     store_rows(last, rows)
+    project_far(rows, weight, keep, send, stacked=True)
+
+
+def near_rows_kernel(weight, rows, keep, send):
     core = lax.rem(lax.axis_index("tp"), 2)
-    chip = lax.axis_index("tp") // 2
-    chips = lax.axis_size("tp") // 2
+    pair = lax.axis_index("tp") // 2 * 2
     columns = keep.shape[1]
     for target, side in ((send, 1 - core), (keep, core)):
-        for d in range(1, chips + 1):
-            first = (2 * lax.rem(chip + d, chips) + side) * columns
-            project(rows, weight, first, columns, target, (d - 1) * rows.shape[0])
+        project(rows, weight, (pair + side) * columns, columns, target)
 
 
 def own_kernel(weight, first, second, after, keep, *refs):
@@ -527,22 +528,35 @@
     )(weight, first, second, summed)
     early_mates = [lax.ppermute(early_send, "tp", swap) for early_send in early_sends]
 
-    keep, send = pl.pallas_call(
+    last, keep, send = pl.pallas_call(
         functools.partial(last_rows_kernel, inst_count, rounds),
         out_shape=[
-            pltpu.VMEM((last_rows * chips, columns), f32),
-            pltpu.VMEM((last_rows * chips, columns), bf16),
+            rows_shape(last_count),
+            pltpu.VMEM((last_rows * (chips - 1), columns), f32),
+            pltpu.VMEM((last_rows * (chips - 1), columns), bf16),
         ],
         in_specs=[SMEM] + [VMEM] * 2 + [ANY] + [VMEM] * len(rounds),
-        out_specs=[VMEM] * 2,
-        scratch_shapes=[pltpu.VMEM((last_rows, width), bf16)],
+        out_specs=[VMEM] * 3,
         compiler_params=limit,
         cost_estimate=light,
         name="last_rows",
     )(migration, weight, in_vmem(extra), early_keep, *answers)
     mate = lax.ppermute(send, "tp", swap)
+    near_keep, near_send = pl.pallas_call(
+        near_rows_kernel,
+        out_shape=[
+            pltpu.VMEM((last_rows, columns), f32),
+            pltpu.VMEM((last_rows, columns), bf16),
+        ],
+        in_specs=[VMEM] * 2,
+        out_specs=[VMEM] * 2,
+        compiler_params=limit,
+        cost_estimate=light,
+        name="near_rows",
+    )(weight, in_vmem(last))
+    near_mate = lax.ppermute(near_send, "tp", swap)
     (keep,) = hold([keep], arrived_second)
-    summed = (keep[:-last_rows] + mate[:-last_rows].astype(f32)).astype(bf16)
+    summed = (keep + mate.astype(f32)).astype(bf16)
     arrived_last = send_far([summed[d * last_rows : (d + 1) * last_rows] for d in range(chips - 1)])
 
     early = slot_count - last_count
@@ -575,7 +589,7 @@
         compiler_params=limit,
         cost_estimate=light,
         name="sum_last",
-    )(migration, in_vmem(keep), mate, *arrived_last, out)
+    )(migration, in_vmem(near_keep), near_mate, *arrived_last, out)
     return out.reshape(row_count, columns)
 
 

time: 46.1 us -> 45.7 us (level)
  waiting for transfers between devices: 13.2 us -> 12.2 us
  starting transfers between devices: 14 us -> 14.5 us
    ppermute x3, waiting for transfers between devices: 4.18 us -> 3.23 us  [on_device(): mate = lax.ppermute(send, 'tp', swap)]
    pallas_call x0 -> x1, Pallas kernels: none -> 0.81 us  [on_device(): pl.pallas_call(near_rows_kernel, out_shape=[pltpu.VMEM((last_rows, column...]
    pallas_call x1, Pallas kernels: 2.26 us -> 1.55 us  [on_device(): pl.pallas_call(functools.partial(last_rows_kernel, inst_count, rounds), o...]
    ppermute x2, waiting for transfers between devices: 0.71 us -> 0.19 us  [on_device(): lax.ppermute(early_send, 'tp', swap)]
    ppermute x0 -> x1, starting transfers between devices: none -> 0.47 us  [on_device(): near_mate = lax.ppermute(near_send, 'tp', swap)]
  transfers between devices with their start and end apart: 14 -> 15, of which waited for: 8 -> 6; matrix products, arithmetic and copies ran while one was open for 0% -> 0% of each run, Pallas kernels for 23% -> 24%
where the time goes in v5:
time: 45.7 us; the launch traced here: 45.4 us
  Pallas kernels  18.3 us (40%)
  starting transfers between devices  14.5 us (32%)
  waiting for transfers between devices  12.2 us (27%)
    pallas_call x1, Pallas kernels, on_device(): pl.pallas_call(functools.partial(first_kernel, inst_count, rounds), out_s...  5.31 us
    ppermute x3, starting transfers between devices, on_device(): lax.ppermute(answer, 'inst', pairs[k])  4.39 us
    ppermute x3, starting transfers between devices, on_device(): lax.ppermute(pack, 'inst', pairs[k])  4.39 us
    ppermute x3, starting transfers between devices, send_far(): lax.ppermute(part, 'tp', [(t, (t + 2 * d) % tp_count) for t in range(tp_c...  4.1 us
    pallas_call x1, Pallas kernels, on_device(): pl.pallas_call(functools.partial(away_kernel, inst_count, rounds), out_sh...  3.31 us
    ppermute x3, waiting for transfers between devices, on_device(): mate = lax.ppermute(send, 'tp', swap)  3.23 us
    ppermute x3, waiting for transfers between devices, on_device(): lax.ppermute(pack, 'inst', pairs[k])  3.1 us
    ppermute x3, waiting for transfers between devices, send_far(): lax.ppermute(part, 'tp', [(t, (t + 2 * d) % tp_count) for t in range(tp_c...  2.89 us
  transfers between devices with their start and end apart: 15, of which 6 were waited for; matrix products, arithmetic and copies ran while one was open for 0% of the time, Pallas kernels for 24%

profile of v5, /device:TPU:0, one launch (start us, length us, event | category | flops | bytes accessed | tf_op | source)
XLA Modules:
  0.0 45.4 jit_solution(14216189652408961448)
XLA Ops:
  0.0 0.0 copy-start
  0.0 0.0 copy-start.1
  0.0 5.3 %attend_first.1 = (bf16[128,512]{1,0:T(8,128)(2,1)S(1)}, bf16[32,8,512]{2,1,0:T(8,128)(2,1)S(1)}, bf16[32,8,256]{2,1,0:T(8,128)(2,1)S(1)}, bf16[8,768]{1,0:T(8,1...) custom-call(s32[4,12]{1,0:T(4,128)} %bitcast.11, s32[128]{0:T(128)} %lengths.5, s32[4,32]{1,0:T(4,128)} %bitcast.17, ...), custom_call_target="tpu_custom_call" | custom-call | flops 1 | bytes 1 | tf_op jit(solution)/shard_map/attend_first/pallas_call | solution.py:454
  5.3 0.0 copy-done
  5.3 0.7 %far_first.1 = (f32[128,2048]{1,0:T(8,128)S(1)}, bf16[128,2048]{1,0:T(8,128)(2,1)S(1)}) custom-call(bf16[128,512]{1,0:T(8,128)(2,1)S(1)} %get-tuple-element.33.attended.first, bf16[512,8192]{1,0:T(8,128)(2,1)S(1)} %copy-done), custom_call_target="tpu_custom_call" | custom-call | flops 1 | bytes 1 | tf_op jit(solution)/shard_map/far_first/pallas_call | solution.py:470
  6.1 0.5 %collective-permute-start = (bf16[128,2048]{1,0:T(8,128)(2,1)S(1)}, bf16[128,2048]{1,0:T(8,128)(2,1)S(1)}, u32[]{:S(2)}, u32[]{:S(2)}) collective-permute-start(bf16[128,2048]{1,0:T(8,128)(2,1)S(1)} %get-tuple-element.35), channel_id=1, source_target_pairs={{0,1},{1,0},{2,3},{3,2},{4,5},{5,4},{6,7},{7,6},{8,9},{9,8},{10,11... | collective-permute-start | bytes 1572872 | tf_op jit(solution)/shard_map/ppermute | solution.py:479
  6.6 1.5 %collective-permute-done = bf16[128,2048]{1,0:T(8,128)(2,1)S(1)} collective-permute-done((bf16[128,2048]{1,0:T(8,128)(2,1)S(1)}, bf16[128,2048]{1,0:T(8,128)(2,1)S(1)}, u32[]{:S(2)}, u32[]{:S(2)}) %collective-permute-start) | collective-permute-done | bytes 524320 | tf_op jit(solution)/shard_map/ppermute | solution.py:479
  8.1 0.1 add_convert_fusion.after.refs_3_
  8.3 3.0 %collective-permute-start.4 = (bf16[128,2048]{1,0:T(8,128)(2,1)S(1)}, bf16[128,2048]{1,0:T(8,128)(2,1)S(1)}, u32[]{:S(2)}, u32[]{:S(2)}) collective-permute-start(bf16[128,2048]{1,0:T(8,128)(2,1)S(1)} %add_convert_fusion.after.refs_3_), channel_id=1, source_target_pairs={{0,2},{1,3},{2,0},{3,1},{4,6},{5,7},{6,4},{7,5},{8,10},{9,11},{10,... | collective-permute-start | bytes 1572872 | tf_op jit(solution)/shard_map/ppermute | solution.py:422
  11.2 1.6 %collective-permute-start.1 = (bf16[8,768]{1,0:T(8,128)(2,1)S(1)}, bf16[8,768]{1,0:T(8,128)(2,1)S(1)}, u32[]{:S(2)}, u32[]{:S(2)}) collective-permute-start(bf16[8,768]{1,0:T(8,128)(2,1)S(1)} %get-tuple-element.41), channel_id=1, source_target_pairs={{0,4},{4,0},{8,12},{12,8},{1,5},{5,1},{9,13},{13,9},{2,6},{6,2},{1... | collective-permute-start | bytes 36872 | tf_op jit(solution)/shard_map/ppermute | solution.py:483
  12.8 2.6 %collective-permute-start.2 = (bf16[8,768]{1,0:T(8,128)(2,1)S(1)}, bf16[8,768]{1,0:T(8,128)(2,1)S(1)}, u32[]{:S(2)}, u32[]{:S(2)}) collective-permute-start(bf16[8,768]{1,0:T(8,128)(2,1)S(1)} %get-tuple-element.42), channel_id=1, source_target_pairs={{0,8},{4,12},{8,0},{12,4},{1,9},{5,13},{9,1},{13,5},{2,10},{6,14},... | collective-permute-start | bytes 36872 | tf_op jit(solution)/shard_map/ppermute | solution.py:483
  15.4 0.2 collective-permute-start.3
  15.6 0.0 copy-done.1
  15.6 2.2 %attend_second.1 = (bf16[96,512]{1,0:T(8,128)(2,1)S(1)}, bf16[1,8,512]{2,1,0:T(8,128)(2,1)S(1)}) custom-call(s32[4,12]{1,0:T(4,128)} %bitcast.12, s32[128]{0:T(128)} %lengths.5, s32[4,32]{1,0:T(4,128)} %bitcast.18, bf16[32,8,512]{2,1,0:T(8,128)(2,1)S(1)} %get-tuple-element.31.queries, bf16[32,8,256]{2,1,0:T(8,128)(2,1)S(1)} %get-tuple-element.32.new_tokens, ...), custom_call_target="tpu_custom_call" | custom-call | flops 1 | bytes 1 | tf_op jit(solution)/shard_map/attend_second/pallas_call | solution.py:485
  17.8 0.0 collective-permute-done.1.refs_0_
  17.8 0.0 collective-permute-done.2.refs_1_
  17.8 3.1 %collective-permute-done.3.refs_2_ = bf16[8,768]{1,0:T(8,128)(2,1)S(1)} collective-permute-done((bf16[8,768]{1,0:T(8,128)(2,1)S(1)}, bf16[8,768]{1,0:T(8,128)(2,1)S(1)}, u32[]{:S(2)}, u32[]{:S(2)}) %collective-permute-start.3) | collective-permute-done | bytes 12320 | tf_op jit(solution)/shard_map/ppermute | solution.py:483
  20.9 3.3 %attend_away.1 = (bf16[8,512]{1,0:T(8,128)(2,1)S(1)}, bf16[8,512]{1,0:T(8,128)(2,1)S(1)}, bf16[8,512]{1,0:T(8,128)(2,1)S(1)}, f32[96,2048]{1,0:T(8,128)S(1)}, bf16[96,2048]{1,0:T(8,128)(2,1)S(1)}) custom-call(s32[128]{0:T(128)} %lengths.5, s32[4,32]{1,0:T(4,128)} %bitcast.19, s32[4,12]{1,0:T(4,128)} %bitcast.13, bf16[128,128,256]{2,1,0:T(8,128)(2,1)} %bitcast.7, ...), custom_call_target="tpu_custom_call" | custom-call | flops 1 | bytes 1 | tf_op jit(solution)/shard_map/attend_away/pallas_call | solution.py:498
  24.2 0.1 collective-permute-start.5
  24.3 0.0 collective-permute-done.4.refs_1_.refs_2_
  24.3 1.7 %collective-permute-done.5 = bf16[96,2048]{1,0:T(8,128)(2,1)S(1)} collective-permute-done((bf16[96,2048]{1,0:T(8,128)(2,1)S(1)}, bf16[96,2048]{1,0:T(8,128)(2,1)S(1)}, u32[]{:S(2)}, u32[]{:S(2)}) %collective-permute-start.5) | collective-permute-done | bytes 393248 | tf_op jit(solution)/shard_map/ppermute | solution.py:508
  26.0 0.1 add_convert_fusion.1.after
  26.1 0.6 %collective-permute-start.10 = (bf16[96,2048]{1,0:T(8,128)(2,1)S(1)}, bf16[96,2048]{1,0:T(8,128)(2,1)S(1)}, u32[]{:S(2)}, u32[]{:S(2)}) collective-permute-start(bf16[96,2048]{1,0:T(8,128)(2,1)S(1)} %add_convert_fusion.1.after), channel_id=1, source_target_pairs={{0,2},{1,3},{2,0},{3,1},{4,6},{5,7},{6,4},{7,5},{8,10},{9,11},{10,... | collective-permute-start | bytes 1179656 | tf_op jit(solution)/shard_map/ppermute | solution.py:422
  26.7 0.3 collective-permute-start.6
  26.9 2.6 %collective-permute-start.7 = (bf16[8,512]{1,0:T(8,128)(2,1)S(1)}, bf16[8,512]{1,0:T(8,128)(2,1)S(1)}, u32[]{:S(2)}, u32[]{:S(2)}) collective-permute-start(bf16[8,512]{1,0:T(8,128)(2,1)S(1)} %get-tuple-element.48), channel_id=1, source_target_pairs={{0,8},{4,12},{8,0},{12,4},{1,9},{5,13},{9,1},{13,5},{2,10},{6,14},... | collective-permute-start | bytes 24584 | tf_op jit(solution)/shard_map/ppermute | solution.py:509
  29.5 1.5 %collective-permute-start.8 = (bf16[8,512]{1,0:T(8,128)(2,1)S(1)}, bf16[8,512]{1,0:T(8,128)(2,1)S(1)}, u32[]{:S(2)}, u32[]{:S(2)}) collective-permute-start(bf16[8,512]{1,0:T(8,128)(2,1)S(1)} %get-tuple-element.49), channel_id=1, source_target_pairs={{0,12},{4,8},{8,4},{12,0},{1,13},{5,9},{9,5},{13,1},{2,14},{6,10},... | collective-permute-start | bytes 24584 | tf_op jit(solution)/shard_map/ppermute | solution.py:509
  31.0 1.1 %own_columns.1 = (f32[224,2048]{1,0:T(8,128)S(1)}, bf16[224,1024]{1,0:T(8,128)(2,1)S(1)}, bf16[224,1024]{1,0:T(8,128)(2,1)S(1)}) custom-call(bf16[512,8192]{1,0:T(8,128)(2,1)S(1)} %copy-done, bf16[128,512]{1,0:T(8,128)(2,1)S(1)} %get-tuple-element.33.attended.first, bf16[96,512]{1,0:T(8,128)(2,1)S(1)} %get-tuple-element.37.second, ...), custom_call_target="tpu_custom_call" | custom-call | flops 1 | bytes 1 | tf_op jit(solution)/shard_map/own_columns/pallas_call | solution.py:516
  32.2 0.0 collective-permute-done.6.refs_0_
  32.2 0.0 collective-permute-done.7.refs_1_
  32.2 2.8 %collective-permute-done.8.refs_2_ = bf16[8,512]{1,0:T(8,128)(2,1)S(1)} collective-permute-done((bf16[8,512]{1,0:T(8,128)(2,1)S(1)}, bf16[8,512]{1,0:T(8,128)(2,1)S(1)}, u32[]{:S(2)}, u32[]{:S(2)}) %collective-permute-start.8) | collective-permute-done | bytes 8224 | tf_op jit(solution)/shard_map/ppermute | solution.py:509
  35.0 1.5 %last_rows.1 = (bf16[32,512]{1,0:T(8,128)(2,1)S(1)}, f32[32,2048]{1,0:T(8,128)S(1)}, bf16[32,2048]{1,0:T(8,128)(2,1)S(1)}) custom-call(s32[4,12]{1,0:T(4,128)} %bitcast.14, bf16[512,8192]{1,0:T(8,128)(2,1)S(1)} %copy-done, bf16[1,8,512]{2,1,0:T(8,128)(2,1)S(1)} %get-tuple-element.36.extra, f32[224,2048]{1,0:T(8,128)S(1)} %get-tuple-element.46.after.keep, ...), custom_call_target="tpu_custom_call" | custom-call | flops 1 | bytes 1 | tf_op jit(solution)/shard_map/last_rows/pallas_call | solution.py:531
  36.5 0.0 collective-permute-start.11
  36.5 0.5 %collective-permute-start.13 = (bf16[224,1024]{1,0:T(8,128)(2,1)S(1)}, bf16[224,1024]{1,0:T(8,128)(2,1)S(1)}, u32[]{:S(2)}, u32[]{:S(2)}) collective-permute-start(bf16[224,1024]{1,0:T(8,128)(2,1)S(1)} %get-tuple-element.55), channel_id=1, source_target_pairs={{0,1},{1,0},{2,3},{3,2},{4,5},{5,4},{6,7},{7,6},{8,9},{9,8},{10,11... | collective-permute-start | bytes 1376264 | tf_op jit(solution)/shard_map/ppermute | solution.py:529
  37.0 0.1 collective-permute-start.14
  37.1 0.8 %near_rows.1 = (f32[32,2048]{1,0:T(8,128)S(1)}, bf16[32,2048]{1,0:T(8,128)(2,1)S(1)}) custom-call(bf16[512,8192]{1,0:T(8,128)(2,1)S(1)} %copy-done, bf16[32,512]{1,0:T(8,128)(2,1)S(1)} %get-tuple-element.50.rows), custom_call_target="tpu_custom_call" | custom-call | flops 1 | bytes 1 | tf_op jit(solution)/shard_map/near_rows/pallas_call | solution.py:545
  37.9 0.5 %collective-permute-start.9 = (bf16[32,2048]{1,0:T(8,128)(2,1)S(1)}, bf16[32,2048]{1,0:T(8,128)(2,1)S(1)}, u32[]{:S(2)}, u32[]{:S(2)}) collective-permute-start(bf16[32,2048]{1,0:T(8,128)(2,1)S(1)} %get-tuple-element.52), channel_id=1, source_target_pairs={{0,1},{1,0},{2,3},{3,2},{4,5},{5,4},{6,7},{7,6},{8,9},{9,8},{10,11... | collective-permute-start | bytes 393224 | tf_op jit(solution)/shard_map/ppermute | solution.py:557
  38.4 0.0 collective-permute-done.10.refs_1_.refs_3_
  38.4 0.0 collective-permute-done.11
  38.4 0.6 %collective-permute-start.12 = (bf16[32,2048]{1,0:T(8,128)(2,1)S(1)}, bf16[32,2048]{1,0:T(8,128)(2,1)S(1)}, u32[]{:S(2)}, u32[]{:S(2)}) collective-permute-start(bf16[32,2048]{1,0:T(8,128)(2,1)S(1)} %add_convert_fusion.2), channel_id=1, source_target_pairs={{0,2},{1,3},{2,0},{3,1},{4,6},{5,7},{6,4},{7,5},{8,10},{9,11},{10,... | collective-permute-start | bytes 393224 | tf_op jit(solution)/shard_map/ppermute | solution.py:422
  39.0 0.0 collective-permute-done.13.refs_0_
  39.0 0.2 collective-permute-done.14.refs_1_
  39.2 1.9 %sum_early.1.refs_1_ = bf16[32,8,2048]{2,1,0:T(8,128)(2,1)} custom-call(s32[4,12]{1,0:T(4,128)} %bitcast.15, f32[224,2048]{1,0:T(8,128)S(1)} %get-tuple-element.46.after.keep, bf16[224,1024]{1,0:T(8,128)(2,1)S(1)} %collective-permute-done.13.refs_0_, bf16[224,1024]{1,0:T(8,128)(2,1)S(1)} %collective-permute-done.14.refs_1_, ...), custom_call_target="tpu_custom_call" | custom-call | flops 1 | bytes 1 | tf_op jit(solution)/shard_map/sum_early/pallas_call | solution.py:564
  41.1 0.0 collective-permute-done.9.mate
  41.1 2.9 %collective-permute-done.12.refs_0_ = bf16[32,2048]{1,0:T(8,128)(2,1)S(1)} collective-permute-done((bf16[32,2048]{1,0:T(8,128)(2,1)S(1)}, bf16[32,2048]{1,0:T(8,128)(2,1)S(1)}, u32[]{:S(2)}, u32[]{:S(2)}) %collective-permute-start.12) | collective-permute-done | bytes 131104 | tf_op jit(solution)/shard_map/ppermute | solution.py:422
  44.0 1.4 %sum_last.1 = bf16[32,8,2048]{2,1,0:T(8,128)(2,1)} custom-call(s32[4,12]{1,0:T(4,128)} %bitcast.16, f32[32,2048]{1,0:T(8,128)S(1)} %get-tuple-element.51.keep, bf16[32,2048]{1,0:T(8,128)(2,1)S(1)} %collective-permute-done.9.mate, bf16[32,2048]{1,0:T(8,128)(2,1)S(1)} %collective-permute-done.12.refs_0_, ...), custom_call_target="tpu_custom_call", output_to_operand_aliasing={{}: (4, {})} | custom-call | flops 1 | bytes 1 | tf_op jit(solution)/shard_map/sum_last/pallas_call | solution.py:579
  (4 shorter events, 0.0 us)
Async XLA Ops:
  0.0 5.3 %copy-start = (bf16[512,8192]{1,0:T(8,128)(2,1)S(1)}, bf16[512,8192]{1,0:T(8,128)(2,1)}, u32[]{:S(2)}) copy-start(bf16[512,8192]{1,0:T(8,128)(2,1)} %weight.9) | copy-start | bytes 25165828
  0.0 15.6 %copy-start.1 = (bf16[1,128,128,256]{3,2,1,0:T(8,128)(2,1)S(1)}, bf16[1,128,128,256]{3,2,1,0:T(8,128)(2,1)}, u32[]{:S(2)}) copy-start(bf16[1,128,128,256]{3,2,1,0:T(8,128)(2,1)} %param.9) | copy-start | bytes 25165828
  6.1 2.1 %collective-permute-start = (bf16[128,2048]{1,0:T(8,128)(2,1)S(1)}, bf16[128,2048]{1,0:T(8,128)(2,1)S(1)}, u32[]{:S(2)}, u32[]{:S(2)}) collective-permute-start(bf16[128,2048]{1,0:T(8,128)(2,1)S(1)} %get-tuple-element.35), channel_id=1, source_target_pairs={{0,1},{1,0},{2,3},{3,2},{4,5},{5,4},{6,7},{7,6},{8,9},{9,8},{10,11... | collective-permute-start | bytes 1572872 | tf_op jit(solution)/shard_map/ppermute | solution.py:479
  8.3 16.0 %collective-permute-start.4 = (bf16[128,2048]{1,0:T(8,128)(2,1)S(1)}, bf16[128,2048]{1,0:T(8,128)(2,1)S(1)}, u32[]{:S(2)}, u32[]{:S(2)}) collective-permute-start(bf16[128,2048]{1,0:T(8,128)(2,1)S(1)} %add_convert_fusion.after.refs_3_), channel_id=1, source_target_pairs={{0,2},{1,3},{2,0},{3,1},{4,6},{5,7},{6,4},{7,5},{8,10},{9,11},{10,... | collective-permute-start | bytes 1572872 | tf_op jit(solution)/shard_map/ppermute | solution.py:422
  11.2 6.6 %collective-permute-start.1 = (bf16[8,768]{1,0:T(8,128)(2,1)S(1)}, bf16[8,768]{1,0:T(8,128)(2,1)S(1)}, u32[]{:S(2)}, u32[]{:S(2)}) collective-permute-start(bf16[8,768]{1,0:T(8,128)(2,1)S(1)} %get-tuple-element.41), channel_id=1, source_target_pairs={{0,4},{4,0},{8,12},{12,8},{1,5},{5,1},{9,13},{13,9},{2,6},{6,2},{1... | collective-permute-start | bytes 36872 | tf_op jit(solution)/shard_map/ppermute | solution.py:483
  12.8 5.0 %collective-permute-start.2 = (bf16[8,768]{1,0:T(8,128)(2,1)S(1)}, bf16[8,768]{1,0:T(8,128)(2,1)S(1)}, u32[]{:S(2)}, u32[]{:S(2)}) collective-permute-start(bf16[8,768]{1,0:T(8,128)(2,1)S(1)} %get-tuple-element.42), channel_id=1, source_target_pairs={{0,8},{4,12},{8,0},{12,4},{1,9},{5,13},{9,1},{13,5},{2,10},{6,14},... | collective-permute-start | bytes 36872 | tf_op jit(solution)/shard_map/ppermute | solution.py:483
  15.4 5.5 %collective-permute-start.3 = (bf16[8,768]{1,0:T(8,128)(2,1)S(1)}, bf16[8,768]{1,0:T(8,128)(2,1)S(1)}, u32[]{:S(2)}, u32[]{:S(2)}) collective-permute-start(bf16[8,768]{1,0:T(8,128)(2,1)S(1)} %get-tuple-element.43), channel_id=1, source_target_pairs={{0,12},{4,8},{8,4},{12,0},{1,13},{5,9},{9,5},{13,1},{2,14},{6,10},... | collective-permute-start | bytes 36872 | tf_op jit(solution)/shard_map/ppermute | solution.py:483
  24.2 1.8 %collective-permute-start.5 = (bf16[96,2048]{1,0:T(8,128)(2,1)S(1)}, bf16[96,2048]{1,0:T(8,128)(2,1)S(1)}, u32[]{:S(2)}, u32[]{:S(2)}) collective-permute-start(bf16[96,2048]{1,0:T(8,128)(2,1)S(1)} %get-tuple-element.45), channel_id=1, source_target_pairs={{0,1},{1,0},{2,3},{3,2},{4,5},{5,4},{6,7},{7,6},{8,9},{9,8},{10,11... | collective-permute-start | bytes 1179656 | tf_op jit(solution)/shard_map/ppermute | solution.py:508
  26.1 12.3 %collective-permute-start.10 = (bf16[96,2048]{1,0:T(8,128)(2,1)S(1)}, bf16[96,2048]{1,0:T(8,128)(2,1)S(1)}, u32[]{:S(2)}, u32[]{:S(2)}) collective-permute-start(bf16[96,2048]{1,0:T(8,128)(2,1)S(1)} %add_convert_fusion.1.after), channel_id=1, source_target_pairs={{0,2},{1,3},{2,0},{3,1},{4,6},{5,7},{6,4},{7,5},{8,10},{9,11},{10,... | collective-permute-start | bytes 1179656 | tf_op jit(solution)/shard_map/ppermute | solution.py:422
  26.7 5.5 %collective-permute-start.6 = (bf16[8,512]{1,0:T(8,128)(2,1)S(1)}, bf16[8,512]{1,0:T(8,128)(2,1)S(1)}, u32[]{:S(2)}, u32[]{:S(2)}) collective-permute-start(bf16[8,512]{1,0:T(8,128)(2,1)S(1)} %get-tuple-element.47), channel_id=1, source_target_pairs={{0,4},{4,0},{8,12},{12,8},{1,5},{5,1},{9,13},{13,9},{2,6},{6,2},{1... | collective-permute-start | bytes 24584 | tf_op jit(solution)/shard_map/ppermute | solution.py:509
  26.9 5.3 %collective-permute-start.7 = (bf16[8,512]{1,0:T(8,128)(2,1)S(1)}, bf16[8,512]{1,0:T(8,128)(2,1)S(1)}, u32[]{:S(2)}, u32[]{:S(2)}) collective-permute-start(bf16[8,512]{1,0:T(8,128)(2,1)S(1)} %get-tuple-element.48), channel_id=1, source_target_pairs={{0,8},{4,12},{8,0},{12,4},{1,9},{5,13},{9,1},{13,5},{2,10},{6,14},... | collective-permute-start | bytes 24584 | tf_op jit(solution)/shard_map/ppermute | solution.py:509
  29.5 5.4 %collective-permute-start.8 = (bf16[8,512]{1,0:T(8,128)(2,1)S(1)}, bf16[8,512]{1,0:T(8,128)(2,1)S(1)}, u32[]{:S(2)}, u32[]{:S(2)}) collective-permute-start(bf16[8,512]{1,0:T(8,128)(2,1)S(1)} %get-tuple-element.49), channel_id=1, source_target_pairs={{0,12},{4,8},{8,4},{12,0},{1,13},{5,9},{9,5},{13,1},{2,14},{6,10},... | collective-permute-start | bytes 24584 | tf_op jit(solution)/shard_map/ppermute | solution.py:509
  36.5 1.9 %collective-permute-start.11 = (bf16[32,2048]{1,0:T(8,128)(2,1)S(1)}, bf16[32,2048]{1,0:T(8,128)(2,1)S(1)}, u32[]{:S(2)}, u32[]{:S(2)}) collective-permute-start(bf16[32,2048]{1,0:T(8,128)(2,1)S(1)} %get-tuple-element.54), channel_id=1, source_target_pairs={{0,1},{1,0},{2,3},{3,2},{4,5},{5,4},{6,7},{7,6},{8,9},{9,8},{10,11... | collective-permute-start | bytes 393224 | tf_op jit(solution)/shard_map/ppermute | solution.py:544
  36.5 2.5 %collective-permute-start.13 = (bf16[224,1024]{1,0:T(8,128)(2,1)S(1)}, bf16[224,1024]{1,0:T(8,128)(2,1)S(1)}, u32[]{:S(2)}, u32[]{:S(2)}) collective-permute-start(bf16[224,1024]{1,0:T(8,128)(2,1)S(1)} %get-tuple-element.55), channel_id=1, source_target_pairs={{0,1},{1,0},{2,3},{3,2},{4,5},{5,4},{6,7},{7,6},{8,9},{9,8},{10,11... | collective-permute-start | bytes 1376264 | tf_op jit(solution)/shard_map/ppermute | solution.py:529
  37.0 2.1 %collective-permute-start.14 = (bf16[224,1024]{1,0:T(8,128)(2,1)S(1)}, bf16[224,1024]{1,0:T(8,128)(2,1)S(1)}, u32[]{:S(2)}, u32[]{:S(2)}) collective-permute-start(bf16[224,1024]{1,0:T(8,128)(2,1)S(1)} %get-tuple-element.56), channel_id=1, source_target_pairs={{0,1},{1,0},{2,3},{3,2},{4,5},{5,4},{6,7},{7,6},{8,9},{9,8},{10,11... | collective-permute-start | bytes 1376264 | tf_op jit(solution)/shard_map/ppermute | solution.py:529
  37.9 3.1 %collective-permute-start.9 = (bf16[32,2048]{1,0:T(8,128)(2,1)S(1)}, bf16[32,2048]{1,0:T(8,128)(2,1)S(1)}, u32[]{:S(2)}, u32[]{:S(2)}) collective-permute-start(bf16[32,2048]{1,0:T(8,128)(2,1)S(1)} %get-tuple-element.52), channel_id=1, source_target_pairs={{0,1},{1,0},{2,3},{3,2},{4,5},{5,4},{6,7},{7,6},{8,9},{9,8},{10,11... | collective-permute-start | bytes 393224 | tf_op jit(solution)/shard_map/ppermute | solution.py:557
  38.4 5.5 %collective-permute-start.12 = (bf16[32,2048]{1,0:T(8,128)(2,1)S(1)}, bf16[32,2048]{1,0:T(8,128)(2,1)S(1)}, u32[]{:S(2)}, u32[]{:S(2)}) collective-permute-start(bf16[32,2048]{1,0:T(8,128)(2,1)S(1)} %add_convert_fusion.2), channel_id=1, source_target_pairs={{0,2},{1,3},{2,0},{3,1},{4,6},{5,7},{6,4},{7,5},{8,10},{9,11},{10,... | collective-permute-start | bytes 393224 | tf_op jit(solution)/shard_map/ppermute | solution.py:422
